TPU v7x, 256 devices: a whole 4x4x8 slice. The times are simulated.
256 devices in a mesh: space: 16 (over x, y_hi, core), replica: 16 (over z, y_lo).
Axes of the slice: x: 4, y: 4 (y_hi: 2, y_lo: 2; y = y_hi * 2 + y_lo), z: 8, core: 2. Of those that a mesh axis runs over, the one named last changes fastest.
Arguments:
- activations: bfloat16 [16, 32, 64, 48, 256], P('replica', None, 'space'), may hold values from -6 to 6
- preact: bfloat16 [16, 32, 32, 24, 128], P('replica', None, 'space'), may hold values from -6 to 6
- cotangent: bfloat16 [16, 32, 32, 24, 128], P('replica', None, 'space'), may hold values from -0.01171875 to 0.01171875
- conv_weight: bfloat16 [27, 32, 32], replicated, may hold values from -0.21875 to 0.21875
Outputs:
- weight_grads: float32 [2, 27648], P(None, 'space')
All inputs are finite; a program needn't handle non-finite values.
Results may differ from a plain program's by a relative error of at most 0.003.
Values may be sent and summed in bfloat16 or wider, within the bound.
No kernel may reach another device: no remote copies, remote signals or barrier semaphores. Data moves between devices by JAX's collectives and lax.ppermute only.
A program may use at most 128 MiB of HBM per device.

v0:
```python
import jax
import jax.numpy as jnp
from jax import lax
from jax.sharding import PartitionSpec as P


def extended(cells, sides, width):
    for axis, dim in sides:
        count = lax.axis_size(axis)
        ends = count - 1
        head = lax.slice_in_dim(cells, 0, width, axis=dim)
        tail = lax.slice_in_dim(cells, cells.shape[dim] - width, cells.shape[dim], axis=dim)
        cells = jnp.concatenate(
            [
                lax.ppermute(tail, axis, [(i, (i + 1) % count) for i in range(ends)]),
                cells,
                lax.ppermute(head, axis, [((i + 1) % count, i) for i in range(ends)]),
            ],
            axis=dim,
        )
    return cells


def passed_along(x, axis, by):
    length = lax.axis_size(axis)
    pairs = [(i, i + by) for i in range(length) if 0 <= i + by < length]
    return lax.ppermute(x, axis, pairs)


def volume_conv(lhs, rhs, dilation):
    return lax.conv_general_dilated(
        lhs,
        rhs,
        (1, 1, 1),
        "VALID",
        rhs_dilation=dilation,
        dimension_numbers=("NCDHW", "OIDHW", "NCDHW"),
        preferred_element_type=jnp.float32,
    )


def second_terms(cot_pad, preact, conv_weight):
    channels = preact.shape[0]
    pre_float = preact.astype(jnp.float32)
    hidden = jax.nn.silu(pre_float).astype(jnp.bfloat16)
    taps = conv_weight.reshape(3, 3, 3, channels, channels)[::-1, ::-1, ::-1]
    kernel = jnp.transpose(taps, (4, 3, 0, 1, 2))
    hidden_grad = volume_conv(cot_pad[None], kernel, (1, 1, 1))[0]
    second_raw = volume_conv(cot_pad[:, None], hidden[:, None], (1, 1, 1))
    second_raw = second_raw[:, :, ::-1, ::-1, ::-1]
    grads_second = jnp.transpose(second_raw, (2, 3, 4, 0, 1)).reshape(27, channels, channels)
    gate_val = jax.nn.sigmoid(pre_float)
    pre_grad = (hidden_grad * gate_val * (1.0 + pre_float * (1.0 - gate_val))).astype(jnp.bfloat16)
    return (grads_second, pre_grad)


def first_terms(act_pad, pre_grad):
    channels = pre_grad.shape[0]
    first_raw = volume_conv(act_pad[:, None], pre_grad[:, None], (2, 2, 2))
    return jnp.transpose(first_raw, (2, 3, 4, 1, 0)).reshape(27, channels, channels)


def on_device(activations, preact, cotangent, conv_weight):
    volume_in = activations[0]
    pre_one = preact[0]
    cot_ext = extended(cotangent[0], (("space", 1),), 1)
    cot_pad = jnp.pad(cot_ext, ((0, 0), (0, 0), (1, 1), (1, 1)))
    grads_second, pre_grad = second_terms(cot_pad, pre_one, conv_weight)
    last_plane = volume_in[:, volume_in.shape[1] - 1 :]
    rim_plane = passed_along(last_plane, "space", 1)
    act_pad = jnp.concatenate([rim_plane, volume_in], axis=1)
    act_pad = jnp.pad(act_pad, ((0, 0), (0, 0), (1, 0), (1, 0)))
    grads_first = first_terms(act_pad, pre_grad)
    terms = jnp.stack([grads_first, grads_second]).reshape(2, -1)
    shared = lax.psum_scatter(terms, "space", scatter_dimension=1, tiled=True)
    result = lax.psum(shared, "replica")
    return result


def solution(mesh):
    return jax.shard_map(
        on_device,
        mesh=mesh,
        in_specs=(
            P("replica", None, "space", None, None),
            P("replica", None, "space", None, None),
            P("replica", None, "space", None, None),
            P(),
        ),
        out_specs=P(None, "space"),
        check_vma=False,
    )
```

profile of v0, /device:TPU:2, one launch (start us, length us, event | category | flops | bytes accessed | tf_op | source)
XLA Modules:
  0.0 487.8 jit_solution(3610019863616893170)
XLA Ops:
  6.5 1.1 copy.52
  7.7 4.5 collective-permute-start.2
  12.2 1.9 collective-permute-start.1
  14.2 3.7 copy.51
  17.8 1.7 copy-done.2
  20.5 2.8 collective-permute-start
  24.4 12.9 %copy.43 = bf16[32,1,4,26,130]{0,1,4,3,2:T(2,128)(2,1)} copy(bf16[32,1,4,26,130]{4,0,3,2,1:T(8,128)(2,1)S(1)} %fusion.37) | data formatting | bytes 1730560 | tf_op jit(solution)/shard_map/broadcast_in_dim | solution.py:49
  38.4 5.0 %copy.48 = bf16[32,4,26,1,130]{0,1,4,2,3:T(4,128)(2,1)} copy(bf16[32,4,26,1,130]{4,0,2,1,3:T(8,128)(2,1)S(1)} %fusion.36) | data formatting | bytes 1730560
  43.3 3.8 pad.10.clone
  47.8 5.0 %fusion.19 = f32[2,24,8,17,32]{4,2,3,1,0:T(8,128)S(1)} fusion(bf16[3,3,3,32,32]{4,3,2,1,0:T(8,128)(2,1)S(1)} %bitcast.43, bf16[32,4,26,1,7,2]{0,4,5,2,1,3:T(8,128)(2,1)S(1)} %slice.17, bf16[32,4,26,1,8,17]{0,4,5,2,1,3:T(8,128)(2,1)S(1)} %copy.37, pred[8,17]{0,1:T(8,128)(4,1)S(1)} %copy-done.5), kind=kOutput, calls=%fused_computation.26 | convolution fusion | flops 364216320 | bytes 1889416 | tf_op jit(solution)/shard_map/conv_general_dilated | solution.py:31
  53.7 1.9 copy.47
  55.6 2.5 fusion.30
  58.1 4.4 copy.44
  62.5 45.3 %fusion.39 = f32[32,32,3,3,3]{1,0,4,3,2:T(8,128)S(1)} fusion(bf16[32,1,4,26,130]{0,1,4,3,2:T(2,128)(2,1)} %copy.43, bf16[32,1,2,24,128]{0,1,4,3,2:T(2,128)(2,1)S(1)} %copy.44), kind=kOutput, calls=%fused_computation.53 | convolution fusion | flops 339738624 | bytes 1369088 | tf_op jit(solution)/shard_map/conv_general_dilated | solution.py:31
  108.6 1.5 stack.8
  110.1 5.6 %copy.41 = bf16[32,1,2,24,128]{0,1,4,3,2:T(2,128)(2,1)} copy(bf16[32,1,2,24,128]{4,3,2,1,0:T(8,128)(2,1)} %get-tuple-element.5) | data formatting | bytes 786432 | tf_op jit(solution)/shard_map/convert_element_type | solution.py:53
  115.7 7.3 %fusion.7 = bf16[32,1,5,49,257]{4,0,3,2,1:T(8,128)(2,1)} fusion(bf16[32,4,48,256]{3,0,2,1:T(8,128)(2,1)S(1)} %bitcast.46, bf16[32,1,48,256]{3,0,2,1:T(8,128)(2,1)} %collective-permute-done), kind=kLoop, calls=%fused_computation.10 | loop fusion | flops 22163680 | bytes 7961920 | tf_op jit(solution)/shard_map/broadcast_in_dim | solution.py:59
  123.0 73.3 %copy.40 = bf16[32,1,5,49,257]{0,1,4,3,2:T(2,128)(2,1)} copy(bf16[32,1,5,49,257]{4,0,3,2,1:T(8,128)(2,1)} %fusion.7) | data formatting | bytes 8059520 | tf_op jit(solution)/shard_map/broadcast_in_dim | solution.py:59
  196.3 71.1 %fusion.38 = f32[3,3,3,32,32]{4,3,2,1,0:T(8,128)} fusion(bf16[32,1,5,49,257]{0,1,4,3,2:T(2,128)(2,1)} %copy.40, bf16[32,1,2,24,128]{0,1,4,3,2:T(2,128)(2,1)S(1)} %copy-done.4), kind=kOutput, calls=%fused_computation.52 | convolution fusion | flops 339738624 | bytes 4533568 | tf_op jit(solution)/shard_map/transpose | solution.py:60
  267.4 1.2 stack.7
  268.9 7.5 %copy.45 = f32[2,27648]{0,1:T(8,128)} copy(f32[2,27648]{1,0:T(2,128)S(1)} %pad_maximum_fusion) | data formatting | bytes 442368
  276.4 140.0 %reduce-scatter.4.cloned.1.call-done = f32[1728,2]{1,0:T(8,128)} async-done(((f32[27648,2]{1,0:T(8,128)}), f32[1728,2]{1,0:T(8,128)}) %reduce-scatter.4.cloned.1.call-update) | async-done | bytes 13840
  416.4 1.5 copy.46
  417.9 63.1 %psum.7 = f32[2,1728]{1,0:T(2,128)} all-reduce(f32[2,1728]{1,0:T(2,128)S(1)} %copy.46), channel_id=1, replica_groups=mesh['space'=16,'replica'=16] {'replica'}, use_global_device_ids=true, to_apply=%region_1.2 | all-reduce | flops 3456 | bytes 27648 | tf_op jit(solution)/shard_map/psum | solution.py:76
  (26 shorter events, 5.6 us)
Async XLA Ops:
  6.5 41.2 %copy-start = (bf16[27,32,32]{2,1,0:T(8,128)(2,1)S(1)}, bf16[27,32,32]{2,1,0:T(8,128)(2,1)}, u32[]{:S(2)}) copy-start(bf16[27,32,32]{2,1,0:T(8,128)(2,1)} %param.7) | copy-start | bytes 165892
  6.5 409.9 %reduce-scatter.4.cloned.1.call-start = ((), (), s32[]{:S(2)}) async-start(), calls=%async_computation.1 | async-start | bytes 15040512
  7.7 15.6 %collective-permute-start.2 = (bf16[32,1,24,128]{3,0,2,1:T(8,128)(2,1)S(1)}, bf16[32,1,24,128]{3,0,2,1:T(8,128)(2,1)S(1)}, u32[]{:S(2)}, u32[]{:S(2)}) collective-permute-start(bf16[32,1,24,128]{3,0,2,1:T(8,128)(2,1)S(1)} %get-tuple-element.8), channel_id=1, source_target_pairs={{16,0},{32,16},{48,32},{64,48},{80,64},{96,80},{112,96},{128,112},... | collective-permute-start | bytes 589832 | tf_op jit(solution)/shard_map/ppermute | solution.py:17
  12.2 11.1 %collective-permute-start.1 = (bf16[32,1,24,128]{3,0,2,1:T(8,128)(2,1)S(1)}, bf16[32,1,24,128]{3,0,2,1:T(8,128)(2,1)S(1)}, u32[]{:S(2)}, u32[]{:S(2)}) collective-permute-start(bf16[32,1,24,128]{3,0,2,1:T(8,128)(2,1)S(1)} %get-tuple-element.7), channel_id=1, source_target_pairs={{0,16},{16,32},{32,48},{48,64},{64,80},{80,96},{96,112},{112,128},... | collective-permute-start | bytes 589832 | tf_op jit(solution)/shard_map/ppermute | solution.py:15
  17.8 1.8 copy-start.2
  20.5 95.2 %collective-permute-start = (bf16[32,1,48,256]{3,0,2,1:T(8,128)(2,1)}, bf16[32,1,48,256]{3,0,2,1:T(8,128)(2,1)}, u32[]{:S(2)}, u32[]{:S(2)}) collective-permute-start(bf16[32,1,48,256]{3,0,2,1:T(8,128)(2,1)} %slice.14), channel_id=1, source_target_pairs={{0,16},{16,32},{32,48},{48,64},{64,80},{80,96},{96,112},{112,128},... | collective-permute-start | bytes 2359304 | tf_op jit(solution)/shard_map/ppermute | solution.py:27
  47.1 0.7 copy-start.5
  107.8 7.9 %copy-start.3 = (bf16[1,32,4,48,256]{4,1,3,2,0:T(8,128)(2,1)S(1)}, bf16[1,32,4,48,256]{4,1,3,2,0:T(8,128)(2,1)}, u32[]{:S(2)}) copy-start(bf16[1,32,4,48,256]{4,1,3,2,0:T(8,128)(2,1)} %copy-done.2) | copy-start | bytes 9437188
  123.0 73.3 %copy-start.4 = (bf16[32,1,2,24,128]{0,1,4,3,2:T(2,128)(2,1)S(1)}, bf16[32,1,2,24,128]{0,1,4,3,2:T(2,128)(2,1)}, u32[]{:S(2)}) copy-start(bf16[32,1,2,24,128]{0,1,4,3,2:T(2,128)(2,1)} %copy.41) | copy-start | bytes 1179652
  276.4 204.5 %copy-start.1 = (bf16[27,32,32]{2,1,0:T(8,128)(2,1)S(1)}, bf16[27,32,32]{2,1,0:T(8,128)(2,1)}, u32[]{:S(2)}) copy-start(bf16[27,32,32]{2,1,0:T(8,128)(2,1)} %param.7) | copy-start | bytes 165892
Sparse Core Ops, SparseCore 0:
  276.5 139.8 reduce-scatter.3
where the time goes:
time: 495 us; the launch traced here: 488 us
  waiting for transfers between devices  140 us (28%)
  local copies, waits for them, and re-layouts  128 us (26%)
  matrix products  121 us (24%)
  blocking collectives  63.1 us (13%)
  between operations  13.6 us (3%)
  other arithmetic  12.1 us (2%)
  starting transfers between devices  9.22 us (2%)
    unnamed x2, waiting for transfers between devices  140 us
    broadcast_in_dim x1, local copies, waits for them, and re-layouts, first_terms(): first_raw = volume_conv(act_pad[:, None], pre_grad[:, None], (2, 2, 2))  73.3 us
    transpose x1, matrix products, first_terms(): jnp.transpose(first_raw, (2, 3, 4, 1, 0)).reshape(27, channels, channels)  71.1 us
    psum x1, blocking collectives, on_device(): result = lax.psum(shared, 'replica')  63.1 us
    conv_general_dilated x2, matrix products, volume_conv(): lax.conv_general_dilated(lhs, rhs, (1, 1, 1), 'VALID', rhs_dilation=dilat...  50.3 us
    unnamed x18, local copies, waits for them, and re-layouts  22.5 us
    broadcast_in_dim x1, local copies, waits for them, and re-layouts, second_terms(): second_raw = volume_conv(cot_pad[:, None], hidden[:, None], (1, 1, 1))  12.9 us
  transfers between devices with their start and end apart: 4, of which 1 were waited for; matrix products, arithmetic and copies ran while one was open for 20% of the time, Pallas kernels for 0%

commit v1 on v0

v1 whole, which is shorter than its diff:
```python
import jax
import jax.numpy as jnp
from jax import lax
from jax.experimental import pallas as pl
from jax.experimental.pallas import tpu as pltpu
from jax.sharding import PartitionSpec as P

BF = jnp.bfloat16
F32 = jnp.float32

C = 32
QX, QZ, QY = 2, 24, 128
IX, IZ, IY = 4, 48, 256
TAPS2 = 288
TAPS1 = 96

NT = (((1,), (1,)), ((), ()))


def relaid(flat_ref, step, stride):
    return flat_ref[pl.ds(step, C, stride=stride), :]


def section_kernel(
    act_ref, act_prev_ref, cot_ref, cot_prev_ref, cot_next_ref, pre_ref, weight_ref,
    out_ref,
    flat_act, flat_small, act_t, cot_t, pre_t, hidden_t, weight_t, second_acc, first_acc, flips, dense,
):
    act_t[:, 0:C, :] = jnp.zeros((IX + 1, C, IY), BF)
    cot_t[:, 0:C, :] = jnp.zeros((QX + 2, C, QY), BF)
    cot_t[:, (QZ + 1) * C : (QZ + 2) * C, :] = jnp.zeros((QX + 2, C, QY), BF)

    for plane in range(IX + 1):
        block = act_prev_ref[...] if plane == 0 else act_ref[:, plane - 1]
        flat = block.astype(F32).reshape(C * IZ, IY)
        for side in range(2):
            flat_act[plane % 2, side] = flat[:, side * 128 : (side + 1) * 128]

        def move_act(z, carry, plane=plane):
            start = pl.multiple_of((z + 1) * C, C)
            for side in range(2):
                tile = relaid(flat_act.at[plane % 2, side], z, IZ).astype(BF)
                act_t[plane, pl.ds(start, C), side * 128 : (side + 1) * 128] = tile
            return carry

        lax.fori_loop(0, IZ, move_act, 0, unroll=8)

    for plane in range(QX + 2):
        if plane == 0:
            block = cot_prev_ref[...]
        elif plane == QX + 1:
            block = cot_next_ref[...]
        else:
            block = cot_ref[:, plane - 1]
        flat_small[plane] = block.astype(F32).reshape(C * QZ, QY)
    for plane in range(QX):
        flat_small[QX + 2 + plane] = pre_ref[:, plane].astype(F32).reshape(C * QZ, QY)

    lanes = lax.broadcasted_iota(jnp.int32, (C, QY), 1)

    def shifted(x, by):
        edge = 0 if by == 1 else QY - 1
        return jnp.where(lanes == edge, 0.0, pltpu.roll(x, by % QY, 1))

    for plane in range(QX + 2):

        def move_cot(z, carry, plane=plane):
            start = pl.multiple_of((z + 1) * C, C)
            cot_t[plane, pl.ds(start, C), :] = relaid(flat_small.at[plane], z, QZ).astype(BF)
            return carry

        lax.fori_loop(0, QZ, move_cot, 0, unroll=8)

    for plane in range(QX):

        def move_pre(z, carry, plane=plane):
            pre = relaid(flat_small.at[QX + 2 + plane], z, QZ)
            gate = jax.nn.sigmoid(pre)
            hidden = (pre * gate).astype(BF).astype(F32)
            hidden_t[plane, z] = jnp.concatenate(
                [shifted(hidden, 1), hidden, shifted(hidden, -1)], axis=0
            ).astype(BF)
            pre_t[plane, z] = gate * (1.0 + pre * (1.0 - gate))
            return carry

        lax.fori_loop(0, QZ, move_pre, 0, unroll=4)

    for j in range(3):
        for k in range(3):
            base = (2 - j) * 9 + (2 - k) * 3
            wide = jnp.concatenate([weight_ref[base + d].astype(F32) for d in range(3)], axis=1)
            weight_t[(j * 3 + k) * C : (j * 3 + k + 1) * C, :] = wide
    weights = weight_t[...].T.astype(BF)

    row = lax.broadcasted_iota(jnp.int32, (QY, 3 * IY), 0)
    col = lax.broadcasted_iota(jnp.int32, (QY, 3 * IY), 1)
    spread = jnp.where(col % IY == 2 * row + col // IY - 1, 1.0, 0.0).astype(BF)

    second_acc[...] = jnp.zeros((TAPS2, TAPS1), F32)
    first_acc[...] = jnp.zeros((TAPS2, TAPS1), F32)

    def pair_step(pair, carry):
        for x in range(QX):
            slabs = []
            for half in range(2):
                z = pair * 2 + half
                start = pl.multiple_of(z * C, C)
                slabs.append(
                    jnp.concatenate([cot_t[x + j, pl.ds(start, 3 * C), :] for j in range(3)], axis=0)
                )
            slab = jnp.concatenate(slabs, axis=1)
            hid = jnp.concatenate([hidden_t[x, pair * 2], hidden_t[x, pair * 2 + 1]], axis=1)
            second_acc[...] += lax.dot_general(slab, hid, NT, preferred_element_type=F32)
            terms = jnp.dot(weights, slab, preferred_element_type=F32)
            rows = []
            for half in range(2):
                part = terms[:, half * QY : (half + 1) * QY]
                hidden_grad = part[C : 2 * C] + shifted(part[0:C], -1) + shifted(part[2 * C :], 1)
                rows.append((hidden_grad * pre_t[x, pair * 2 + half]).astype(BF))
            grads = jnp.concatenate(rows, axis=0)
            wide = jnp.dot(grads, spread, preferred_element_type=F32).astype(BF)
            for half in range(2):
                z = pair * 2 + half
                ups = jnp.concatenate(
                    [wide[half * C : (half + 1) * C, d * IY : (d + 1) * IY] for d in range(3)], axis=0
                )
                start = pl.multiple_of(z * 2 * C, C)
                acts = jnp.concatenate(
                    [act_t[2 * x + a, pl.ds(start, 3 * C), :] for a in range(3)], axis=0
                )
                first_acc[...] += lax.dot_general(acts, ups, NT, preferred_element_type=F32)
        return carry

    lax.fori_loop(0, QZ // 2, pair_step, 0)

    first_flip = first_acc[...].T
    for side in range(3):
        wide = min(128, TAPS2 - side * 128)
        flips[side, 0:TAPS1, 0:wide] = first_flip[:, side * 128 : side * 128 + wide]
    flips[3, :, 0:TAPS1] = second_acc[...]
    lane = lax.broadcasted_iota(jnp.int32, (8, 128), 1)
    for ab in range(9):
        ab_rev = (2 - ab // 3) * 3 + (2 - ab % 3)
        for d in range(3):
            for which in range(2):
                total = jnp.zeros((8, 128), F32)
                for r in range(4):
                    if which == 0:
                        side, offset, begin = ab // 4, (ab % 4) * C, d * C + r
                    else:
                        side, offset, begin = 3, d * C, ab_rev * C + r
                    part = flips[side, pl.ds(begin, 8, stride=4), :]
                    turn = (r * C - offset) % 128
                    part = pltpu.roll(part, turn, 1) if turn else part
                    total = jnp.where(lane // C == r, part, total)
                dense[which, (ab * 3 + d) * 8 : (ab * 3 + d + 1) * 8, :] = total

    for s in range(16):
        begin = (27 * s) // 2
        for which in range(2):
            out_ref[s, which, 0:14, :] = dense[which, begin : begin + 14, :]
            out_ref[s, which, 14:16, :] = jnp.zeros((2, 128), F32)


def section_terms(act, act_prev, cot, cot_prev, cot_next, pre, weight):
    vmem = pl.BlockSpec(memory_space=pltpu.VMEM)
    return pl.pallas_call(
        section_kernel,
        out_shape=jax.ShapeDtypeStruct((16, 2, 16, 128), F32),
        in_specs=[vmem] * 7,
        out_specs=vmem,
        scratch_shapes=[
            pltpu.VMEM((2, 2, C * IZ, 128), F32),
            pltpu.VMEM((2 * QX + 2, C * QZ, QY), F32),
            pltpu.VMEM((IX + 1, (IZ + 1) * C, IY), BF),
            pltpu.VMEM((QX + 2, (QZ + 2) * C, QY), BF),
            pltpu.VMEM((QX, QZ, C, QY), F32),
            pltpu.VMEM((QX, QZ, TAPS1, QY), BF),
            pltpu.VMEM((TAPS2, TAPS1), F32),
            pltpu.VMEM((TAPS2, TAPS1), F32),
            pltpu.VMEM((TAPS2, TAPS1), F32),
            pltpu.VMEM((4, TAPS2, 128), F32),
            pltpu.VMEM((2, 216, 128), F32),
        ],
        compiler_params=pltpu.CompilerParams(vmem_limit_bytes=48 * 2**20),
        name="section_terms",
    )(act, act_prev, cot, cot_prev, cot_next, pre, weight)


def moved(x, axis, by):
    length = lax.axis_size(axis)
    pairs = [(i, i + by) for i in range(length) if 0 <= i + by < length]
    return lax.ppermute(x, axis, pairs)


def on_device(activations, preact, cotangent, conv_weight):
    act, pre, cot = activations[0], preact[0], cotangent[0]
    cot_prev = moved(cot[:, QX - 1], "space", 1)
    cot_next = moved(cot[:, 0], "space", -1)
    act_prev = moved(act[:, IX - 1], "space", 1)
    terms = section_terms(act, act_prev, cot, cot_prev, cot_next, pre, conv_weight)
    shares = lax.all_to_all(terms, "space", 0, 0, tiled=True)
    share = jnp.sum(shares, axis=0)
    copies = lax.all_to_all(jnp.broadcast_to(share[None], (16, 2, 16, 128)), "replica", 0, 0, tiled=True)
    total = jnp.sum(copies, axis=0)[:, :14].reshape(2, 14 * 128)
    odd = lax.axis_index("space") % 2
    return lax.dynamic_slice(total, (0, 64 * odd), (2, 1728))


def solution(mesh):
    return jax.shard_map(
        on_device,
        mesh=mesh,
        in_specs=(
            P("replica", None, "space", None, None),
            P("replica", None, "space", None, None),
            P("replica", None, "space", None, None),
            P(),
        ),
        out_specs=P(None, "space"),
        check_vma=False,
    )
```

time: 495 us -> 79.7 us (0.16); the launches traced: 488 us -> 79 us
  local copies, waits for them, and re-layouts: 128 us -> 3.83 us
  matrix products: 121 us -> 0 us
  waiting for transfers between devices: 140 us -> 21 us
  blocking collectives: 63.1 us -> 15.5 us
  Pallas kernels: 0 us -> 19.7 us
  between operations: 13.6 us -> 0.15 us
  other arithmetic: 12.1 us -> 0.04 us
  starting transfers between devices: 9.22 us -> 18.8 us
    unnamed x2 -> x0, waiting for transfers between devices: 140 us -> none
    broadcast_in_dim x3 -> x1, local copies, waits for them, and re-layouts: 90 us -> 0.72 us  [on_device(): jnp.broadcast_to(share[None], (16, 2, 16, 128))]
    transpose x1 -> x0, matrix products: 71.1 us -> none  [first_terms(): jnp.transpose(first_raw, (2, 3, 4, 1, 0)).reshape(27, channels, channels)]
    psum x1 -> x0, blocking collectives: 63.1 us -> none  [on_device(): result = lax.psum(shared, 'replica')]
    conv_general_dilated x2 -> x0, matrix products: 50.3 us -> none  [volume_conv(): lax.conv_general_dilated(lhs, rhs, (1, 1, 1), 'VALID', rhs_dilation=dilat...]
    unnamed x18 -> x12, local copies, waits for them, and re-layouts: 22.5 us -> 2.33 us
    pallas_call x0 -> x1, Pallas kernels: none -> 19.7 us  [section_terms(): pl.pallas_call(section_kernel, out_shape=jax.ShapeDtypeStruct((16, 2, 16,...]
    all_to_all x0 -> x1, blocking collectives: none -> 15.5 us  [on_device(): shares = lax.all_to_all(terms, 'space', 0, 0, tiled=True)]
  transfers between devices with their start and end apart: 4 -> 4, of which waited for: 1 -> 2; matrix products, arithmetic and copies ran while one was open for 20% -> 0% of each run, Pallas kernels for 0% -> 0%
where the time goes in v1:
time: 79.7 us; the launch traced here: 79 us
  waiting for transfers between devices  21 us (26%)
  Pallas kernels  19.7 us (25%)
  starting transfers between devices  18.8 us (24%)
  blocking collectives  15.5 us (19%)
  local copies, waits for them, and re-layouts  3.83 us (5%)
    pallas_call x1, Pallas kernels, section_terms(): pl.pallas_call(section_kernel, out_shape=jax.ShapeDtypeStruct((16, 2, 16,...  19.7 us
    all_to_all x1, blocking collectives, on_device(): shares = lax.all_to_all(terms, 'space', 0, 0, tiled=True)  15.5 us
    all_to_all x1, waiting for transfers between devices, on_device(): lax.all_to_all(jnp.broadcast_to(share[None], (16, 2, 16, 128)), 'replica'...  13.1 us
    ppermute x3, starting transfers between devices, moved(): return lax.ppermute(x, axis, pairs)  10.1 us
    all_to_all x1, starting transfers between devices, on_device(): lax.all_to_all(jnp.broadcast_to(share[None], (16, 2, 16, 128)), 'replica'...  8.67 us
    ppermute x3, waiting for transfers between devices, moved(): return lax.ppermute(x, axis, pairs)  7.9 us
    unnamed x12, local copies, waits for them, and re-layouts  2.33 us
  transfers between devices with their start and end apart: 4, of which 2 were waited for; matrix products, arithmetic and copies ran while one was open for 0% of the time, Pallas kernels for 0%

profile of v1, /device:TPU:2, one launch (start us, length us, event | category | flops | bytes accessed | tf_op | source)
XLA Modules:
  0.0 79.0 jit_solution(3727342927132813233)
XLA Ops:
  0.0 0.0 copy-start.1
  0.0 0.0 copy-start.2
  0.0 0.0 copy-start.3
  0.0 2.3 %copy.23 = bf16[1,32,4,48,256]{4,3,1,2,0:T(8,128)(2,1)S(1)} copy(bf16[1,32,4,48,256]{4,3,2,1,0:T(8,128)(2,1)} %param.4) | data formatting | bytes 6291456 | tf_op args[0]
  2.3 0.0 copy-start
  2.3 0.1 slice_bitcast_fusion
  2.3 2.2 %collective-permute-start = (bf16[32,48,256]{2,1,0:T(8,128)(2,1)S(1)}, bf16[32,48,256]{2,1,0:T(8,128)(2,1)S(1)}, u32[]{:S(2)}, u32[]{:S(2)}) collective-permute-start(bf16[32,48,256]{2,1,0:T(8,128)(2,1)S(1)} %slice_bitcast_fusion), channel_id=1, source_target_pairs={{0,16},{16,32},{32,48},{48,64},{64,80},{80,96},{96,112},{112,128},... | collective-permute-start | bytes 2359304 | tf_op jit(solution)/shard_map/ppermute | solution.py:193
  4.5 0.0 copy-done.1
  4.6 5.2 %collective-permute-start.1 = (bf16[32,24,128]{2,1,0:T(8,128)(2,1)S(1)}, bf16[32,24,128]{2,1,0:T(8,128)(2,1)S(1)}, u32[]{:S(2)}, u32[]{:S(2)}) collective-permute-start(bf16[32,24,128]{2,1,0:T(8,128)(2,1)S(1)} %get-tuple-element.6), channel_id=1, source_target_pairs={{0,16},{16,32},{32,48},{48,64},{64,80},{80,96},{96,112},{112,128},... | collective-permute-start | bytes 589832 | tf_op jit(solution)/shard_map/ppermute | solution.py:193
  9.9 2.8 %collective-permute-start.2 = (bf16[32,24,128]{2,1,0:T(8,128)(2,1)S(1)}, bf16[32,24,128]{2,1,0:T(8,128)(2,1)S(1)}, u32[]{:S(2)}, u32[]{:S(2)}) collective-permute-start(bf16[32,24,128]{2,1,0:T(8,128)(2,1)S(1)} %get-tuple-element.5), channel_id=1, source_target_pairs={{16,0},{32,16},{48,32},{64,48},{80,64},{96,80},{112,96},{128,112},... | collective-permute-start | bytes 589832 | tf_op jit(solution)/shard_map/ppermute | solution.py:193
  12.6 7.9 %collective-permute-done.1.cot_prev_ref = bf16[32,24,128]{2,1,0:T(8,128)(2,1)S(1)} collective-permute-done((bf16[32,24,128]{2,1,0:T(8,128)(2,1)S(1)}, bf16[32,24,128]{2,1,0:T(8,128)(2,1)S(1)}, u32[]{:S(2)}, u32[]{:S(2)}) %collective-permute-start.1) | collective-permute-done | bytes 196640 | tf_op jit(solution)/shard_map/ppermute | solution.py:193
  20.5 0.0 collective-permute-done.2.cot_next_ref
  20.5 0.0 collective-permute-done.act_prev_ref
  20.5 0.0 copy-done.2
  20.5 0.0 copy-done.3
  20.6 0.0 copy-done
  20.6 19.7 %section_terms.1 = f32[16,2,16,128]{3,2,1,0:T(8,128)S(1)} custom-call(bf16[32,4,48,256]{3,2,1,0:T(8,128)(2,1)S(1)} %bitcast.20, bf16[32,48,256]{2,1,0:T(8,128)(2,1)S(1)} %collective-permute-done.act_prev_ref, bf16[32,2,24,128]{3,2,1,0:T(8,128)(2,1)S(1)} %bitcast.21, bf16[32,24,128]{2,1,0:T(8,128)(2,1)S(1)} %collective-permute-done.1.cot_prev_ref, ...), custom_call_target="tpu_custom_call" | custom-call | tf_op jit(solution)/shard_map/section_terms/pallas_call | solution.py:167
  40.3 15.5 %all_to_all.10 = f32[16,2,16,128]{3,2,1,0:T(8,128)S(1)} all-to-all(f32[16,2,16,128]{3,2,1,0:T(8,128)S(1)} %section_terms.1), channel_id=1, replica_groups=mesh['space'=16,'replica'=16] {'space'}, dimensions={0} | all-to-all | bytes 524288 | tf_op jit(solution)/shard_map/all_to_all | solution.py:202
  55.7 0.7 broadcast_in_dim.2
  56.5 8.7 %all-to-all-start.1 = ((f32[16,2,16,128]{3,2,1,0:T(8,128)}), f32[16,2,16,128]{3,2,1,0:T(8,128)S(1)}, u32[]{:S(2)}, u32[]{:S(2)}) async-start(f32[16,2,16,128]{3,2,1,0:T(8,128)} %broadcast_in_dim.2), calls=%async_computation.1 | async-start | bytes 524288 | tf_op jit(solution)/shard_map/all_to_all | solution.py:204
  65.2 13.1 %all-to-all-done.1 = f32[16,2,16,128]{3,2,1,0:T(8,128)S(1)} async-done(((f32[16,2,16,128]{3,2,1,0:T(8,128)}), f32[16,2,16,128]{3,2,1,0:T(8,128)S(1)}, u32[]{:S(2)}, u32[]{:S(2)}) %all-to-all-start.1) | async-done | bytes 262176 | tf_op jit(solution)/shard_map/all_to_all | solution.py:204
  78.3 0.7 constant_dynamic-slice_fusion
  (6 shorter events, 0.1 us)
Async XLA Ops:
  0.0 4.5 %copy-start.1 = (bf16[1,32,2,24,128]{4,3,2,1,0:T(8,128)(2,1)S(1)}, bf16[1,32,2,24,128]{4,3,2,1,0:T(8,128)(2,1)}, u32[]{:S(2)}) copy-start(bf16[1,32,2,24,128]{4,3,2,1,0:T(8,128)(2,1)} %param.6) | copy-start | bytes 1179652
  0.0 20.5 %copy-start.2 = (bf16[1,32,2,24,128]{4,3,2,1,0:T(8,128)(2,1)S(1)}, bf16[1,32,2,24,128]{4,3,2,1,0:T(8,128)(2,1)}, u32[]{:S(2)}) copy-start(bf16[1,32,2,24,128]{4,3,2,1,0:T(8,128)(2,1)} %param.5) | copy-start | bytes 1179652
  0.0 20.5 %copy-start.3 = (bf16[27,32,32]{2,1,0:T(8,128)(2,1)S(1)}, bf16[27,32,32]{2,1,0:T(8,128)(2,1)}, u32[]{:S(2)}) copy-start(bf16[27,32,32]{2,1,0:T(8,128)(2,1)} %weight_ref.1) | copy-start | bytes 165892
  2.3 18.3 %copy-start = (bf16[1,32,4,48,256]{4,3,2,1,0:T(8,128)(2,1)S(1)}, bf16[1,32,4,48,256]{4,3,2,1,0:T(8,128)(2,1)}, u32[]{:S(2)}) copy-start(bf16[1,32,4,48,256]{4,3,2,1,0:T(8,128)(2,1)} %param.4) | copy-start | bytes 9437188
  2.3 18.2 %collective-permute-start = (bf16[32,48,256]{2,1,0:T(8,128)(2,1)S(1)}, bf16[32,48,256]{2,1,0:T(8,128)(2,1)S(1)}, u32[]{:S(2)}, u32[]{:S(2)}) collective-permute-start(bf16[32,48,256]{2,1,0:T(8,128)(2,1)S(1)} %slice_bitcast_fusion), channel_id=1, source_target_pairs={{0,16},{16,32},{32,48},{48,64},{64,80},{80,96},{96,112},{112,128},... | collective-permute-start | bytes 2359304 | tf_op jit(solution)/shard_map/ppermute | solution.py:193
  4.6 15.9 %collective-permute-start.1 = (bf16[32,24,128]{2,1,0:T(8,128)(2,1)S(1)}, bf16[32,24,128]{2,1,0:T(8,128)(2,1)S(1)}, u32[]{:S(2)}, u32[]{:S(2)}) collective-permute-start(bf16[32,24,128]{2,1,0:T(8,128)(2,1)S(1)} %get-tuple-element.6), channel_id=1, source_target_pairs={{0,16},{16,32},{32,48},{48,64},{64,80},{80,96},{96,112},{112,128},... | collective-permute-start | bytes 589832 | tf_op jit(solution)/shard_map/ppermute | solution.py:193
  9.9 10.7 %collective-permute-start.2 = (bf16[32,24,128]{2,1,0:T(8,128)(2,1)S(1)}, bf16[32,24,128]{2,1,0:T(8,128)(2,1)S(1)}, u32[]{:S(2)}, u32[]{:S(2)}) collective-permute-start(bf16[32,24,128]{2,1,0:T(8,128)(2,1)S(1)} %get-tuple-element.5), channel_id=1, source_target_pairs={{16,0},{32,16},{48,32},{64,48},{80,64},{96,80},{112,96},{128,112},... | collective-permute-start | bytes 589832 | tf_op jit(solution)/shard_map/ppermute | solution.py:193
  56.5 21.8 %all-to-all-start.1 = ((f32[16,2,16,128]{3,2,1,0:T(8,128)}), f32[16,2,16,128]{3,2,1,0:T(8,128)S(1)}, u32[]{:S(2)}, u32[]{:S(2)}) async-start(f32[16,2,16,128]{3,2,1,0:T(8,128)} %broadcast_in_dim.2), calls=%async_computation.1 | async-start | bytes 524288 | tf_op jit(solution)/shard_map/all_to_all | solution.py:204

commit v2 on v0

v2 whole, which is shorter than its diff:
```python
import jax
import jax.numpy as jnp
from jax import lax
from jax.experimental import pallas as pl
from jax.experimental.pallas import tpu as pltpu
from jax.sharding import Mesh, PartitionSpec as P

BF = jnp.bfloat16
F32 = jnp.float32

C = 32
QX, QZ, QY = 2, 24, 128
IX, IZ, IY = 4, 48, 256
T3 = 3 * C
COT_ROWS = (QZ + 3) * C
ACT_ROWS = (IZ + 1) * C
TAPS = 9 * C

NT = (((1,), (1,)), ((), ()))


def nt_dot(a, b):
    return lax.dot_general(a, b, NT, preferred_element_type=F32)


def lane_shift(x, by):
    lanes = lax.broadcasted_iota(jnp.int32, x.shape, 1)
    return jnp.where(lanes == (0 if by == 1 else QY - 1), 0.0, pltpu.roll(x, by % QY, 1))


def taps_joined(part):
    return part[C : 2 * C] + lane_shift(part[0:C], -1) + lane_shift(part[2 * C : T3], 1)


def four_blocks(rows):
    return jnp.concatenate([rows, rows[0:C]], axis=0)


def cot_kernel(cot_ref, first_ref, last_ref, flat):
    for plane, out_ref in ((0, first_ref), (1, last_ref)):
        flat[plane] = cot_ref[:, plane].astype(F32).reshape(C * QZ, QY)
        out_ref[0:C, :] = jnp.zeros((C, QY), BF)
        out_ref[(QZ + 1) * C :, :] = jnp.zeros((2 * C, QY), BF)
        for z in range(QZ):
            block = flat[plane, pl.ds(z, C, stride=QZ), :]
            out_ref[(z + 1) * C : (z + 2) * C, :] = block.astype(BF)


def local_kernel(
    act_ref, pre_ref, weight_ref, cot0_ref, cot1_ref,
    act_t, hidden_t, scale_t, partial_t, rim_weights, spread_ref, second_ref,
    flat_act, flat_pre, weight_t,
):
    for j in range(3):
        for k in range(3):
            base = (2 - j) * 9 + (2 - k) * 3
            wide = jnp.concatenate([weight_ref[base + d].astype(F32) for d in range(3)], axis=1)
            weight_t[(j * 4 + k) * C : (j * 4 + k + 1) * C, 0:T3] = wide
        weight_t[(j * 4 + 3) * C : (j * 4 + 4) * C, :] = jnp.zeros((C, 128), F32)
    flipped = [weight_t[j * 128 : (j + 1) * 128, 0:T3].T.astype(BF) for j in range(3)]
    rim_weights[0] = flipped[0]
    rim_weights[1] = flipped[2]
    weights = jnp.concatenate(
        [
            jnp.concatenate([flipped[1], flipped[2]], axis=1),
            jnp.concatenate([flipped[0], flipped[1]], axis=1),
        ],
        axis=0,
    )

    row = lax.broadcasted_iota(jnp.int32, (QY, 3 * IY), 0)
    col = lax.broadcasted_iota(jnp.int32, (QY, 3 * IY), 1)
    spread_ref[...] = jnp.where(col % IY == 2 * row + col // IY - 1, 1.0, 0.0).astype(BF)

    for plane in range(QX):
        flat_pre[plane] = pre_ref[:, plane].astype(F32).reshape(C * QZ, QY)
        for z in range(QZ):
            pre = flat_pre[plane, pl.ds(z, C, stride=QZ), :]
            gate = jax.nn.sigmoid(pre)
            hidden = (pre * gate).astype(BF).astype(F32)
            hidden_t[plane, z * T3 : (z + 1) * T3, :] = jnp.concatenate(
                [lane_shift(hidden, 1), hidden, lane_shift(hidden, -1)], axis=0
            ).astype(BF)
            scale_t[plane, z * C : (z + 1) * C, :] = gate * (1.0 + pre * (1.0 - gate))

    for plane in range(IX):
        act_t[plane, 0:C, :] = jnp.zeros((C, IY), BF)
        flat = act_ref[:, plane].astype(F32).reshape(C * IZ, IY)
        for side in range(2):
            flat_act[plane % 2, side] = flat[:, side * 128 : (side + 1) * 128]
        for z in range(IZ):
            for side in range(2):
                tile = flat_act[plane % 2, side, pl.ds(z, C, stride=IZ), :].astype(BF)
                act_t[plane, (z + 1) * C : (z + 2) * C, side * 128 : (side + 1) * 128] = tile

    for z in range(0, QZ, 2):
        slab = jnp.concatenate(
            [
                jnp.concatenate([ref[(z + h) * C : (z + h + 4) * C, :] for h in range(2)], axis=1)
                for ref in (cot0_ref, cot1_ref)
            ],
            axis=0,
        )
        terms = jnp.dot(weights, slab, preferred_element_type=F32)
        for x in range(QX):
            for h in range(2):
                part = terms[x * T3 : (x + 1) * T3, h * QY : (h + 1) * QY]
                partial_t[x, (z + h) * C : (z + h + 1) * C, :] = taps_joined(part)

    total = jnp.zeros((2 * T3, 256), F32)
    for z0 in range(0, QZ, 8):
        slab = jnp.concatenate(
            [
                jnp.concatenate([ref[z * C : (z + 3) * C, :] for z in range(z0, z0 + 8)], axis=1)
                for ref in (cot0_ref, cot1_ref)
            ],
            axis=0,
        )
        hid = jnp.concatenate(
            [
                jnp.concatenate(
                    [four_blocks(hidden_t[x, z * T3 : (z + 1) * T3, :]) for x in range(QX)], axis=0
                )
                for z in range(z0, z0 + 8)
            ],
            axis=1,
        )
        total = total + nt_dot(slab, hid)
    second_ref[0:T3, :] = total[0:T3, 128:256]
    second_ref[T3 : 2 * T3, :] = total[0:T3, 0:128] + total[T3:, 128:256]
    second_ref[2 * T3 :, :] = total[T3:, 0:128]


def pre_grads(cot_ref, weights, partial, scale, put):
    for z in range(0, QZ, 2):
        slab = jnp.concatenate([cot_ref[(z + h) * C : (z + h + 4) * C, :] for h in range(2)], axis=1)
        terms = jnp.dot(weights, slab, preferred_element_type=F32)
        for h in range(2):
            rows = slice((z + h) * C, (z + h + 1) * C)
            grad = partial[rows, :] + taps_joined(terms[:, h * QY : (h + 1) * QY])
            put(rows, (grad * scale[rows, :]).astype(BF))


def rim_kernel(cot_prev_ref, rim_weights, partial_ref, scale_ref, out_ref):
    def put(rows, value):
        out_ref[rows, :] = value

    pre_grads(cot_prev_ref, rim_weights[0], partial_ref.at[0], scale_ref.at[0], put)


def spread_plane(grad_ref, spread_ref, wide_ref):
    for z0 in range(0, QZ, 4):
        wide = jnp.dot(
            grad_ref[z0 * C : (z0 + 4) * C, :], spread_ref[...], preferred_element_type=F32
        ).astype(BF)
        for h in range(4):
            for d in range(3):
                begin = (z0 + h) * T3 + d * C
                wide_ref[begin : begin + C, :] = wide[h * C : (h + 1) * C, d * IY : (d + 1) * IY]


def main_kernel(
    cot_prev_ref, cot_next_ref, rim_weights, partial_ref, scale_ref, hidden_t, act_t, grad0_ref,
    spread_ref, second_in,
    first_ref, second_ref,
    grad1, wide, acc,
):
    def put(rows, value):
        grad1[rows, :] = value

    pre_grads(cot_next_ref, rim_weights[1], partial_ref.at[1], scale_ref.at[1], put)
    spread_plane(grad0_ref, spread_ref, wide.at[0])
    spread_plane(grad1, spread_ref, wide.at[1])

    second_ref[T3 : 2 * T3, :] = second_in[T3 : 2 * T3, :]
    for x, ref in ((0, cot_prev_ref), (1, cot_next_ref)):
        rows = slice(2 * x * T3, (2 * x + 1) * T3)
        total = second_in[rows, :]
        for z0 in range(0, QZ, 8):
            slab = jnp.concatenate([ref[z * C : (z + 3) * C, :] for z in range(z0, z0 + 8)], axis=1)
            hid = jnp.concatenate(
                [four_blocks(hidden_t[x, z * T3 : (z + 1) * T3, :]) for z in range(z0, z0 + 8)], axis=1
            )
            total = total + nt_dot(slab, hid)
        second_ref[rows, :] = total

    for z0 in range(0, QZ, 4):
        acts = jnp.concatenate(
            [
                jnp.concatenate(
                    [act_t[plane, 2 * z * C : (2 * z + 3) * C, :] for z in range(z0, z0 + 4)], axis=1
                )
                for plane in range(IX)
            ],
            axis=0,
        )
        ups = jnp.concatenate(
            [
                jnp.concatenate(
                    [four_blocks(wide[x, z * T3 : (z + 1) * T3, :]) for x in range(QX)], axis=0
                )
                for z in range(z0, z0 + 4)
            ],
            axis=1,
        )
        part = nt_dot(acts, ups)
        if z0 == 0:
            acc[...] = part
        else:
            acc[...] += part
    first_ref[0:T3, :] = acc[T3 : 2 * T3, 128:256]
    first_ref[T3 : 2 * T3, :] = acc[0:T3, 0:128] + acc[2 * T3 : 3 * T3, 128:256]
    first_ref[2 * T3 :, :] = acc[T3 : 2 * T3, 0:128] + acc[3 * T3 :, 128:256]


def last_kernel(grad_next_ref, spread_ref, act_t, first_ref, second_ref, out_ref, wide, flips, dense):
    spread_plane(grad_next_ref, spread_ref, wide)
    total = first_ref[0:T3, :]
    for z0 in range(0, QZ, 4):
        acts = jnp.concatenate(
            [act_t[IX - 1, 2 * z * C : (2 * z + 3) * C, :] for z in range(z0, z0 + 4)], axis=1
        )
        ups = jnp.concatenate(
            [four_blocks(wide[z * T3 : (z + 1) * T3, :]) for z in range(z0, z0 + 4)], axis=1
        )
        total = total + nt_dot(acts, ups)

    turned = jnp.concatenate([total, first_ref[T3:, :]], axis=0).T
    for side in range(3):
        width = min(128, TAPS - side * 128)
        flips[side, 0:128, 0:width] = turned[:, side * 128 : side * 128 + width]
    flips[3] = second_ref[...]
    lane = lax.broadcasted_iota(jnp.int32, (8, 128), 1)
    for ab in range(9):
        ab_rev = (2 - ab // 3) * 3 + (2 - ab % 3)
        for d in range(3):
            for which in range(2):
                row = jnp.zeros((8, 128), F32)
                for r in range(4):
                    if which == 0:
                        side, offset, begin = ab // 4, (ab % 4) * C, d * C + r
                    else:
                        side, offset, begin = 3, d * C, ab_rev * C + r
                    part = flips[side, pl.ds(begin, 8, stride=4), :]
                    turn = (r * C - offset) % 128
                    part = pltpu.roll(part, turn, 1) if turn else part
                    row = jnp.where(lane // C == r, part, row)
                dense[which, (ab * 3 + d) * 8 : (ab * 3 + d + 1) * 8, :] = row

    for s in range(16):
        begin = (27 * s) // 2
        for which in range(2):
            out_ref[s, which, 0:14, :] = dense[which, begin : begin + 14, :]
            out_ref[s, which, 14:16, :] = jnp.zeros((2, 128), F32)


def call(kernel, name, outs, scratch, flops, *args):
    vmem = pl.BlockSpec(memory_space=pltpu.VMEM)
    shapes = [jax.ShapeDtypeStruct(shape, dtype) for shape, dtype in outs]
    moved = sum(a.size * a.dtype.itemsize for a in args)
    return pl.pallas_call(
        kernel,
        out_shape=shapes,
        in_specs=[vmem] * len(args),
        out_specs=[vmem] * len(shapes),
        scratch_shapes=[pltpu.VMEM(shape, dtype) for shape, dtype in scratch],
        compiler_params=pltpu.CompilerParams(vmem_limit_bytes=24 * 2**20),
        cost_estimate=pl.CostEstimate(flops=flops, bytes_accessed=moved, transcendentals=0),
        name=name,
    )(*args)


def relay_cot(cot):
    plane = ((COT_ROWS, QY), BF)
    return call(cot_kernel, "relay_cot", [plane, plane], [((QX, C * QZ, QY), F32)], 10**8, cot)


def local_terms(act, pre, weight, cot0, cot1):
    return call(
        local_kernel,
        "local_terms",
        [
            ((IX, ACT_ROWS, IY), BF),
            ((QX, QZ * T3, QY), BF),
            ((QX, QZ * C, QY), F32),
            ((QX, QZ * C, QY), F32),
            ((2, T3, 128), BF),
            ((QY, 3 * IY), BF),
            ((TAPS, 128), F32),
        ],
        [((2, 2, C * IZ, 128), F32), ((QX, C * QZ, QY), F32), ((3 * 128, 128), F32)],
        5 * 10**9,
        act, pre, weight, cot0, cot1,
    )


def rim_grad(cot_prev, rim_weights, partial, scale):
    return call(
        rim_kernel, "rim_grad", [((QZ * C, QY), BF)], [], 10**9, cot_prev, rim_weights, partial, scale
    )[0]


def main_terms(*args):
    return call(
        main_kernel,
        "main_terms",
        [((TAPS, 128), F32), ((TAPS, 128), F32)],
        [((QZ * C, QY), BF), ((QX, QZ * T3, IY), BF), ((4 * T3, 256), F32)],
        5 * 10**9,
        *args,
    )


def last_terms(*args):
    return call(
        last_kernel,
        "last_terms",
        [((16, 2, 16, 128), F32)],
        [((QZ * T3, IY), BF), ((4, TAPS, 128), F32), ((2, 216, 128), F32)],
        10**9,
        *args,
    )[0]


def moved(x, axis, by):
    length = lax.axis_size(axis)
    pairs = [(i, i + by) for i in range(length) if 0 <= i + by < length]
    return lax.ppermute(x, axis, pairs)


def on_device(activations, preact, cotangent, conv_weight):
    act, pre, cot = activations[0], preact[0], cotangent[0]
    cot0, cot1 = relay_cot(cot)
    cot_prev = moved(cot1, "space", 1)
    cot_next = moved(cot0, "space", -1)
    act_t, hidden_t, scale, partial, rim_weights, spread, second = local_terms(
        act, pre, conv_weight, cot0, cot1
    )
    grad0 = rim_grad(cot_prev, rim_weights, partial, scale)
    grad_next = moved(grad0, "space", -1)
    first, second = main_terms(
        cot_prev, cot_next, rim_weights, partial, scale, hidden_t, act_t, grad0, spread, second
    )
    terms = last_terms(grad_next, spread, act_t, first, second)
    shares = lax.all_to_all(terms.reshape(32, 16, 128), ("space", "lane"), 0, 0, tiled=True)
    share = jnp.sum(shares, axis=0)
    copies = lax.all_to_all(
        jnp.broadcast_to(share[None], (16, 16, 128)), ("deep", "lane"), 0, 0, tiled=True
    )
    total = jnp.sum(copies.reshape(8, 2, 16, 128), axis=0)[:, :14].reshape(2, 14 * 128)
    odd = lax.axis_index("space") % 2
    return lax.dynamic_slice(total, (0, 64 * odd), (2, 1728))


def solution(mesh):
    split = Mesh(mesh.devices.reshape(16, 8, 2), ("space", "deep", "lane"))
    rows = P(("deep", "lane"), None, "space", None, None)
    return jax.shard_map(
        on_device,
        mesh=split,
        in_specs=(rows, rows, rows, P()),
        out_specs=P(None, "space"),
        check_vma=False,
    )
```

time: 495 us -> 60.9 us (0.12); the launches traced: 488 us -> 60.2 us
  waiting for transfers between devices: 140 us -> 10.3 us
  local copies, waits for them, and re-layouts: 128 us -> 6.17 us
  matrix products: 121 us -> 0 us
  blocking collectives: 63.1 us -> 16.3 us
  between operations: 13.6 us -> 0.12 us
  other arithmetic: 12.1 us -> 0.05 us
  starting transfers between devices: 9.22 us -> 18.7 us
  Pallas kernels: 0 us -> 8.47 us
    unnamed x2 -> x0, waiting for transfers between devices: 140 us -> none
    broadcast_in_dim x3 -> x1, local copies, waits for them, and re-layouts: 90 us -> 0.66 us  [on_device(): jnp.broadcast_to(share[None], (16, 16, 128))]
    transpose x1 -> x0, matrix products: 71.1 us -> none  [first_terms(): jnp.transpose(first_raw, (2, 3, 4, 1, 0)).reshape(27, channels, channels)]
    psum x1 -> x0, blocking collectives: 63.1 us -> none  [on_device(): result = lax.psum(shared, 'replica')]
    conv_general_dilated x2 -> x0, matrix products: 50.3 us -> none  [volume_conv(): lax.conv_general_dilated(lhs, rhs, (1, 1, 1), 'VALID', rhs_dilation=dilat...]
    unnamed x18 -> x10, local copies, waits for them, and re-layouts: 22.5 us -> 4.82 us
    all_to_all x0 -> x1, blocking collectives: none -> 16.3 us  [on_device(): lax.all_to_all(terms.reshape(32, 16, 128), ('space', 'lane'), 0, 0, tiled...]
    convert_element_type x2 -> x0, local copies, waits for them, and re-layouts: 9.95 us -> none  [the longest x1 5.58 us: second_terms(): (hidden_grad * gate_val * (1.0 + pre_float * (1.0 - gate_val))).astype(jn...]
  transfers between devices with their start and end apart: 4 -> 4, of which waited for: 1 -> 2; matrix products, arithmetic and copies ran while one was open for 20% -> 0% of each run, Pallas kernels for 0% -> 11%
where the time goes in v2:
time: 60.9 us; the launch traced here: 60.2 us
  starting transfers between devices  18.7 us (31%)
  blocking collectives  16.3 us (27%)
  waiting for transfers between devices  10.3 us (17%)
  Pallas kernels  8.47 us (14%)
  local copies, waits for them, and re-layouts  6.17 us (10%)
    all_to_all x1, blocking collectives, on_device(): lax.all_to_all(terms.reshape(32, 16, 128), ('space', 'lane'), 0, 0, tiled...  16.3 us
    all_to_all x1, waiting for transfers between devices, on_device(): lax.all_to_all(jnp.broadcast_to(share[None], (16, 16, 128)), ('deep', 'la...  9.9 us
    ppermute x3, starting transfers between devices, moved(): return lax.ppermute(x, axis, pairs)  9.89 us
    all_to_all x1, starting transfers between devices, on_device(): lax.all_to_all(jnp.broadcast_to(share[None], (16, 16, 128)), ('deep', 'la...  8.81 us
    pallas_call x5, Pallas kernels, call(): pl.pallas_call(kernel, out_shape=shapes, in_specs=[vmem] * len(args), out...  8.47 us
    unnamed x10, local copies, waits for them, and re-layouts  4.82 us
  transfers between devices with their start and end apart: 4, of which 2 were waited for; matrix products, arithmetic and copies ran while one was open for 0% of the time, Pallas kernels for 11%

profile of v2, /device:TPU:2, one launch (start us, length us, event | category | flops | bytes accessed | tf_op | source)
XLA Modules:
  0.0 60.2 jit_solution(17558405162748185422)
XLA Ops:
  0.0 0.0 copy-start
  0.0 1.0 %copy-done = bf16[1,32,2,24,128]{4,3,2,1,0:T(8,128)(2,1)S(1)} copy-done((bf16[1,32,2,24,128]{4,3,2,1,0:T(8,128)(2,1)S(1)}, bf16[1,32,2,24,128]{4,3,2,1,0:T(8,128)(2,1)}, u32[]{:S(2)}) %copy-start) | copy-done | bytes 393240
  1.0 0.2 relay_cot.1
  1.2 1.9 %collective-permute-start = (bf16[864,128]{1,0:T(8,128)(2,1)S(1)}, bf16[864,128]{1,0:T(8,128)(2,1)S(1)}, u32[]{:S(2)}, u32[]{:S(2)}) collective-permute-start(bf16[864,128]{1,0:T(8,128)(2,1)S(1)} %get-tuple-element.16.cot1_ref), channel_id=1, source_target_pairs={{0,16},{16,32},{32,48},{48,64},{64,80},{80,96},{96,112},{112,128},... | collective-permute-start | bytes 663560 | tf_op jit(solution)/shard_map/ppermute | solution.py:328
  3.1 6.0 %collective-permute-start.2 = (bf16[864,128]{1,0:T(8,128)(2,1)S(1)}, bf16[864,128]{1,0:T(8,128)(2,1)S(1)}, u32[]{:S(2)}, u32[]{:S(2)}) collective-permute-start(bf16[864,128]{1,0:T(8,128)(2,1)S(1)} %get-tuple-element.17.cot0_ref), channel_id=1, source_target_pairs={{16,0},{32,16},{48,32},{64,48},{80,64},{96,80},{112,96},{128,112},... | collective-permute-start | bytes 663560 | tf_op jit(solution)/shard_map/ppermute | solution.py:328
  9.2 0.0 copy-start.1
  9.2 1.9 %copy-done.1 = bf16[1,32,4,48,256]{4,3,2,1,0:T(8,128)(2,1)S(1)} copy-done((bf16[1,32,4,48,256]{4,3,2,1,0:T(8,128)(2,1)S(1)}, bf16[1,32,4,48,256]{4,3,2,1,0:T(8,128)(2,1)}, u32[]{:S(2)}) %copy-start.1) | copy-done | bytes 3145752
  11.1 0.0 copy-start.2
  11.1 1.0 %copy-done.2 = bf16[1,32,2,24,128]{4,3,2,1,0:T(8,128)(2,1)S(1)} copy-done((bf16[1,32,2,24,128]{4,3,2,1,0:T(8,128)(2,1)S(1)}, bf16[1,32,2,24,128]{4,3,2,1,0:T(8,128)(2,1)}, u32[]{:S(2)}) %copy-start.2) | copy-done | bytes 393240
  12.1 0.0 copy-start.3
  12.1 0.9 %copy-done.3 = bf16[27,32,32]{2,1,0:T(8,128)(2,1)S(1)} copy-done((bf16[27,32,32]{2,1,0:T(8,128)(2,1)S(1)}, bf16[27,32,32]{2,1,0:T(8,128)(2,1)}, u32[]{:S(2)}) %copy-start.3) | copy-done | bytes 55320
  13.0 3.8 %local_terms.1 = (bf16[4,1568,256]{2,1,0:T(8,128)(2,1)S(1)}, bf16[2,2304,128]{2,1,0:T(8,128)(2,1)S(1)}, f32[2,768,128]{2,1,0:T(8,128)S(1)}, f32[2,768,128]{2,1,0...) custom-call(bf16[32,4,48,256]{3,2,1,0:T(8,128)(2,1)S(1)} %bitcast.12, ...), custom_call_target="tpu_custom_call" | custom-call | flops 5000000000 | bytes 4036608 | tf_op jit(solution)/shard_map/local_terms/pallas_call | solution.py:261
  16.8 0.0 collective-permute-done.cot_prev_ref
  16.8 0.4 rim_grad.1.grad0_ref
  17.2 1.9 %collective-permute-start.1 = (bf16[768,128]{1,0:T(8,128)(2,1)S(1)}, bf16[768,128]{1,0:T(8,128)(2,1)S(1)}, u32[]{:S(2)}, u32[]{:S(2)}) collective-permute-start(bf16[768,128]{1,0:T(8,128)(2,1)S(1)} %rim_grad.1.grad0_ref), channel_id=1, source_target_pairs={{16,0},{32,16},{48,32},{64,48},{80,64},{96,80},{112,96},{128,112},... | collective-permute-start | bytes 589832 | tf_op jit(solution)/shard_map/ppermute | solution.py:328
  19.2 0.0 collective-permute-done.2.cot_next_ref
  19.2 2.7 %main_terms.1 = (f32[288,128]{1,0:T(8,128)S(1)}, f32[288,128]{1,0:T(8,128)S(1)}) custom-call(bf16[864,128]{1,0:T(8,128)(2,1)S(1)} %collective-permute-done.cot_prev_ref, bf16[864,128]{1,0:T(8,128)(2,1)S(1)} %collective-permute-done.2.cot_next_ref, bf16[2,96,128]{2,1,0:T(8,128)(2,1)S(1)} %get-tuple-element.18.rim_weights, ...), custom_call_target="tpu_custom_call" | custom-call | flops 5000000000 | bytes 6995968 | tf_op jit(solution)/shard_map/main_terms/pallas_call | solution.py:261
  21.9 0.4 collective-permute-done.1.grad_next_ref
  22.3 1.4 %last_terms.1 = f32[16,2,16,128]{3,2,1,0:T(8,128)S(1)} custom-call(bf16[768,128]{1,0:T(8,128)(2,1)S(1)} %collective-permute-done.1.grad_next_ref, bf16[128,768]{1,0:T(8,128)(2,1)S(1)} %get-tuple-element.21.spread_ref, bf16[4,1568,256]{2,1,0:T(8,128)(2,1)S(1)} %get-tuple-element.22.act_t, f32[288,128]{1,0:T(8,128)S(1)} %get-tuple-element.25.first_ref, ...), custom_call_target="tpu_custom_call" | custom-call | flops 1000000000 | bytes 3899392 | tf_op jit(solution)/shard_map/last_terms/pallas_call | solution.py:261
  23.7 16.3 %all_to_all.10 = f32[32,16,128]{2,1,0:T(8,128)S(1)} all-to-all(f32[32,16,128]{2,1,0:T(8,128)S(1)} %bitcast.10), channel_id=1, replica_groups=mesh['space'=16,'deep'=8,'lane'=2] {'space','lane'}, dimensions={0} | all-to-all | bytes 524288 | tf_op jit(solution)/shard_map/all_to_all | solution.py:345
  40.1 0.7 %broadcast_in_dim.2 = f32[16,16,128]{2,1,0:T(8,128)} broadcast(f32[16,128]{1,0:T(8,128)S(1)} %reduce_sum.18), dimensions={1,2} | broadcast | bytes 139264 | tf_op jit(solution)/shard_map/broadcast_in_dim | solution.py:348
  40.7 8.8 %all-to-all-start.1 = ((f32[16,16,128]{2,1,0:T(8,128)}), f32[16,16,128]{2,1,0:T(8,128)S(1)}, u32[]{:S(2)}, u32[]{:S(2)}) async-start(f32[16,16,128]{2,1,0:T(8,128)} %broadcast_in_dim.2), calls=%async_computation.1 | async-start | bytes 262144 | tf_op jit(solution)/shard_map/all_to_all | solution.py:347
  49.6 9.9 %all-to-all-done.1 = f32[16,16,128]{2,1,0:T(8,128)S(1)} async-done(((f32[16,16,128]{2,1,0:T(8,128)}), f32[16,16,128]{2,1,0:T(8,128)S(1)}, u32[]{:S(2)}, u32[]{:S(2)}) %all-to-all-start.1) | async-done | bytes 131104 | tf_op jit(solution)/shard_map/all_to_all | solution.py:347
  59.5 0.7 %constant_dynamic-slice_fusion = f32[2,1728]{1,0:T(2,128)} fusion(f32[2,1792]{1,0:T(2,128)S(1)} %bitcast.15, s32[]{:T(128)S(6)} %select_n.11), kind=kLoop, calls=%fused_computation.2 | loop fusion | bytes 27652 | tf_op jit(solution)/shard_map/dynamic_slice | solution.py:352
  (4 shorter events, 0.1 us)
Async XLA Ops:
  0.0 1.0 %copy-start = (bf16[1,32,2,24,128]{4,3,2,1,0:T(8,128)(2,1)S(1)}, bf16[1,32,2,24,128]{4,3,2,1,0:T(8,128)(2,1)}, u32[]{:S(2)}) copy-start(bf16[1,32,2,24,128]{4,3,2,1,0:T(8,128)(2,1)} %param.6) | copy-start | bytes 1179652
  1.2 15.6 %collective-permute-start = (bf16[864,128]{1,0:T(8,128)(2,1)S(1)}, bf16[864,128]{1,0:T(8,128)(2,1)S(1)}, u32[]{:S(2)}, u32[]{:S(2)}) collective-permute-start(bf16[864,128]{1,0:T(8,128)(2,1)S(1)} %get-tuple-element.16.cot1_ref), channel_id=1, source_target_pairs={{0,16},{16,32},{32,48},{48,64},{64,80},{80,96},{96,112},{112,128},... | collective-permute-start | bytes 663560 | tf_op jit(solution)/shard_map/ppermute | solution.py:328
  3.1 16.0 %collective-permute-start.2 = (bf16[864,128]{1,0:T(8,128)(2,1)S(1)}, bf16[864,128]{1,0:T(8,128)(2,1)S(1)}, u32[]{:S(2)}, u32[]{:S(2)}) collective-permute-start(bf16[864,128]{1,0:T(8,128)(2,1)S(1)} %get-tuple-element.17.cot0_ref), channel_id=1, source_target_pairs={{16,0},{32,16},{48,32},{64,48},{80,64},{96,80},{112,96},{128,112},... | collective-permute-start | bytes 663560 | tf_op jit(solution)/shard_map/ppermute | solution.py:328
  9.2 1.9 %copy-start.1 = (bf16[1,32,4,48,256]{4,3,2,1,0:T(8,128)(2,1)S(1)}, bf16[1,32,4,48,256]{4,3,2,1,0:T(8,128)(2,1)}, u32[]{:S(2)}) copy-start(bf16[1,32,4,48,256]{4,3,2,1,0:T(8,128)(2,1)} %param.4) | copy-start | bytes 9437188
  11.1 1.0 %copy-start.2 = (bf16[1,32,2,24,128]{4,3,2,1,0:T(8,128)(2,1)S(1)}, bf16[1,32,2,24,128]{4,3,2,1,0:T(8,128)(2,1)}, u32[]{:S(2)}) copy-start(bf16[1,32,2,24,128]{4,3,2,1,0:T(8,128)(2,1)} %param.5) | copy-start | bytes 1179652
  12.1 0.9 %copy-start.3 = (bf16[27,32,32]{2,1,0:T(8,128)(2,1)S(1)}, bf16[27,32,32]{2,1,0:T(8,128)(2,1)}, u32[]{:S(2)}) copy-start(bf16[27,32,32]{2,1,0:T(8,128)(2,1)} %weight_ref.1) | copy-start | bytes 165892
  17.2 5.1 %collective-permute-start.1 = (bf16[768,128]{1,0:T(8,128)(2,1)S(1)}, bf16[768,128]{1,0:T(8,128)(2,1)S(1)}, u32[]{:S(2)}, u32[]{:S(2)}) collective-permute-start(bf16[768,128]{1,0:T(8,128)(2,1)S(1)} %rim_grad.1.grad0_ref), channel_id=1, source_target_pairs={{16,0},{32,16},{48,32},{64,48},{80,64},{96,80},{112,96},{128,112},... | collective-permute-start | bytes 589832 | tf_op jit(solution)/shard_map/ppermute | solution.py:328
  40.7 18.7 %all-to-all-start.1 = ((f32[16,16,128]{2,1,0:T(8,128)}), f32[16,16,128]{2,1,0:T(8,128)S(1)}, u32[]{:S(2)}, u32[]{:S(2)}) async-start(f32[16,16,128]{2,1,0:T(8,128)} %broadcast_in_dim.2), calls=%async_computation.1 | async-start | bytes 262144 | tf_op jit(solution)/shard_map/all_to_all | solution.py:347

commit v3 on v2

--- a/solution.py
+++ b/solution.py
@@ -36,21 +36,33 @@
     return jnp.concatenate([rows, rows[0:C]], axis=0)
 
 
-def cot_kernel(cot_ref, first_ref, last_ref, flat):
-    for plane, out_ref in ((0, first_ref), (1, last_ref)):
+def on_odd():
+    return lax.rem(lax.axis_index("space"), 2) == 1
+
+
+def cot_kernel(cot_ref, planes_ref, chip_ref, far_ref, flat):
+    odd = on_odd()
+    for plane in range(QX):
+        planes_ref[plane, 0:C, :] = jnp.zeros((C, QY), BF)
+        planes_ref[plane, (QZ + 1) * C :, :] = jnp.zeros((2 * C, QY), BF)
+    for plane in range(QX):
         flat[plane] = cot_ref[:, plane].astype(F32).reshape(C * QZ, QY)
-        out_ref[0:C, :] = jnp.zeros((C, QY), BF)
-        out_ref[(QZ + 1) * C :, :] = jnp.zeros((2 * C, QY), BF)
         for z in range(QZ):
             block = flat[plane, pl.ds(z, C, stride=QZ), :]
-            out_ref[(z + 1) * C : (z + 2) * C, :] = block.astype(BF)
+            planes_ref[plane, (z + 1) * C : (z + 2) * C, :] = block.astype(BF)
+    chip_ref[...] = jnp.where(odd, planes_ref[0], planes_ref[1])
+    far_ref[...] = jnp.where(odd, planes_ref[1], planes_ref[0])
 
 
 def local_kernel(
-    act_ref, pre_ref, weight_ref, cot0_ref, cot1_ref,
+    act_ref, pre_ref, weight_ref, planes_ref,
     act_t, hidden_t, scale_t, partial_t, rim_weights, spread_ref, second_ref,
     flat_act, flat_pre, weight_t,
 ):
+    row = lax.broadcasted_iota(jnp.int32, (QY, 3 * IY), 0)
+    col = lax.broadcasted_iota(jnp.int32, (QY, 3 * IY), 1)
+    spread_ref[...] = jnp.where(col % IY == 2 * row + col // IY - 1, 1.0, 0.0).astype(BF)
+
     for j in range(3):
         for k in range(3):
             base = (2 - j) * 9 + (2 - k) * 3
@@ -68,10 +80,6 @@
         axis=0,
     )
 
-    row = lax.broadcasted_iota(jnp.int32, (QY, 3 * IY), 0)
-    col = lax.broadcasted_iota(jnp.int32, (QY, 3 * IY), 1)
-    spread_ref[...] = jnp.where(col % IY == 2 * row + col // IY - 1, 1.0, 0.0).astype(BF)
-
     for plane in range(QX):
         flat_pre[plane] = pre_ref[:, plane].astype(F32).reshape(C * QZ, QY)
         for z in range(QZ):
@@ -96,8 +104,10 @@
     for z in range(0, QZ, 2):
         slab = jnp.concatenate(
             [
-                jnp.concatenate([ref[(z + h) * C : (z + h + 4) * C, :] for h in range(2)], axis=1)
-                for ref in (cot0_ref, cot1_ref)
+                jnp.concatenate(
+                    [planes_ref[x, (z + h) * C : (z + h + 4) * C, :] for h in range(2)], axis=1
+                )
+                for x in range(QX)
             ],
             axis=0,
         )
@@ -111,8 +121,10 @@
     for z0 in range(0, QZ, 8):
         slab = jnp.concatenate(
             [
-                jnp.concatenate([ref[z * C : (z + 3) * C, :] for z in range(z0, z0 + 8)], axis=1)
-                for ref in (cot0_ref, cot1_ref)
+                jnp.concatenate(
+                    [planes_ref[x, z * C : (z + 3) * C, :] for z in range(z0, z0 + 8)], axis=1
+                )
+                for x in range(QX)
             ],
             axis=0,
         )
@@ -141,11 +153,15 @@
             put(rows, (grad * scale[rows, :]).astype(BF))
 
 
-def rim_kernel(cot_prev_ref, rim_weights, partial_ref, scale_ref, out_ref):
+def rim_kernel(chip_ref, far_ref, rim_weights, partial_ref, scale_ref, out_ref, halo_ref):
+    odd = on_odd()
+    halo_ref[0] = jnp.where(odd, chip_ref[...], far_ref[...])
+    halo_ref[1] = jnp.where(odd, far_ref[...], chip_ref[...])
+
     def put(rows, value):
         out_ref[rows, :] = value
 
-    pre_grads(cot_prev_ref, rim_weights[0], partial_ref.at[0], scale_ref.at[0], put)
+    pre_grads(halo_ref.at[0], rim_weights[0], partial_ref.at[0], scale_ref.at[0], put)
 
 
 def spread_plane(grad_ref, spread_ref, wide_ref):
@@ -159,30 +175,50 @@
                 wide_ref[begin : begin + C, :] = wide[h * C : (h + 1) * C, d * IY : (d + 1) * IY]
 
 
+def dense_row(flips, second, ab, d):
+    lane = lax.broadcasted_iota(jnp.int32, (8, 128), 1)
+    row = jnp.zeros((8, 128), F32)
+    for r in range(4):
+        if second:
+            ab_rev = (2 - ab // 3) * 3 + (2 - ab % 3)
+            side, offset, begin = 0, d * C, ab_rev * C + r
+        else:
+            side, offset, begin = ab // 4, (ab % 4) * C, d * C + r
+        part = flips[side, pl.ds(begin, 8, stride=4), :]
+        turn = (r * C - offset) % 128
+        part = pltpu.roll(part, turn, 1) if turn else part
+        row = jnp.where(lane // C == r, part, row)
+    return row
+
+
 def main_kernel(
-    cot_prev_ref, cot_next_ref, rim_weights, partial_ref, scale_ref, hidden_t, act_t, grad0_ref,
+    halo_ref, rim_weights, partial_ref, scale_ref, hidden_t, act_t, grad0_ref,
     spread_ref, second_in,
-    first_ref, second_ref,
-    grad1, wide, acc,
+    first_ref, dense_ref,
+    grad1, wide, acc, second_ref, flips,
 ):
     def put(rows, value):
         grad1[rows, :] = value
 
-    pre_grads(cot_next_ref, rim_weights[1], partial_ref.at[1], scale_ref.at[1], put)
+    pre_grads(halo_ref.at[1], rim_weights[1], partial_ref.at[1], scale_ref.at[1], put)
     spread_plane(grad0_ref, spread_ref, wide.at[0])
     spread_plane(grad1, spread_ref, wide.at[1])
 
-    second_ref[T3 : 2 * T3, :] = second_in[T3 : 2 * T3, :]
-    for x, ref in ((0, cot_prev_ref), (1, cot_next_ref)):
+    second_ref[0, T3 : 2 * T3, :] = second_in[T3 : 2 * T3, :]
+    for x in range(QX):
         rows = slice(2 * x * T3, (2 * x + 1) * T3)
         total = second_in[rows, :]
         for z0 in range(0, QZ, 8):
-            slab = jnp.concatenate([ref[z * C : (z + 3) * C, :] for z in range(z0, z0 + 8)], axis=1)
+            slab = jnp.concatenate([halo_ref[x, z * C : (z + 3) * C, :] for z in range(z0, z0 + 8)], axis=1)
             hid = jnp.concatenate(
                 [four_blocks(hidden_t[x, z * T3 : (z + 1) * T3, :]) for z in range(z0, z0 + 8)], axis=1
             )
             total = total + nt_dot(slab, hid)
-        second_ref[rows, :] = total
+        second_ref[0, rows, :] = total
+    for ab in range(9):
+        for d in range(3):
+            begin = (ab * 3 + d) * 8
+            dense_ref[1, begin : begin + 8, :] = dense_row(second_ref, True, ab, d)
 
     for z0 in range(0, QZ, 4):
         acts = jnp.concatenate(
@@ -208,14 +244,25 @@
             acc[...] = part
         else:
             acc[...] += part
-    first_ref[0:T3, :] = acc[T3 : 2 * T3, 128:256]
-    first_ref[T3 : 2 * T3, :] = acc[0:T3, 0:128] + acc[2 * T3 : 3 * T3, 128:256]
-    first_ref[2 * T3 :, :] = acc[T3 : 2 * T3, 0:128] + acc[3 * T3 :, 128:256]
-
-
-def last_kernel(grad_next_ref, spread_ref, act_t, first_ref, second_ref, out_ref, wide, flips, dense):
+    first_ref[...] = acc[T3 : 2 * T3, 128:256]
+    turned = jnp.concatenate(
+        [
+            acc[0:T3, 0:128] + acc[2 * T3 : 3 * T3, 128:256],
+            acc[T3 : 2 * T3, 0:128] + acc[3 * T3 :, 128:256],
+        ],
+        axis=0,
+    ).T
+    flips[0] = turned[:, 0:128]
+    flips[1, :, 0 : 2 * T3 - 128] = turned[:, 128:]
+    for ab in range(6):
+        for d in range(3):
+            begin = ((ab + 3) * 3 + d) * 8
+            dense_ref[0, begin : begin + 8, :] = dense_row(flips, False, ab, d)
+
+
+def last_kernel(grad_next_ref, spread_ref, act_t, first_ref, dense_ref, out_ref, wide, flips, head):
     spread_plane(grad_next_ref, spread_ref, wide)
-    total = first_ref[0:T3, :]
+    total = first_ref[...]
     for z0 in range(0, QZ, 4):
         acts = jnp.concatenate(
             [act_t[IX - 1, 2 * z * C : (2 * z + 3) * C, :] for z in range(z0, z0 + 4)], axis=1
@@ -225,45 +272,35 @@
         )
         total = total + nt_dot(acts, ups)
 
-    turned = jnp.concatenate([total, first_ref[T3:, :]], axis=0).T
-    for side in range(3):
-        width = min(128, TAPS - side * 128)
-        flips[side, 0:128, 0:width] = turned[:, side * 128 : side * 128 + width]
-    flips[3] = second_ref[...]
-    lane = lax.broadcasted_iota(jnp.int32, (8, 128), 1)
-    for ab in range(9):
-        ab_rev = (2 - ab // 3) * 3 + (2 - ab % 3)
+    flips[0, :, 0:T3] = total.T
+    for ab in range(3):
         for d in range(3):
-            for which in range(2):
-                row = jnp.zeros((8, 128), F32)
-                for r in range(4):
-                    if which == 0:
-                        side, offset, begin = ab // 4, (ab % 4) * C, d * C + r
-                    else:
-                        side, offset, begin = 3, d * C, ab_rev * C + r
-                    part = flips[side, pl.ds(begin, 8, stride=4), :]
-                    turn = (r * C - offset) % 128
-                    part = pltpu.roll(part, turn, 1) if turn else part
-                    row = jnp.where(lane // C == r, part, row)
-                dense[which, (ab * 3 + d) * 8 : (ab * 3 + d + 1) * 8, :] = row
+            begin = (ab * 3 + d) * 8
+            head[begin : begin + 8, :] = dense_row(flips, False, ab, d)
 
     for s in range(16):
         begin = (27 * s) // 2
         for which in range(2):
-            out_ref[s, which, 0:14, :] = dense[which, begin : begin + 14, :]
+            known = min(max(72 - begin, 0), 14) if which == 0 else 0
+            if known:
+                out_ref[s, which, 0:known, :] = head[begin : begin + known, :]
+            if known < 14:
+                out_ref[s, which, known:14, :] = dense_ref[which, begin + known : begin + 14, :]
             out_ref[s, which, 14:16, :] = jnp.zeros((2, 128), F32)
 
 
+VMEM = pltpu.VMEM
+
+
 def call(kernel, name, outs, scratch, flops, *args):
-    vmem = pl.BlockSpec(memory_space=pltpu.VMEM)
     shapes = [jax.ShapeDtypeStruct(shape, dtype) for shape, dtype in outs]
     moved = sum(a.size * a.dtype.itemsize for a in args)
     return pl.pallas_call(
         kernel,
         out_shape=shapes,
-        in_specs=[vmem] * len(args),
-        out_specs=[vmem] * len(shapes),
-        scratch_shapes=[pltpu.VMEM(shape, dtype) for shape, dtype in scratch],
+        in_specs=[pl.BlockSpec(memory_space=VMEM)] * len(args),
+        out_specs=[pl.BlockSpec(memory_space=VMEM)] * len(shapes),
+        scratch_shapes=scratch,
         compiler_params=pltpu.CompilerParams(vmem_limit_bytes=24 * 2**20),
         cost_estimate=pl.CostEstimate(flops=flops, bytes_accessed=moved, transcendentals=0),
         name=name,
@@ -272,10 +309,17 @@
 
 def relay_cot(cot):
     plane = ((COT_ROWS, QY), BF)
-    return call(cot_kernel, "relay_cot", [plane, plane], [((QX, C * QZ, QY), F32)], 10**8, cot)
-
-
-def local_terms(act, pre, weight, cot0, cot1):
+    return call(
+        cot_kernel,
+        "relay_cot",
+        [((QX, COT_ROWS, QY), BF), plane, plane],
+        [VMEM((QX, C * QZ, QY), F32)],
+        10**10,
+        cot,
+    )
+
+
+def local_terms(act, pre, weight, planes):
     return call(
         local_kernel,
         "local_terms",
@@ -288,24 +332,39 @@
             ((QY, 3 * IY), BF),
             ((TAPS, 128), F32),
         ],
-        [((2, 2, C * IZ, 128), F32), ((QX, C * QZ, QY), F32), ((3 * 128, 128), F32)],
+        [
+            VMEM((2, 2, C * IZ, 128), F32),
+            VMEM((QX, C * QZ, QY), F32),
+            VMEM((3 * 128, 128), F32),
+        ],
         5 * 10**9,
-        act, pre, weight, cot0, cot1,
-    )
-
-
-def rim_grad(cot_prev, rim_weights, partial, scale):
+        act, pre, weight, planes,
+    )
+
+
+def rim_grad(*args):
     return call(
-        rim_kernel, "rim_grad", [((QZ * C, QY), BF)], [], 10**9, cot_prev, rim_weights, partial, scale
-    )[0]
+        rim_kernel,
+        "rim_grad",
+        [((QZ * C, QY), BF), ((QX, COT_ROWS, QY), BF)],
+        [],
+        10**9,
+        *args,
+    )
 
 
 def main_terms(*args):
     return call(
         main_kernel,
         "main_terms",
-        [((TAPS, 128), F32), ((TAPS, 128), F32)],
-        [((QZ * C, QY), BF), ((QX, QZ * T3, IY), BF), ((4 * T3, 256), F32)],
+        [((T3, 128), F32), ((2, 216, 128), F32)],
+        [
+            VMEM((QZ * C, QY), BF),
+            VMEM((QX, QZ * T3, IY), BF),
+            VMEM((4 * T3, 256), F32),
+            VMEM((1, TAPS, 128), F32),
+            VMEM((2, 128, 128), F32),
+        ],
         5 * 10**9,
         *args,
     )
@@ -316,32 +375,34 @@
         last_kernel,
         "last_terms",
         [((16, 2, 16, 128), F32)],
-        [((QZ * T3, IY), BF), ((4, TAPS, 128), F32), ((2, 216, 128), F32)],
+        [VMEM((QZ * T3, IY), BF), VMEM((1, 128, 128), F32), VMEM((72, 128), F32)],
         10**9,
         *args,
     )[0]
 
 
-def moved(x, axis, by):
-    length = lax.axis_size(axis)
-    pairs = [(i, i + by) for i in range(length) if 0 <= i + by < length]
-    return lax.ppermute(x, axis, pairs)
+def swapped(x, begin):
+    pairs = []
+    for i in range(begin, lax.axis_size("space") - 1, 2):
+        pairs += [(i, i + 1), (i + 1, i)]
+    return lax.ppermute(x, "space", pairs)
 
 
 def on_device(activations, preact, cotangent, conv_weight):
     act, pre, cot = activations[0], preact[0], cotangent[0]
-    cot0, cot1 = relay_cot(cot)
-    cot_prev = moved(cot1, "space", 1)
-    cot_next = moved(cot0, "space", -1)
+    planes, to_chip, to_far = relay_cot(cot)
+    far = swapped(to_far, 1)
+    chip = swapped(to_chip, 0)
     act_t, hidden_t, scale, partial, rim_weights, spread, second = local_terms(
-        act, pre, conv_weight, cot0, cot1
-    )
-    grad0 = rim_grad(cot_prev, rim_weights, partial, scale)
-    grad_next = moved(grad0, "space", -1)
-    first, second = main_terms(
-        cot_prev, cot_next, rim_weights, partial, scale, hidden_t, act_t, grad0, spread, second
-    )
-    terms = last_terms(grad_next, spread, act_t, first, second)
+        act, pre, conv_weight, planes
+    )
+    grad0, halo = rim_grad(chip, far, rim_weights, partial, scale)
+    count = lax.axis_size("space")
+    grad_next = lax.ppermute(grad0, "space", [(i + 1, i) for i in range(count - 1)])
+    first, dense = main_terms(
+        halo, rim_weights, partial, scale, hidden_t, act_t, grad0, spread, second
+    )
+    terms = last_terms(grad_next, spread, act_t, first, dense)
     shares = lax.all_to_all(terms.reshape(32, 16, 128), ("space", "lane"), 0, 0, tiled=True)
     share = jnp.sum(shares, axis=0)
     copies = lax.all_to_all(

time: 60.9 us -> 58.1 us (0.954)
  local copies, waits for them, and re-layouts: 6.17 us -> 2.37 us
  starting transfers between devices: 18.7 us -> 19.4 us
    unnamed x10, local copies, waits for them, and re-layouts: 4.82 us -> 1.02 us
    ppermute x3, starting transfers between devices: 9.89 us -> 10.5 us  [the longest x2 5.39 us: swapped(): return lax.ppermute(x, 'space', pairs)]
  transfers between devices with their start and end apart: 4 -> 4, of which waited for: 2 -> 3; matrix products, arithmetic and copies ran while one was open for 0% -> 0% of each run, Pallas kernels for 11% -> 12%
where the time goes in v3:
time: 58.1 us; the launch traced here: 57.5 us
  starting transfers between devices  19.4 us (33%)
  blocking collectives  15.9 us (27%)
  waiting for transfers between devices  10.9 us (19%)
  Pallas kernels  8.78 us (15%)
  local copies, waits for them, and re-layouts  2.37 us (4%)
    all_to_all x1, blocking collectives, on_device(): lax.all_to_all(terms.reshape(32, 16, 128), ('space', 'lane'), 0, 0, tiled...  15.9 us
    all_to_all x1, waiting for transfers between devices, on_device(): lax.all_to_all(jnp.broadcast_to(share[None], (16, 16, 128)), ('deep', 'la...  9.9 us
    all_to_all x1, starting transfers between devices, on_device(): lax.all_to_all(jnp.broadcast_to(share[None], (16, 16, 128)), ('deep', 'la...  8.81 us
    pallas_call x5, Pallas kernels, call(): pl.pallas_call(kernel, out_shape=shapes, in_specs=[pl.BlockSpec(memory_sp...  8.78 us
    ppermute x2, starting transfers between devices, swapped(): return lax.ppermute(x, 'space', pairs)  5.39 us
    ppermute x1, starting transfers between devices, on_device(): lax.ppermute(grad0, 'space', [(i + 1, i) for i in range(count - 1)])  5.16 us
  transfers between devices with their start and end apart: 4, of which 3 were waited for; matrix products, arithmetic and copies ran while one was open for 0% of the time, Pallas kernels for 12%

profile of v3, /device:TPU:2, one launch (start us, length us, event | category | flops | bytes accessed | tf_op | source)
XLA Modules:
  0.0 57.5 jit_solution(5627598044423756782)
XLA Ops:
  0.0 0.0 copy-start.1
  0.0 1.0 %copy-done.1 = bf16[1,32,2,24,128]{4,3,2,1,0:T(8,128)(2,1)S(1)} copy-done((bf16[1,32,2,24,128]{4,3,2,1,0:T(8,128)(2,1)S(1)}, bf16[1,32,2,24,128]{4,3,2,1,0:T(8,128)(2,1)}, u32[]{:S(2)}) %copy-start.1) | copy-done | bytes 393240
  1.0 0.0 copy-start
  1.0 0.0 copy-start.2
  1.0 0.0 copy-start.3
  1.0 0.3 relay_cot.1
  1.3 0.1 collective-permute-start
  1.4 5.3 %collective-permute-start.1 = (bf16[864,128]{1,0:T(8,128)(2,1)S(1)}, bf16[864,128]{1,0:T(8,128)(2,1)S(1)}, u32[]{:S(2)}, u32[]{:S(2)}) collective-permute-start(bf16[864,128]{1,0:T(8,128)(2,1)S(1)} %get-tuple-element.20), channel_id=1, source_target_pairs={{16,32},{32,16},{48,64},{64,48},{80,96},{96,80},{112,128},{128,112... | collective-permute-start | bytes 663560 | tf_op jit(solution)/shard_map/ppermute | solution.py:388
  6.7 0.0 copy-done
  6.7 0.0 copy-done.2
  6.7 0.0 copy-done.3
  6.7 3.8 %local_terms.1 = (bf16[4,1568,256]{2,1,0:T(8,128)(2,1)S(1)}, bf16[2,2304,128]{2,1,0:T(8,128)(2,1)S(1)}, f32[2,768,128]{2,1,0:T(8,128)S(1)}, f32[2,768,128]{2,1,0...) custom-call(bf16[32,4,48,256]{3,2,1,0:T(8,128)(2,1)S(1)} %bitcast.11, ...), custom_call_target="tpu_custom_call" | custom-call | flops 5000000000 | bytes 4036608 | tf_op jit(solution)/shard_map/local_terms/pallas_call | solution.py:298
  10.5 0.0 collective-permute-done.chip_ref
  10.5 0.8 %collective-permute-done.1.far_ref = bf16[864,128]{1,0:T(8,128)(2,1)S(1)} collective-permute-done((bf16[864,128]{1,0:T(8,128)(2,1)S(1)}, bf16[864,128]{1,0:T(8,128)(2,1)S(1)}, u32[]{:S(2)}, u32[]{:S(2)}) %collective-permute-start.1) | collective-permute-done | bytes 221216 | tf_op jit(solution)/shard_map/ppermute | solution.py:388
  11.3 0.5 rim_grad.1
  11.8 5.2 %collective-permute-start.2 = (bf16[768,128]{1,0:T(8,128)(2,1)S(1)}, bf16[768,128]{1,0:T(8,128)(2,1)S(1)}, u32[]{:S(2)}, u32[]{:S(2)}) collective-permute-start(bf16[768,128]{1,0:T(8,128)(2,1)S(1)} %get-tuple-element.25.grad0_ref), channel_id=1, source_target_pairs={{16,0},{32,16},{48,32},{64,48},{80,64},{96,80},{112,96},{128,112},... | collective-permute-start | bytes 589832 | tf_op jit(solution)/shard_map/ppermute | solution.py:401
  17.0 2.9 %main_terms.1 = (f32[96,128]{1,0:T(8,128)S(1)}, f32[2,216,128]{2,1,0:T(8,128)S(1)}) custom-call(bf16[2,864,128]{2,1,0:T(8,128)(2,1)S(1)} %get-tuple-element.28.halo_ref, bf16[2,96,128]{2,1,0:T(8,128)(2,1)S(1)} %get-tuple-element.22.rim_weights, f32[2,768,128]{2,1,0:T(8,128)S(1)} %get-tuple-element.23.partial_ref, ...), custom_call_target="tpu_custom_call" | custom-call | flops 5000000000 | bytes 6995968 | tf_op jit(solution)/shard_map/main_terms/pallas_call | solution.py:298
  19.9 0.3 collective-permute-done.2.grad_next_ref
  20.1 1.3 %last_terms.1 = f32[16,2,16,128]{3,2,1,0:T(8,128)S(1)} custom-call(bf16[768,128]{1,0:T(8,128)(2,1)S(1)} %collective-permute-done.2.grad_next_ref, bf16[128,768]{1,0:T(8,128)(2,1)S(1)} %get-tuple-element.26.spread_ref, bf16[4,1568,256]{2,1,0:T(8,128)(2,1)S(1)} %get-tuple-element.27.act_t, f32[96,128]{1,0:T(8,128)S(1)} %get-tuple-element.31.first_ref, ...), custom_call_target="tpu_custom_call" | custom-call | flops 1000000000 | bytes 3874816 | tf_op jit(solution)/shard_map/last_terms/pallas_call | solution.py:298
  21.5 15.9 %all_to_all.10 = f32[32,16,128]{2,1,0:T(8,128)S(1)} all-to-all(f32[32,16,128]{2,1,0:T(8,128)S(1)} %bitcast.10), channel_id=1, replica_groups=mesh['space'=16,'deep'=8,'lane'=2] {'space','lane'}, dimensions={0} | all-to-all | bytes 524288 | tf_op jit(solution)/shard_map/all_to_all | solution.py:406
  37.4 0.7 %broadcast_in_dim.2 = f32[16,16,128]{2,1,0:T(8,128)} broadcast(f32[16,128]{1,0:T(8,128)S(1)} %reduce_sum.18), dimensions={1,2} | broadcast | bytes 139264 | tf_op jit(solution)/shard_map/broadcast_in_dim | solution.py:409
  38.1 8.8 %all-to-all-start.1 = ((f32[16,16,128]{2,1,0:T(8,128)}), f32[16,16,128]{2,1,0:T(8,128)S(1)}, u32[]{:S(2)}, u32[]{:S(2)}) async-start(f32[16,16,128]{2,1,0:T(8,128)} %broadcast_in_dim.2), calls=%async_computation.1 | async-start | bytes 262144 | tf_op jit(solution)/shard_map/all_to_all | solution.py:408
  46.9 9.9 %all-to-all-done.1 = f32[16,16,128]{2,1,0:T(8,128)S(1)} async-done(((f32[16,16,128]{2,1,0:T(8,128)}), f32[16,16,128]{2,1,0:T(8,128)S(1)}, u32[]{:S(2)}, u32[]{:S(2)}) %all-to-all-start.1) | async-done | bytes 131104 | tf_op jit(solution)/shard_map/all_to_all | solution.py:408
  56.8 0.7 %constant_dynamic-slice_fusion = f32[2,1728]{1,0:T(2,128)} fusion(f32[2,1792]{1,0:T(2,128)S(1)} %bitcast.15, s32[]{:T(128)S(6)} %select_n.11), kind=kLoop, calls=%fused_computation.2 | loop fusion | bytes 27652 | tf_op jit(solution)/shard_map/dynamic_slice | solution.py:413
  (4 shorter events, 0.1 us)
Async XLA Ops:
  0.0 1.0 %copy-start.1 = (bf16[1,32,2,24,128]{4,3,2,1,0:T(8,128)(2,1)S(1)}, bf16[1,32,2,24,128]{4,3,2,1,0:T(8,128)(2,1)}, u32[]{:S(2)}) copy-start(bf16[1,32,2,24,128]{4,3,2,1,0:T(8,128)(2,1)} %param.6) | copy-start | bytes 1179652
  1.0 5.7 %copy-start = (bf16[1,32,4,48,256]{4,3,2,1,0:T(8,128)(2,1)S(1)}, bf16[1,32,4,48,256]{4,3,2,1,0:T(8,128)(2,1)}, u32[]{:S(2)}) copy-start(bf16[1,32,4,48,256]{4,3,2,1,0:T(8,128)(2,1)} %param.4) | copy-start | bytes 9437188
  1.0 5.7 %copy-start.2 = (bf16[1,32,2,24,128]{4,3,2,1,0:T(8,128)(2,1)S(1)}, bf16[1,32,2,24,128]{4,3,2,1,0:T(8,128)(2,1)}, u32[]{:S(2)}) copy-start(bf16[1,32,2,24,128]{4,3,2,1,0:T(8,128)(2,1)} %param.5) | copy-start | bytes 1179652
  1.0 5.7 %copy-start.3 = (bf16[27,32,32]{2,1,0:T(8,128)(2,1)S(1)}, bf16[27,32,32]{2,1,0:T(8,128)(2,1)}, u32[]{:S(2)}) copy-start(bf16[27,32,32]{2,1,0:T(8,128)(2,1)} %weight_ref.1) | copy-start | bytes 165892
  1.3 9.2 %collective-permute-start = (bf16[864,128]{1,0:T(8,128)(2,1)S(1)}, bf16[864,128]{1,0:T(8,128)(2,1)S(1)}, u32[]{:S(2)}, u32[]{:S(2)}) collective-permute-start(bf16[864,128]{1,0:T(8,128)(2,1)S(1)} %get-tuple-element.19), channel_id=1, source_target_pairs={{0,16},{16,0},{32,48},{48,32},{64,80},{80,64},{96,112},{112,96},{1... | collective-permute-start | bytes 663560 | tf_op jit(solution)/shard_map/ppermute | solution.py:388
  1.4 9.9 %collective-permute-start.1 = (bf16[864,128]{1,0:T(8,128)(2,1)S(1)}, bf16[864,128]{1,0:T(8,128)(2,1)S(1)}, u32[]{:S(2)}, u32[]{:S(2)}) collective-permute-start(bf16[864,128]{1,0:T(8,128)(2,1)S(1)} %get-tuple-element.20), channel_id=1, source_target_pairs={{16,32},{32,16},{48,64},{64,48},{80,96},{96,80},{112,128},{128,112... | collective-permute-start | bytes 663560 | tf_op jit(solution)/shard_map/ppermute | solution.py:388
  11.8 8.3 %collective-permute-start.2 = (bf16[768,128]{1,0:T(8,128)(2,1)S(1)}, bf16[768,128]{1,0:T(8,128)(2,1)S(1)}, u32[]{:S(2)}, u32[]{:S(2)}) collective-permute-start(bf16[768,128]{1,0:T(8,128)(2,1)S(1)} %get-tuple-element.25.grad0_ref), channel_id=1, source_target_pairs={{16,0},{32,16},{48,32},{64,48},{80,64},{96,80},{112,96},{128,112},... | collective-permute-start | bytes 589832 | tf_op jit(solution)/shard_map/ppermute | solution.py:401
  38.1 18.7 %all-to-all-start.1 = ((f32[16,16,128]{2,1,0:T(8,128)}), f32[16,16,128]{2,1,0:T(8,128)S(1)}, u32[]{:S(2)}, u32[]{:S(2)}) async-start(f32[16,16,128]{2,1,0:T(8,128)} %broadcast_in_dim.2), calls=%async_computation.1 | async-start | bytes 262144 | tf_op jit(solution)/shard_map/all_to_all | solution.py:408

commit v4 on v3

--- a/solution.py
+++ b/solution.py
@@ -40,18 +40,27 @@
     return lax.rem(lax.axis_index("space"), 2) == 1
 
 
-def cot_kernel(cot_ref, planes_ref, chip_ref, far_ref, flat):
+def relay_kernel(cot_ref, planes_ref, chip_ref, far_ref, flat):
     odd = on_odd()
     for plane in range(QX):
         planes_ref[plane, 0:C, :] = jnp.zeros((C, QY), BF)
         planes_ref[plane, (QZ + 1) * C :, :] = jnp.zeros((2 * C, QY), BF)
-    for plane in range(QX):
         flat[plane] = cot_ref[:, plane].astype(F32).reshape(C * QZ, QY)
-        for z in range(QZ):
-            block = flat[plane, pl.ds(z, C, stride=QZ), :]
-            planes_ref[plane, (z + 1) * C : (z + 2) * C, :] = block.astype(BF)
-    chip_ref[...] = jnp.where(odd, planes_ref[0], planes_ref[1])
-    far_ref[...] = jnp.where(odd, planes_ref[1], planes_ref[0])
+    for z in range(QZ):
+        rows = slice(z * C, (z + 1) * C)
+        first, last = [flat[i, pl.ds(z, C, stride=QZ), :].astype(BF) for i in range(QX)]
+        planes_ref[0, (z + 1) * C : (z + 2) * C, :] = first
+        planes_ref[1, (z + 1) * C : (z + 2) * C, :] = last
+        chip_ref[rows, :] = jnp.where(odd, first, last)
+        far_ref[rows, :] = jnp.where(odd, last, first)
+
+
+def prev_kernel(pre_ref, planes_ref, prev_ref, flat):
+    flat[...] = pre_ref[:, 0].astype(F32).reshape(C * QZ, QY)
+    for z in range(QZ):
+        rows = slice(z * C, (z + 1) * C)
+        prev_ref[0, rows, :] = flat[pl.ds(z, C, stride=QZ), :].astype(BF)
+        prev_ref[1, rows, :] = planes_ref[1, (z + 1) * C : (z + 2) * C, :]
 
 
 def local_kernel(
@@ -70,8 +79,8 @@
             weight_t[(j * 4 + k) * C : (j * 4 + k + 1) * C, 0:T3] = wide
         weight_t[(j * 4 + 3) * C : (j * 4 + 4) * C, :] = jnp.zeros((C, 128), F32)
     flipped = [weight_t[j * 128 : (j + 1) * 128, 0:T3].T.astype(BF) for j in range(3)]
-    rim_weights[0] = flipped[0]
-    rim_weights[1] = flipped[2]
+    for j in range(3):
+        rim_weights[j] = flipped[j]
     weights = jnp.concatenate(
         [
             jnp.concatenate([flipped[1], flipped[2]], axis=1),
@@ -151,17 +160,6 @@
             rows = slice((z + h) * C, (z + h + 1) * C)
             grad = partial[rows, :] + taps_joined(terms[:, h * QY : (h + 1) * QY])
             put(rows, (grad * scale[rows, :]).astype(BF))
-
-
-def rim_kernel(chip_ref, far_ref, rim_weights, partial_ref, scale_ref, out_ref, halo_ref):
-    odd = on_odd()
-    halo_ref[0] = jnp.where(odd, chip_ref[...], far_ref[...])
-    halo_ref[1] = jnp.where(odd, far_ref[...], chip_ref[...])
-
-    def put(rows, value):
-        out_ref[rows, :] = value
-
-    pre_grads(halo_ref.at[0], rim_weights[0], partial_ref.at[0], scale_ref.at[0], put)
 
 
 def spread_plane(grad_ref, spread_ref, wide_ref):
@@ -192,17 +190,26 @@
 
 
 def main_kernel(
-    halo_ref, rim_weights, partial_ref, scale_ref, hidden_t, act_t, grad0_ref,
+    chip_ref, far_ref, planes_ref, rim_weights, partial_ref, scale_ref, hidden_t, act_t,
     spread_ref, second_in,
-    first_ref, dense_ref,
-    grad1, wide, acc, second_ref, flips,
+    first_ref, dense_ref, partial_next,
+    halo_ref, grads, wide, acc, second_ref, flips,
 ):
-    def put(rows, value):
-        grad1[rows, :] = value
-
-    pre_grads(halo_ref.at[1], rim_weights[1], partial_ref.at[1], scale_ref.at[1], put)
-    spread_plane(grad0_ref, spread_ref, wide.at[0])
-    spread_plane(grad1, spread_ref, wide.at[1])
+    odd = on_odd()
+    for x in range(QX):
+        halo_ref[x, 0:C, :] = jnp.zeros((C, QY), BF)
+        halo_ref[x, (QZ + 1) * C :, :] = jnp.zeros((2 * C, QY), BF)
+    inner = slice(C, (QZ + 1) * C)
+    halo_ref[0, inner, :] = jnp.where(odd, chip_ref[...], far_ref[...])
+    halo_ref[1, inner, :] = jnp.where(odd, far_ref[...], chip_ref[...])
+
+    for x in range(QX):
+
+        def put(rows, value, x=x):
+            grads[x, rows, :] = value
+
+        pre_grads(halo_ref.at[x], rim_weights[2 * x], partial_ref.at[x], scale_ref.at[x], put)
+        spread_plane(grads.at[x], spread_ref, wide.at[x])
 
     second_ref[0, T3 : 2 * T3, :] = second_in[T3 : 2 * T3, :]
     for x in range(QX):
@@ -244,6 +251,20 @@
             acc[...] = part
         else:
             acc[...] += part
+    weights = jnp.concatenate([rim_weights[0], rim_weights[1]], axis=1)
+    for z in range(0, QZ, 2):
+        slab = jnp.concatenate(
+            [
+                jnp.concatenate([ref[1, (z + h) * C : (z + h + 4) * C, :] for h in range(2)], axis=1)
+                for ref in (planes_ref, halo_ref)
+            ],
+            axis=0,
+        )
+        terms = jnp.dot(weights, slab, preferred_element_type=F32)
+        for h in range(2):
+            partial_next[(z + h) * C : (z + h + 1) * C, :] = taps_joined(
+                terms[:, h * QY : (h + 1) * QY]
+            )
     first_ref[...] = acc[T3 : 2 * T3, 128:256]
     turned = jnp.concatenate(
         [
@@ -260,8 +281,24 @@
             dense_ref[0, begin : begin + 8, :] = dense_row(flips, False, ab, d)
 
 
-def last_kernel(grad_next_ref, spread_ref, act_t, first_ref, dense_ref, out_ref, wide, flips, head):
-    spread_plane(grad_next_ref, spread_ref, wide)
+def last_kernel(
+    next_ref, rim_weights, partial_ref, spread_ref, act_t, first_ref, dense_ref,
+    out_ref,
+    plane, scale, grads, wide, flips, head,
+):
+    more = lax.axis_index("space") < lax.axis_size("space") - 1
+    plane[0:C, :] = jnp.zeros((C, QY), BF)
+    plane[(QZ + 1) * C :, :] = jnp.zeros((2 * C, QY), BF)
+    plane[C : (QZ + 1) * C, :] = next_ref[1]
+    pre = next_ref[0].astype(F32)
+    gate = jax.nn.sigmoid(pre)
+    scale[...] = jnp.where(more, gate * (1.0 + pre * (1.0 - gate)), 0.0)
+
+    def put(rows, value):
+        grads[rows, :] = value
+
+    pre_grads(plane, rim_weights[2], partial_ref, scale, put)
+    spread_plane(grads, spread_ref, wide)
     total = first_ref[...]
     for z0 in range(0, QZ, 4):
         acts = jnp.concatenate(
@@ -307,11 +344,11 @@
     )(*args)
 
 
-def relay_cot(cot):
-    plane = ((COT_ROWS, QY), BF)
+def relay(cot):
+    plane = ((QZ * C, QY), BF)
     return call(
-        cot_kernel,
-        "relay_cot",
+        relay_kernel,
+        "relay",
         [((QX, COT_ROWS, QY), BF), plane, plane],
         [VMEM((QX, C * QZ, QY), F32)],
         10**10,
@@ -319,6 +356,12 @@
     )
 
 
+def for_prev(pre, planes):
+    return call(
+        prev_kernel, "for_prev", [((2, QZ * C, QY), BF)], [VMEM((C * QZ, QY), F32)], 10**9, pre, planes
+    )[0]
+
+
 def local_terms(act, pre, weight, planes):
     return call(
         local_kernel,
@@ -328,7 +371,7 @@
             ((QX, QZ * T3, QY), BF),
             ((QX, QZ * C, QY), F32),
             ((QX, QZ * C, QY), F32),
-            ((2, T3, 128), BF),
+            ((3, T3, 128), BF),
             ((QY, 3 * IY), BF),
             ((TAPS, 128), F32),
         ],
@@ -339,17 +382,6 @@
         ],
         5 * 10**9,
         act, pre, weight, planes,
-    )
-
-
-def rim_grad(*args):
-    return call(
-        rim_kernel,
-        "rim_grad",
-        [((QZ * C, QY), BF), ((QX, COT_ROWS, QY), BF)],
-        [],
-        10**9,
-        *args,
     )
 
 
@@ -357,9 +389,10 @@
     return call(
         main_kernel,
         "main_terms",
-        [((T3, 128), F32), ((2, 216, 128), F32)],
-        [
-            VMEM((QZ * C, QY), BF),
+        [((T3, 128), F32), ((2, 216, 128), F32), ((QZ * C, QY), F32)],
+        [
+            VMEM((QX, COT_ROWS, QY), BF),
+            VMEM((QX, QZ * C, QY), BF),
             VMEM((QX, QZ * T3, IY), BF),
             VMEM((4 * T3, 256), F32),
             VMEM((1, TAPS, 128), F32),
@@ -375,7 +408,14 @@
         last_kernel,
         "last_terms",
         [((16, 2, 16, 128), F32)],
-        [VMEM((QZ * T3, IY), BF), VMEM((1, 128, 128), F32), VMEM((72, 128), F32)],
+        [
+            VMEM((COT_ROWS, QY), BF),
+            VMEM((QZ * C, QY), F32),
+            VMEM((QZ * C, QY), BF),
+            VMEM((QZ * T3, IY), BF),
+            VMEM((1, 128, 128), F32),
+            VMEM((72, 128), F32),
+        ],
         10**9,
         *args,
     )[0]
@@ -390,19 +430,18 @@
 
 def on_device(activations, preact, cotangent, conv_weight):
     act, pre, cot = activations[0], preact[0], cotangent[0]
-    planes, to_chip, to_far = relay_cot(cot)
+    planes, to_chip, to_far = relay(cot)
+    to_prev = for_prev(pre, planes)
     far = swapped(to_far, 1)
+    after = lax.ppermute(to_prev, "space", [(i + 1, i) for i in range(lax.axis_size("space") - 1)])
     chip = swapped(to_chip, 0)
     act_t, hidden_t, scale, partial, rim_weights, spread, second = local_terms(
         act, pre, conv_weight, planes
     )
-    grad0, halo = rim_grad(chip, far, rim_weights, partial, scale)
-    count = lax.axis_size("space")
-    grad_next = lax.ppermute(grad0, "space", [(i + 1, i) for i in range(count - 1)])
-    first, dense = main_terms(
-        halo, rim_weights, partial, scale, hidden_t, act_t, grad0, spread, second
-    )
-    terms = last_terms(grad_next, spread, act_t, first, dense)
+    first, dense, partial_next = main_terms(
+        chip, far, planes, rim_weights, partial, scale, hidden_t, act_t, spread, second
+    )
+    terms = last_terms(after, rim_weights, partial_next, spread, act_t, first, dense)
     shares = lax.all_to_all(terms.reshape(32, 16, 128), ("space", "lane"), 0, 0, tiled=True)
     share = jnp.sum(shares, axis=0)
     copies = lax.all_to_all(

time: 58.1 us -> 53.6 us (0.923)
  starting transfers between devices: 19.4 us -> 17.1 us
  blocking collectives: 15.9 us -> 14.2 us
  waiting for transfers between devices: 10.9 us -> 9.9 us
    ppermute x1, starting transfers between devices: 5.16 us -> 2.93 us  [on_device(): lax.ppermute(to_prev, 'space', [(i + 1, i) for i in range(lax.axis_size('...]
    all_to_all x1, blocking collectives: 15.9 us -> 14.2 us  [on_device(): lax.all_to_all(terms.reshape(32, 16, 128), ('space', 'lane'), 0, 0, tiled...]
    ppermute x2, waiting for transfers between devices: 0.78 us -> 0.01 us  [swapped(): return lax.ppermute(x, 'space', pairs)]
  transfers between devices with their start and end apart: 4 -> 4, of which waited for: 3 -> 1; matrix products, arithmetic and copies ran while one was open for 0% -> 0% of each run, Pallas kernels for 12% -> 14%
where the time goes in v4:
time: 53.6 us; the launch traced here: 53.1 us
  starting transfers between devices  17.1 us (32%)
  blocking collectives  14.2 us (26%)
  waiting for transfers between devices  9.9 us (18%)
  Pallas kernels  9.27 us (17%)
  local copies, waits for them, and re-layouts  2.37 us (4%)
    all_to_all x1, blocking collectives, on_device(): lax.all_to_all(terms.reshape(32, 16, 128), ('space', 'lane'), 0, 0, tiled...  14.2 us
    all_to_all x1, waiting for transfers between devices, on_device(): lax.all_to_all(jnp.broadcast_to(share[None], (16, 16, 128)), ('deep', 'la...  9.9 us
    pallas_call x5, Pallas kernels, call(): pl.pallas_call(kernel, out_shape=shapes, in_specs=[pl.BlockSpec(memory_sp...  9.27 us
    all_to_all x1, starting transfers between devices, on_device(): lax.all_to_all(jnp.broadcast_to(share[None], (16, 16, 128)), ('deep', 'la...  8.82 us
    ppermute x2, starting transfers between devices, swapped(): return lax.ppermute(x, 'space', pairs)  5.39 us
    ppermute x1, starting transfers between devices, on_device(): lax.ppermute(to_prev, 'space', [(i + 1, i) for i in range(lax.axis_size('...  2.93 us
  transfers between devices with their start and end apart: 4, of which 1 were waited for; matrix products, arithmetic and copies ran while one was open for 0% of the time, Pallas kernels for 14%

profile of v4, /device:TPU:2, one launch (start us, length us, event | category | flops | bytes accessed | tf_op | source)
XLA Modules:
  0.0 53.1 jit_solution(10334564520878679476)
XLA Ops:
  0.0 0.0 copy-start.1
  0.0 1.0 %copy-done.1 = bf16[1,32,2,24,128]{4,3,2,1,0:T(8,128)(2,1)S(1)} copy-done((bf16[1,32,2,24,128]{4,3,2,1,0:T(8,128)(2,1)S(1)}, bf16[1,32,2,24,128]{4,3,2,1,0:T(8,128)(2,1)}, u32[]{:S(2)}) %copy-start.1) | copy-done | bytes 393240
  1.0 0.0 copy-start.2
  1.0 0.2 relay.1
  1.2 0.0 copy-start
  1.2 0.0 copy-start.3
  1.2 0.1 collective-permute-start.1
  1.3 5.3 %collective-permute-start.2 = (bf16[768,128]{1,0:T(8,128)(2,1)S(1)}, bf16[768,128]{1,0:T(8,128)(2,1)S(1)}, u32[]{:S(2)}, u32[]{:S(2)}) collective-permute-start(bf16[768,128]{1,0:T(8,128)(2,1)S(1)} %get-tuple-element.21), channel_id=1, source_target_pairs={{16,32},{32,16},{48,64},{64,48},{80,96},{96,80},{112,128},{128,112... | collective-permute-start | bytes 589832 | tf_op jit(solution)/shard_map/ppermute | solution.py:428
  6.6 0.0 copy-done.2
  6.7 0.1 for_prev.1
  6.8 2.9 %collective-permute-start = (bf16[2,768,128]{2,1,0:T(8,128)(2,1)S(1)}, bf16[2,768,128]{2,1,0:T(8,128)(2,1)S(1)}, u32[]{:S(2)}, u32[]{:S(2)}) collective-permute-start(bf16[2,768,128]{2,1,0:T(8,128)(2,1)S(1)} %for_prev.1), channel_id=1, source_target_pairs={{16,0},{32,16},{48,32},{64,48},{80,64},{96,80},{112,96},{128,112},... | collective-permute-start | bytes 1179656 | tf_op jit(solution)/shard_map/ppermute | solution.py:436
  9.7 0.0 copy-done
  9.7 0.0 copy-done.3
  9.7 3.8 %local_terms.1 = (bf16[4,1568,256]{2,1,0:T(8,128)(2,1)S(1)}, bf16[2,2304,128]{2,1,0:T(8,128)(2,1)S(1)}, f32[2,768,128]{2,1,0:T(8,128)S(1)}, f32[2,768,128]{2,1,0...) custom-call(bf16[32,4,48,256]{3,2,1,0:T(8,128)(2,1)S(1)} %bitcast.11, ...), custom_call_target="tpu_custom_call" | custom-call | flops 5000000000 | bytes 4036608 | tf_op jit(solution)/shard_map/local_terms/pallas_call | solution.py:335
  13.5 0.0 collective-permute-done.1.chip_ref
  13.5 0.0 collective-permute-done.2.far_ref
  13.5 3.6 %main_terms.1 = (f32[96,128]{1,0:T(8,128)S(1)}, f32[2,216,128]{2,1,0:T(8,128)S(1)}, f32[768,128]{1,0:T(8,128)S(1)}) custom-call(bf16[768,128]{1,0:T(8,128)(2,1)S(1)} %collective-permute-done.1.chip_ref, bf16[768,128]{1,0:T(8,128)(2,1)S(1)} %collective-permute-done.2.far_ref, bf16[2,864,128]{2,1,0:T(8,128)(2,1)S(1)} %get-tuple-element.18.planes_ref, ...), custom_call_target="tpu_custom_call" | custom-call | flops 5000000000 | bytes 7217152 | tf_op jit(solution)/shard_map/main_terms/pallas_call | solution.py:335
  17.1 0.0 collective-permute-done.next_ref
  17.1 1.6 %last_terms.1 = f32[16,2,16,128]{3,2,1,0:T(8,128)S(1)} custom-call(bf16[2,768,128]{2,1,0:T(8,128)(2,1)S(1)} %collective-permute-done.next_ref, bf16[3,96,128]{2,1,0:T(8,128)(2,1)S(1)} %get-tuple-element.19.rim_weights, f32[768,128]{1,0:T(8,128)S(1)} %get-tuple-element.28.partial_ref, bf16[128,768]{1,0:T(8,128)(2,1)S(1)} %get-tuple-element.26.spread_ref, ...), custom_call_target="tpu_custom_call" | custom-call | flops 1000000000 | bytes 4538368 | tf_op jit(solution)/shard_map/last_terms/pallas_call | solution.py:335
  18.7 14.2 %all_to_all.10 = f32[32,16,128]{2,1,0:T(8,128)S(1)} all-to-all(f32[32,16,128]{2,1,0:T(8,128)S(1)} %bitcast.10), channel_id=1, replica_groups=mesh['space'=16,'deep'=8,'lane'=2] {'space','lane'}, dimensions={0} | all-to-all | bytes 524288 | tf_op jit(solution)/shard_map/all_to_all | solution.py:445
  33.0 0.7 %broadcast_in_dim.2 = f32[16,16,128]{2,1,0:T(8,128)} broadcast(f32[16,128]{1,0:T(8,128)S(1)} %reduce_sum.18), dimensions={1,2} | broadcast | bytes 139264 | tf_op jit(solution)/shard_map/broadcast_in_dim | solution.py:448
  33.6 8.8 %all-to-all-start.1 = ((f32[16,16,128]{2,1,0:T(8,128)}), f32[16,16,128]{2,1,0:T(8,128)S(1)}, u32[]{:S(2)}, u32[]{:S(2)}) async-start(f32[16,16,128]{2,1,0:T(8,128)} %broadcast_in_dim.2), calls=%async_computation.1 | async-start | bytes 262144 | tf_op jit(solution)/shard_map/all_to_all | solution.py:447
  42.5 9.9 %all-to-all-done.1 = f32[16,16,128]{2,1,0:T(8,128)S(1)} async-done(((f32[16,16,128]{2,1,0:T(8,128)}), f32[16,16,128]{2,1,0:T(8,128)S(1)}, u32[]{:S(2)}, u32[]{:S(2)}) %all-to-all-start.1) | async-done | bytes 131104 | tf_op jit(solution)/shard_map/all_to_all | solution.py:447
  52.4 0.7 %constant_dynamic-slice_fusion = f32[2,1728]{1,0:T(2,128)} fusion(f32[2,1792]{1,0:T(2,128)S(1)} %bitcast.16, s32[]{:T(128)S(6)} %select_n.11), kind=kLoop, calls=%fused_computation.2 | loop fusion | bytes 27652 | tf_op jit(solution)/shard_map/dynamic_slice | solution.py:452
  (4 shorter events, 0.1 us)
Async XLA Ops:
  0.0 1.0 %copy-start.1 = (bf16[1,32,2,24,128]{4,3,2,1,0:T(8,128)(2,1)S(1)}, bf16[1,32,2,24,128]{4,3,2,1,0:T(8,128)(2,1)}, u32[]{:S(2)}) copy-start(bf16[1,32,2,24,128]{4,3,2,1,0:T(8,128)(2,1)} %param.6) | copy-start | bytes 1179652
  1.0 5.6 %copy-start.2 = (bf16[1,32,2,24,128]{4,3,2,1,0:T(8,128)(2,1)S(1)}, bf16[1,32,2,24,128]{4,3,2,1,0:T(8,128)(2,1)}, u32[]{:S(2)}) copy-start(bf16[1,32,2,24,128]{4,3,2,1,0:T(8,128)(2,1)} %param.5) | copy-start | bytes 1179652
  1.2 8.5 %copy-start = (bf16[1,32,4,48,256]{4,3,2,1,0:T(8,128)(2,1)S(1)}, bf16[1,32,4,48,256]{4,3,2,1,0:T(8,128)(2,1)}, u32[]{:S(2)}) copy-start(bf16[1,32,4,48,256]{4,3,2,1,0:T(8,128)(2,1)} %param.4) | copy-start | bytes 9437188
  1.2 8.5 %copy-start.3 = (bf16[27,32,32]{2,1,0:T(8,128)(2,1)S(1)}, bf16[27,32,32]{2,1,0:T(8,128)(2,1)}, u32[]{:S(2)}) copy-start(bf16[27,32,32]{2,1,0:T(8,128)(2,1)} %weight_ref.1) | copy-start | bytes 165892
  1.2 12.3 %collective-permute-start.1 = (bf16[768,128]{1,0:T(8,128)(2,1)S(1)}, bf16[768,128]{1,0:T(8,128)(2,1)S(1)}, u32[]{:S(2)}, u32[]{:S(2)}) collective-permute-start(bf16[768,128]{1,0:T(8,128)(2,1)S(1)} %get-tuple-element.20), channel_id=1, source_target_pairs={{0,16},{16,0},{32,48},{48,32},{64,80},{80,64},{96,112},{112,96},{1... | collective-permute-start | bytes 589832 | tf_op jit(solution)/shard_map/ppermute | solution.py:428
  1.3 12.2 %collective-permute-start.2 = (bf16[768,128]{1,0:T(8,128)(2,1)S(1)}, bf16[768,128]{1,0:T(8,128)(2,1)S(1)}, u32[]{:S(2)}, u32[]{:S(2)}) collective-permute-start(bf16[768,128]{1,0:T(8,128)(2,1)S(1)} %get-tuple-element.21), channel_id=1, source_target_pairs={{16,32},{32,16},{48,64},{64,48},{80,96},{96,80},{112,128},{128,112... | collective-permute-start | bytes 589832 | tf_op jit(solution)/shard_map/ppermute | solution.py:428
  6.8 10.3 %collective-permute-start = (bf16[2,768,128]{2,1,0:T(8,128)(2,1)S(1)}, bf16[2,768,128]{2,1,0:T(8,128)(2,1)S(1)}, u32[]{:S(2)}, u32[]{:S(2)}) collective-permute-start(bf16[2,768,128]{2,1,0:T(8,128)(2,1)S(1)} %for_prev.1), channel_id=1, source_target_pairs={{16,0},{32,16},{48,32},{64,48},{80,64},{96,80},{112,96},{128,112},... | collective-permute-start | bytes 1179656 | tf_op jit(solution)/shard_map/ppermute | solution.py:436
  33.6 18.7 %all-to-all-start.1 = ((f32[16,16,128]{2,1,0:T(8,128)}), f32[16,16,128]{2,1,0:T(8,128)S(1)}, u32[]{:S(2)}, u32[]{:S(2)}) async-start(f32[16,16,128]{2,1,0:T(8,128)} %broadcast_in_dim.2), calls=%async_computation.1 | async-start | bytes 262144 | tf_op jit(solution)/shard_map/all_to_all | solution.py:447

commit v5 on v4

--- a/solution.py
+++ b/solution.py
@@ -28,6 +28,21 @@
     return jnp.where(lanes == (0 if by == 1 else QY - 1), 0.0, pltpu.roll(x, by % QY, 1))
 
 
+def by_depth(block):
+    channels, depth, last = block.shape
+    return jnp.transpose(block, (1, 0, 2)).reshape(depth * channels, last)
+
+
+def depth_pair(refs, z):
+    return jnp.concatenate(
+        [
+            jnp.concatenate([ref[(z + h) * C : (z + h + 4) * C, :] for h in range(2)], axis=1)
+            for ref in refs
+        ],
+        axis=0,
+    )
+
+
 def taps_joined(part):
     return part[C : 2 * C] + lane_shift(part[0:C], -1) + lane_shift(part[2 * C : T3], 1)
 
@@ -40,33 +55,43 @@
     return lax.rem(lax.axis_index("space"), 2) == 1
 
 
-def relay_kernel(cot_ref, planes_ref, chip_ref, far_ref, flat):
+def relay_kernel(cot_ref, planes_ref, chip_ref, far_ref):
     odd = on_odd()
     for plane in range(QX):
         planes_ref[plane, 0:C, :] = jnp.zeros((C, QY), BF)
         planes_ref[plane, (QZ + 1) * C :, :] = jnp.zeros((2 * C, QY), BF)
-        flat[plane] = cot_ref[:, plane].astype(F32).reshape(C * QZ, QY)
-    for z in range(QZ):
-        rows = slice(z * C, (z + 1) * C)
-        first, last = [flat[i, pl.ds(z, C, stride=QZ), :].astype(BF) for i in range(QX)]
-        planes_ref[0, (z + 1) * C : (z + 2) * C, :] = first
-        planes_ref[1, (z + 1) * C : (z + 2) * C, :] = last
-        chip_ref[rows, :] = jnp.where(odd, first, last)
-        far_ref[rows, :] = jnp.where(odd, last, first)
-
-
-def prev_kernel(pre_ref, planes_ref, prev_ref, flat):
-    flat[...] = pre_ref[:, 0].astype(F32).reshape(C * QZ, QY)
-    for z in range(QZ):
-        rows = slice(z * C, (z + 1) * C)
-        prev_ref[0, rows, :] = flat[pl.ds(z, C, stride=QZ), :].astype(BF)
-        prev_ref[1, rows, :] = planes_ref[1, (z + 1) * C : (z + 2) * C, :]
+    first, last = [by_depth(cot_ref[:, plane]) for plane in range(QX)]
+    planes_ref[0, C : (QZ + 1) * C, :] = first
+    planes_ref[1, C : (QZ + 1) * C, :] = last
+    chip_ref[...] = jnp.where(odd, first, last)
+    far_ref[...] = jnp.where(odd, last, first)
+
+
+def prev_kernel(pre_ref, planes_ref, prev_ref):
+    prev_ref[0] = by_depth(pre_ref[:, 0])
+    prev_ref[1] = planes_ref[1, C : (QZ + 1) * C, :]
+
+
+def hidden_rows(hidden_t, z0):
+    return jnp.concatenate(
+        [
+            jnp.concatenate(
+                [four_blocks(hidden_t[x, z * T3 : (z + 1) * T3, :]) for x in range(QX)], axis=0
+            )
+            for z in range(z0, z0 + 8)
+        ],
+        axis=1,
+    )
+
+
+def weight_rows(blocks):
+    return jnp.concatenate([jnp.concatenate(row, axis=1) for row in blocks], axis=0)
 
 
 def local_kernel(
     act_ref, pre_ref, weight_ref, planes_ref,
     act_t, hidden_t, scale_t, partial_t, rim_weights, spread_ref, second_ref,
-    flat_act, flat_pre, weight_t,
+    weight_t,
 ):
     row = lax.broadcasted_iota(jnp.int32, (QY, 3 * IY), 0)
     col = lax.broadcasted_iota(jnp.int32, (QY, 3 * IY), 1)
@@ -79,20 +104,14 @@
             weight_t[(j * 4 + k) * C : (j * 4 + k + 1) * C, 0:T3] = wide
         weight_t[(j * 4 + 3) * C : (j * 4 + 4) * C, :] = jnp.zeros((C, 128), F32)
     flipped = [weight_t[j * 128 : (j + 1) * 128, 0:T3].T.astype(BF) for j in range(3)]
-    for j in range(3):
-        rim_weights[j] = flipped[j]
-    weights = jnp.concatenate(
-        [
-            jnp.concatenate([flipped[1], flipped[2]], axis=1),
-            jnp.concatenate([flipped[0], flipped[1]], axis=1),
-        ],
-        axis=0,
-    )
+    none = jnp.zeros((T3, 128), BF)
+    weights = weight_rows(((flipped[1], flipped[2]), (flipped[0], flipped[1]), (none, flipped[0])))
+    rim_weights[...] = weight_rows(((flipped[0], none), (none, flipped[2]), (none, flipped[1])))
 
     for plane in range(QX):
-        flat_pre[plane] = pre_ref[:, plane].astype(F32).reshape(C * QZ, QY)
+        rows = by_depth(pre_ref[:, plane]).astype(F32)
         for z in range(QZ):
-            pre = flat_pre[plane, pl.ds(z, C, stride=QZ), :]
+            pre = rows[z * C : (z + 1) * C]
             gate = jax.nn.sigmoid(pre)
             hidden = (pre * gate).astype(BF).astype(F32)
             hidden_t[plane, z * T3 : (z + 1) * T3, :] = jnp.concatenate(
@@ -102,26 +121,12 @@
 
     for plane in range(IX):
         act_t[plane, 0:C, :] = jnp.zeros((C, IY), BF)
-        flat = act_ref[:, plane].astype(F32).reshape(C * IZ, IY)
-        for side in range(2):
-            flat_act[plane % 2, side] = flat[:, side * 128 : (side + 1) * 128]
-        for z in range(IZ):
-            for side in range(2):
-                tile = flat_act[plane % 2, side, pl.ds(z, C, stride=IZ), :].astype(BF)
-                act_t[plane, (z + 1) * C : (z + 2) * C, side * 128 : (side + 1) * 128] = tile
+        act_t[plane, C:, :] = by_depth(act_ref[:, plane])
 
     for z in range(0, QZ, 2):
-        slab = jnp.concatenate(
-            [
-                jnp.concatenate(
-                    [planes_ref[x, (z + h) * C : (z + h + 4) * C, :] for h in range(2)], axis=1
-                )
-                for x in range(QX)
-            ],
-            axis=0,
-        )
+        slab = depth_pair([planes_ref.at[x] for x in range(QX)], z)
         terms = jnp.dot(weights, slab, preferred_element_type=F32)
-        for x in range(QX):
+        for x in range(QX + 1):
             for h in range(2):
                 part = terms[x * T3 : (x + 1) * T3, h * QY : (h + 1) * QY]
                 partial_t[x, (z + h) * C : (z + h + 1) * C, :] = taps_joined(part)
@@ -137,29 +142,10 @@
             ],
             axis=0,
         )
-        hid = jnp.concatenate(
-            [
-                jnp.concatenate(
-                    [four_blocks(hidden_t[x, z * T3 : (z + 1) * T3, :]) for x in range(QX)], axis=0
-                )
-                for z in range(z0, z0 + 8)
-            ],
-            axis=1,
-        )
-        total = total + nt_dot(slab, hid)
+        total = total + nt_dot(slab, hidden_rows(hidden_t, z0))
     second_ref[0:T3, :] = total[0:T3, 128:256]
     second_ref[T3 : 2 * T3, :] = total[0:T3, 0:128] + total[T3:, 128:256]
     second_ref[2 * T3 :, :] = total[T3:, 0:128]
-
-
-def pre_grads(cot_ref, weights, partial, scale, put):
-    for z in range(0, QZ, 2):
-        slab = jnp.concatenate([cot_ref[(z + h) * C : (z + h + 4) * C, :] for h in range(2)], axis=1)
-        terms = jnp.dot(weights, slab, preferred_element_type=F32)
-        for h in range(2):
-            rows = slice((z + h) * C, (z + h + 1) * C)
-            grad = partial[rows, :] + taps_joined(terms[:, h * QY : (h + 1) * QY])
-            put(rows, (grad * scale[rows, :]).astype(BF))
 
 
 def spread_plane(grad_ref, spread_ref, wide_ref):
@@ -190,7 +176,7 @@
 
 
 def main_kernel(
-    chip_ref, far_ref, planes_ref, rim_weights, partial_ref, scale_ref, hidden_t, act_t,
+    far_ref, chip_ref, rim_weights, partial_ref, scale_ref, hidden_t, act_t,
     spread_ref, second_in,
     first_ref, dense_ref, partial_next,
     halo_ref, grads, wide, acc, second_ref, flips,
@@ -203,25 +189,35 @@
     halo_ref[0, inner, :] = jnp.where(odd, chip_ref[...], far_ref[...])
     halo_ref[1, inner, :] = jnp.where(odd, far_ref[...], chip_ref[...])
 
+    for z in range(0, QZ, 2):
+        slab = depth_pair([halo_ref.at[x] for x in range(QX)], z)
+        terms = jnp.dot(rim_weights[...], slab, preferred_element_type=F32)
+        for h in range(2):
+            rows = slice((z + h) * C, (z + h + 1) * C)
+            parts = [
+                partial_ref[x, rows, :]
+                + taps_joined(terms[x * T3 : (x + 1) * T3, h * QY : (h + 1) * QY])
+                for x in range(QX + 1)
+            ]
+            for x in range(QX):
+                grads[x, rows, :] = (parts[x] * scale_ref[x, rows, :]).astype(BF)
+            partial_next[rows, :] = parts[QX]
     for x in range(QX):
-
-        def put(rows, value, x=x):
-            grads[x, rows, :] = value
-
-        pre_grads(halo_ref.at[x], rim_weights[2 * x], partial_ref.at[x], scale_ref.at[x], put)
         spread_plane(grads.at[x], spread_ref, wide.at[x])
 
+    total = jnp.zeros((2 * T3, 256), F32)
+    for z0 in range(0, QZ, 8):
+        slab = jnp.concatenate(
+            [
+                jnp.concatenate([halo_ref[x, z * C : (z + 3) * C, :] for z in range(z0, z0 + 8)], axis=1)
+                for x in range(QX)
+            ],
+            axis=0,
+        )
+        total = total + nt_dot(slab, hidden_rows(hidden_t, z0))
+    second_ref[0, 0:T3, :] = second_in[0:T3, :] + total[0:T3, 0:128]
     second_ref[0, T3 : 2 * T3, :] = second_in[T3 : 2 * T3, :]
-    for x in range(QX):
-        rows = slice(2 * x * T3, (2 * x + 1) * T3)
-        total = second_in[rows, :]
-        for z0 in range(0, QZ, 8):
-            slab = jnp.concatenate([halo_ref[x, z * C : (z + 3) * C, :] for z in range(z0, z0 + 8)], axis=1)
-            hid = jnp.concatenate(
-                [four_blocks(hidden_t[x, z * T3 : (z + 1) * T3, :]) for z in range(z0, z0 + 8)], axis=1
-            )
-            total = total + nt_dot(slab, hid)
-        second_ref[0, rows, :] = total
+    second_ref[0, 2 * T3 :, :] = second_in[2 * T3 :, :] + total[T3:, 128:256]
     for ab in range(9):
         for d in range(3):
             begin = (ab * 3 + d) * 8
@@ -251,20 +247,6 @@
             acc[...] = part
         else:
             acc[...] += part
-    weights = jnp.concatenate([rim_weights[0], rim_weights[1]], axis=1)
-    for z in range(0, QZ, 2):
-        slab = jnp.concatenate(
-            [
-                jnp.concatenate([ref[1, (z + h) * C : (z + h + 4) * C, :] for h in range(2)], axis=1)
-                for ref in (planes_ref, halo_ref)
-            ],
-            axis=0,
-        )
-        terms = jnp.dot(weights, slab, preferred_element_type=F32)
-        for h in range(2):
-            partial_next[(z + h) * C : (z + h + 1) * C, :] = taps_joined(
-                terms[:, h * QY : (h + 1) * QY]
-            )
     first_ref[...] = acc[T3 : 2 * T3, 128:256]
     turned = jnp.concatenate(
         [
@@ -294,10 +276,13 @@
     gate = jax.nn.sigmoid(pre)
     scale[...] = jnp.where(more, gate * (1.0 + pre * (1.0 - gate)), 0.0)
 
-    def put(rows, value):
-        grads[rows, :] = value
-
-    pre_grads(plane, rim_weights[2], partial_ref, scale, put)
+    weights = rim_weights[T3 : 2 * T3, 128:256]
+    for z in range(0, QZ, 2):
+        terms = jnp.dot(weights, depth_pair([plane], z), preferred_element_type=F32)
+        for h in range(2):
+            rows = slice((z + h) * C, (z + h + 1) * C)
+            grad = partial_ref[rows, :] + taps_joined(terms[:, h * QY : (h + 1) * QY])
+            grads[rows, :] = (grad * scale[rows, :]).astype(BF)
     spread_plane(grads, spread_ref, wide)
     total = first_ref[...]
     for z0 in range(0, QZ, 4):
@@ -324,6 +309,31 @@
             if known < 14:
                 out_ref[s, which, known:14, :] = dense_ref[which, begin + known : begin + 14, :]
             out_ref[s, which, 14:16, :] = jnp.zeros((2, 128), F32)
+
+
+def share_kernel(shares_ref, copies_ref):
+    total = shares_ref[0].astype(F32)
+    for i in range(1, 32):
+        total = total + shares_ref[i].astype(F32)
+    for i in range(16):
+        copies_ref[i] = total.astype(copies_ref.dtype)
+
+
+def total_kernel(copies_ref, out_ref):
+    odd = on_odd()
+    lane = lax.broadcasted_iota(jnp.int32, (16, 128), 1)
+    rows = []
+    for which in range(2):
+        total = copies_ref[which].astype(F32)
+        for deep in range(1, 8):
+            total = total + copies_ref[2 * deep + which].astype(F32)
+        turned = pltpu.roll(total, 64, 1)
+        after = jnp.concatenate([turned[1:], turned[0:1]], axis=0)
+        rows.append(jnp.where(odd, jnp.where(lane < 64, turned, after), total))
+    for k in range(14):
+        width = min(128, 1728 - 128 * k)
+        both = jnp.concatenate([rows[0][k : k + 1], rows[1][k : k + 1]], axis=0)
+        out_ref[:, 128 * k : 128 * k + width] = both[:, 0:width]
 
 
 VMEM = pltpu.VMEM
@@ -350,7 +360,7 @@
         relay_kernel,
         "relay",
         [((QX, COT_ROWS, QY), BF), plane, plane],
-        [VMEM((QX, C * QZ, QY), F32)],
+        [],
         10**10,
         cot,
     )
@@ -358,7 +368,7 @@
 
 def for_prev(pre, planes):
     return call(
-        prev_kernel, "for_prev", [((2, QZ * C, QY), BF)], [VMEM((C * QZ, QY), F32)], 10**9, pre, planes
+        prev_kernel, "for_prev", [((2, QZ * C, QY), BF)], [], 10**9, pre, planes
     )[0]
 
 
@@ -370,14 +380,12 @@
             ((IX, ACT_ROWS, IY), BF),
             ((QX, QZ * T3, QY), BF),
             ((QX, QZ * C, QY), F32),
-            ((QX, QZ * C, QY), F32),
-            ((3, T3, 128), BF),
+            ((QX + 1, QZ * C, QY), F32),
+            ((3 * T3, 256), BF),
             ((QY, 3 * IY), BF),
             ((TAPS, 128), F32),
         ],
         [
-            VMEM((2, 2, C * IZ, 128), F32),
-            VMEM((QX, C * QZ, QY), F32),
             VMEM((3 * 128, 128), F32),
         ],
         5 * 10**9,
@@ -419,6 +427,14 @@
         10**9,
         *args,
     )[0]
+
+
+def share_copies(shares):
+    return call(share_kernel, "share_copies", [((16, 16, 128), F32)], [], 10**6, shares)[0]
+
+
+def total_rows(copies):
+    return call(total_kernel, "total_rows", [((2, 1728), F32)], [], 10**6, copies)[0]
 
 
 def swapped(x, begin):
@@ -439,17 +455,12 @@
         act, pre, conv_weight, planes
     )
     first, dense, partial_next = main_terms(
-        chip, far, planes, rim_weights, partial, scale, hidden_t, act_t, spread, second
+        far, chip, rim_weights, partial, scale, hidden_t, act_t, spread, second
     )
     terms = last_terms(after, rim_weights, partial_next, spread, act_t, first, dense)
     shares = lax.all_to_all(terms.reshape(32, 16, 128), ("space", "lane"), 0, 0, tiled=True)
-    share = jnp.sum(shares, axis=0)
-    copies = lax.all_to_all(
-        jnp.broadcast_to(share[None], (16, 16, 128)), ("deep", "lane"), 0, 0, tiled=True
-    )
-    total = jnp.sum(copies.reshape(8, 2, 16, 128), axis=0)[:, :14].reshape(2, 14 * 128)
-    odd = lax.axis_index("space") % 2
-    return lax.dynamic_slice(total, (0, 64 * odd), (2, 1728))
+    copies = lax.all_to_all(share_copies(shares), ("deep", "lane"), 0, 0, tiled=True)
+    return total_rows(copies)
 
 
 def solution(mesh):

time: 53.6 us -> 52.6 us (0.981)
  blocking collectives: 14.2 us -> 34.3 us
  waiting for transfers between devices: 9.9 us -> 0.01 us
  starting transfers between devices: 17.1 us -> 8.34 us
  local copies, waits for them, and re-layouts: 2.37 us -> 1.01 us
  Pallas kernels: 9.27 us -> 8.39 us
    all_to_all x0 -> x1, blocking collectives: none -> 18.5 us  [on_device(): lax.all_to_all(share_copies(shares), ('deep', 'lane'), 0, 0, tiled=True)]
    all_to_all x1 -> x0, waiting for transfers between devices: 9.9 us -> none  [on_device(): lax.all_to_all(jnp.broadcast_to(share[None], (16, 16, 128)), ('deep', 'la...]
    all_to_all x1 -> x0, starting transfers between devices: 8.82 us -> none  [on_device(): lax.all_to_all(jnp.broadcast_to(share[None], (16, 16, 128)), ('deep', 'la...]
    all_to_all x1, blocking collectives: 14.2 us -> 15.7 us  [on_device(): lax.all_to_all(terms.reshape(32, 16, 128), ('space', 'lane'), 0, 0, tiled...]
    pallas_call x5 -> x7, Pallas kernels: 9.27 us -> 8.39 us  [call(): pl.pallas_call(kernel, out_shape=shapes, in_specs=[pl.BlockSpec(memory_sp...]
    dynamic_slice x1 -> x0, local copies, waits for them, and re-layouts: 0.69 us -> none  [on_device(): return lax.dynamic_slice(total, (0, 64 * odd), (2, 1728))]
    broadcast_in_dim x1 -> x0, local copies, waits for them, and re-layouts: 0.66 us -> none  [on_device(): jnp.broadcast_to(share[None], (16, 16, 128))]
  transfers between devices with their start and end apart: 4 -> 3, of which waited for: 1 -> 0; matrix products, arithmetic and copies ran while one was open for 0% -> 0% of each run, Pallas kernels for 14% -> 11%
where the time goes in v5:
time: 52.6 us; the launch traced here: 52.1 us
  blocking collectives  34.3 us (65%)
  Pallas kernels  8.39 us (16%)
  starting transfers between devices  8.34 us (16%)
  local copies, waits for them, and re-layouts  1.01 us (2%)
    all_to_all x1, blocking collectives, on_device(): lax.all_to_all(share_copies(shares), ('deep', 'lane'), 0, 0, tiled=True)  18.5 us
    all_to_all x1, blocking collectives, on_device(): lax.all_to_all(terms.reshape(32, 16, 128), ('space', 'lane'), 0, 0, tiled...  15.7 us
    pallas_call x7, Pallas kernels, call(): pl.pallas_call(kernel, out_shape=shapes, in_specs=[pl.BlockSpec(memory_sp...  8.39 us
    ppermute x2, starting transfers between devices, swapped(): return lax.ppermute(x, 'space', pairs)  5.57 us
    ppermute x1, starting transfers between devices, on_device(): lax.ppermute(to_prev, 'space', [(i + 1, i) for i in range(lax.axis_size('...  2.77 us
  transfers between devices with their start and end apart: 3, of which 0 were waited for; matrix products, arithmetic and copies ran while one was open for 0% of the time, Pallas kernels for 11%

profile of v5, /device:TPU:2, one launch (start us, length us, event | category | flops | bytes accessed | tf_op | source)
XLA Modules:
  0.0 52.1 jit_solution(726697500298573428)
XLA Ops:
  0.0 0.0 copy-start.1
  0.0 1.0 %copy-done.1 = bf16[1,32,2,24,128]{4,3,2,1,0:T(8,128)(2,1)S(1)} copy-done((bf16[1,32,2,24,128]{4,3,2,1,0:T(8,128)(2,1)S(1)}, bf16[1,32,2,24,128]{4,3,2,1,0:T(8,128)(2,1)}, u32[]{:S(2)}) %copy-start.1) | copy-done | bytes 393240
  1.0 0.0 copy-start.2
  1.0 0.2 relay.1
  1.2 0.0 copy-start
  1.2 0.0 copy-start.3
  1.2 4.8 %collective-permute-start.1 = (bf16[768,128]{1,0:T(8,128)(2,1)S(1)}, bf16[768,128]{1,0:T(8,128)(2,1)S(1)}, u32[]{:S(2)}, u32[]{:S(2)}) collective-permute-start(bf16[768,128]{1,0:T(8,128)(2,1)S(1)} %get-tuple-element.20), channel_id=1, source_target_pairs={{16,32},{32,16},{48,64},{64,48},{80,96},{96,80},{112,128},{128,112... | collective-permute-start | bytes 589832 | tf_op jit(solution)/shard_map/ppermute | solution.py:444
  6.0 0.8 %collective-permute-start.2 = (bf16[768,128]{1,0:T(8,128)(2,1)S(1)}, bf16[768,128]{1,0:T(8,128)(2,1)S(1)}, u32[]{:S(2)}, u32[]{:S(2)}) collective-permute-start(bf16[768,128]{1,0:T(8,128)(2,1)S(1)} %get-tuple-element.21), channel_id=1, source_target_pairs={{0,16},{16,0},{32,48},{48,32},{64,80},{80,64},{96,112},{112,96},{1... | collective-permute-start | bytes 589832 | tf_op jit(solution)/shard_map/ppermute | solution.py:444
  6.8 0.0 copy-done.2
  6.8 0.1 for_prev.1
  6.9 2.8 %collective-permute-start = (bf16[2,768,128]{2,1,0:T(8,128)(2,1)S(1)}, bf16[2,768,128]{2,1,0:T(8,128)(2,1)S(1)}, u32[]{:S(2)}, u32[]{:S(2)}) collective-permute-start(bf16[2,768,128]{2,1,0:T(8,128)(2,1)S(1)} %for_prev.1), channel_id=1, source_target_pairs={{16,0},{32,16},{48,32},{64,48},{80,64},{96,80},{112,96},{128,112},... | collective-permute-start | bytes 1179656 | tf_op jit(solution)/shard_map/ppermute | solution.py:452
  9.7 0.0 copy-done
  9.7 0.0 copy-done.3
  9.7 2.5 %local_terms.1 = (bf16[4,1568,256]{2,1,0:T(8,128)(2,1)S(1)}, bf16[2,2304,128]{2,1,0:T(8,128)(2,1)S(1)}, f32[2,768,128]{2,1,0:T(8,128)S(1)}, f32[3,768,128]{2,1,0...) custom-call(bf16[32,4,48,256]{3,2,1,0:T(8,128)(2,1)S(1)} %bitcast.5, ...), custom_call_target="tpu_custom_call" | custom-call | flops 5000000000 | bytes 4036608 | tf_op jit(solution)/shard_map/local_terms/pallas_call | solution.py:345
  12.2 0.0 collective-permute-done.1.far_ref
  12.2 0.0 collective-permute-done.2.chip_ref
  12.2 3.3 %main_terms.1 = (f32[96,128]{1,0:T(8,128)S(1)}, f32[2,216,128]{2,1,0:T(8,128)S(1)}, f32[768,128]{1,0:T(8,128)S(1)}) custom-call(bf16[768,128]{1,0:T(8,128)(2,1)S(1)} %collective-permute-done.1.far_ref, bf16[768,128]{1,0:T(8,128)(2,1)S(1)} %collective-permute-done.2.chip_ref, bf16[288,256]{1,0:T(8,128)(2,1)S(1)} %get-tuple-element.19.rim_weights, ...), custom_call_target="tpu_custom_call" | custom-call | flops 5000000000 | bytes 7241728 | tf_op jit(solution)/shard_map/main_terms/pallas_call | solution.py:345
  15.5 0.0 collective-permute-done.next_ref
  15.5 1.6 %last_terms.1 = f32[16,2,16,128]{3,2,1,0:T(8,128)S(1)} custom-call(bf16[2,768,128]{2,1,0:T(8,128)(2,1)S(1)} %collective-permute-done.next_ref, bf16[288,256]{1,0:T(8,128)(2,1)S(1)} %get-tuple-element.19.rim_weights, f32[768,128]{1,0:T(8,128)S(1)} %get-tuple-element.28.partial_ref, bf16[128,768]{1,0:T(8,128)(2,1)S(1)} %get-tuple-element.26.spread_ref, ...), custom_call_target="tpu_custom_call" | custom-call | flops 1000000000 | bytes 4612096 | tf_op jit(solution)/shard_map/last_terms/pallas_call | solution.py:345
  17.1 15.7 %all_to_all.10.shares_ref = f32[32,16,128]{2,1,0:T(8,128)S(1)} all-to-all(f32[32,16,128]{2,1,0:T(8,128)S(1)} %bitcast.4), channel_id=1, replica_groups=mesh['space'=16,'deep'=8,'lane'=2] {'space','lane'}, dimensions={0} | all-to-all | bytes 524288 | tf_op jit(solution)/shard_map/all_to_all | solution.py:461
  32.9 18.5 %all_to_all.11.copies_ref = f32[16,16,128]{2,1,0:T(8,128)S(1)} all-to-all(f32[16,16,128]{2,1,0:T(8,128)S(1)} %share_copies.1), channel_id=1, replica_groups=mesh['space'=16,'deep'=8,'lane'=2] {'deep','lane'}, dimensions={0} | all-to-all | bytes 262144 | tf_op jit(solution)/shard_map/all_to_all | solution.py:462
  51.4 0.7 %total_rows.1 = f32[2,1728]{1,0:T(2,128)} custom-call(f32[16,16,128]{2,1,0:T(8,128)S(1)} %all_to_all.11.copies_ref), custom_call_target="tpu_custom_call" | custom-call | flops 1000000 | bytes 131072 | tf_op jit(solution)/shard_map/total_rows/pallas_call | solution.py:345
  (1 shorter events, 0.0 us)
Async XLA Ops:
  0.0 1.0 %copy-start.1 = (bf16[1,32,2,24,128]{4,3,2,1,0:T(8,128)(2,1)S(1)}, bf16[1,32,2,24,128]{4,3,2,1,0:T(8,128)(2,1)}, u32[]{:S(2)}) copy-start(bf16[1,32,2,24,128]{4,3,2,1,0:T(8,128)(2,1)} %param.6) | copy-start | bytes 1179652
  1.0 5.8 %copy-start.2 = (bf16[1,32,2,24,128]{4,3,2,1,0:T(8,128)(2,1)S(1)}, bf16[1,32,2,24,128]{4,3,2,1,0:T(8,128)(2,1)}, u32[]{:S(2)}) copy-start(bf16[1,32,2,24,128]{4,3,2,1,0:T(8,128)(2,1)} %param.5) | copy-start | bytes 1179652
  1.2 8.5 %copy-start = (bf16[1,32,4,48,256]{4,3,2,1,0:T(8,128)(2,1)S(1)}, bf16[1,32,4,48,256]{4,3,2,1,0:T(8,128)(2,1)}, u32[]{:S(2)}) copy-start(bf16[1,32,4,48,256]{4,3,2,1,0:T(8,128)(2,1)} %param.4) | copy-start | bytes 9437188
  1.2 8.5 %copy-start.3 = (bf16[27,32,32]{2,1,0:T(8,128)(2,1)S(1)}, bf16[27,32,32]{2,1,0:T(8,128)(2,1)}, u32[]{:S(2)}) copy-start(bf16[27,32,32]{2,1,0:T(8,128)(2,1)} %weight_ref.1) | copy-start | bytes 165892
  1.2 10.9 %collective-permute-start.1 = (bf16[768,128]{1,0:T(8,128)(2,1)S(1)}, bf16[768,128]{1,0:T(8,128)(2,1)S(1)}, u32[]{:S(2)}, u32[]{:S(2)}) collective-permute-start(bf16[768,128]{1,0:T(8,128)(2,1)S(1)} %get-tuple-element.20), channel_id=1, source_target_pairs={{16,32},{32,16},{48,64},{64,48},{80,96},{96,80},{112,128},{128,112... | collective-permute-start | bytes 589832 | tf_op jit(solution)/shard_map/ppermute | solution.py:444
  6.0 6.2 %collective-permute-start.2 = (bf16[768,128]{1,0:T(8,128)(2,1)S(1)}, bf16[768,128]{1,0:T(8,128)(2,1)S(1)}, u32[]{:S(2)}, u32[]{:S(2)}) collective-permute-start(bf16[768,128]{1,0:T(8,128)(2,1)S(1)} %get-tuple-element.21), channel_id=1, source_target_pairs={{0,16},{16,0},{32,48},{48,32},{64,80},{80,64},{96,112},{112,96},{1... | collective-permute-start | bytes 589832 | tf_op jit(solution)/shard_map/ppermute | solution.py:444
  6.9 8.6 %collective-permute-start = (bf16[2,768,128]{2,1,0:T(8,128)(2,1)S(1)}, bf16[2,768,128]{2,1,0:T(8,128)(2,1)S(1)}, u32[]{:S(2)}, u32[]{:S(2)}) collective-permute-start(bf16[2,768,128]{2,1,0:T(8,128)(2,1)S(1)} %for_prev.1), channel_id=1, source_target_pairs={{16,0},{32,16},{48,32},{64,48},{80,64},{96,80},{112,96},{128,112},... | collective-permute-start | bytes 1179656 | tf_op jit(solution)/shard_map/ppermute | solution.py:452

commit v6 on v5

--- a/solution.py
+++ b/solution.py
@@ -304,11 +304,11 @@
         begin = (27 * s) // 2
         for which in range(2):
             known = min(max(72 - begin, 0), 14) if which == 0 else 0
-            if known:
-                out_ref[s, which, 0:known, :] = head[begin : begin + known, :]
+            begins = [head[begin : begin + known, :]] if known else []
             if known < 14:
-                out_ref[s, which, known:14, :] = dense_ref[which, begin + known : begin + 14, :]
-            out_ref[s, which, 14:16, :] = jnp.zeros((2, 128), F32)
+                begins.append(dense_ref[which, begin + known : begin + 14, :])
+            begins.append(jnp.zeros((2, 128), F32))
+            out_ref[s, which] = jnp.concatenate(begins, axis=0).astype(BF)
 
 
 def share_kernel(shares_ref, copies_ref):
@@ -415,7 +415,7 @@
     return call(
         last_kernel,
         "last_terms",
-        [((16, 2, 16, 128), F32)],
+        [((16, 2, 16, 128), BF)],
         [
             VMEM((COT_ROWS, QY), BF),
             VMEM((QZ * C, QY), F32),
@@ -430,7 +430,7 @@
 
 
 def share_copies(shares):
-    return call(share_kernel, "share_copies", [((16, 16, 128), F32)], [], 10**6, shares)[0]
+    return call(share_kernel, "share_copies", [((16, 16, 128), BF)], [], 10**6, shares)[0]
 
 
 def total_rows(copies):

time: 52.6 us -> 51.1 us (0.971)
  blocking collectives: 34.3 us -> 32.5 us
    all_to_all x1, blocking collectives: 18.5 us -> 17.4 us  [on_device(): lax.all_to_all(share_copies(shares), ('deep', 'lane'), 0, 0, tiled=True)]
    all_to_all x1, blocking collectives: 15.7 us -> 15.1 us  [on_device(): lax.all_to_all(terms.reshape(32, 16, 128), ('space', 'lane'), 0, 0, tiled...]
  transfers between devices with their start and end apart: 3 -> 3, of which waited for: 0 -> 0; matrix products, arithmetic and copies ran while one was open for 0% -> 0% of each run, Pallas kernels for 11% -> 12%
where the time goes in v6:
time: 51.1 us; the launch traced here: 50.3 us
  blocking collectives  32.5 us (64%)
  Pallas kernels  8.4 us (16%)
  starting transfers between devices  8.34 us (16%)
  local copies, waits for them, and re-layouts  1.01 us (2%)
    all_to_all x1, blocking collectives, on_device(): lax.all_to_all(share_copies(shares), ('deep', 'lane'), 0, 0, tiled=True)  17.4 us
    all_to_all x1, blocking collectives, on_device(): lax.all_to_all(terms.reshape(32, 16, 128), ('space', 'lane'), 0, 0, tiled...  15.1 us
    pallas_call x7, Pallas kernels, call(): pl.pallas_call(kernel, out_shape=shapes, in_specs=[pl.BlockSpec(memory_sp...  8.4 us
    ppermute x2, starting transfers between devices, swapped(): return lax.ppermute(x, 'space', pairs)  5.57 us
    ppermute x1, starting transfers between devices, on_device(): lax.ppermute(to_prev, 'space', [(i + 1, i) for i in range(lax.axis_size('...  2.77 us
  transfers between devices with their start and end apart: 3, of which 0 were waited for; matrix products, arithmetic and copies ran while one was open for 0% of the time, Pallas kernels for 12%

profile of v6, /device:TPU:2, one launch (start us, length us, event | category | flops | bytes accessed | tf_op | source)
XLA Modules:
  0.0 50.3 jit_solution(6732234011021688310)
XLA Ops:
  0.0 0.0 copy-start.1
  0.0 1.0 %copy-done.1 = bf16[1,32,2,24,128]{4,3,2,1,0:T(8,128)(2,1)S(1)} copy-done((bf16[1,32,2,24,128]{4,3,2,1,0:T(8,128)(2,1)S(1)}, bf16[1,32,2,24,128]{4,3,2,1,0:T(8,128)(2,1)}, u32[]{:S(2)}) %copy-start.1) | copy-done | bytes 393240
  1.0 0.0 copy-start.2
  1.0 0.2 relay.1
  1.2 0.0 copy-start
  1.2 0.0 copy-start.3
  1.2 4.8 %collective-permute-start.1 = (bf16[768,128]{1,0:T(8,128)(2,1)S(1)}, bf16[768,128]{1,0:T(8,128)(2,1)S(1)}, u32[]{:S(2)}, u32[]{:S(2)}) collective-permute-start(bf16[768,128]{1,0:T(8,128)(2,1)S(1)} %get-tuple-element.20), channel_id=1, source_target_pairs={{16,32},{32,16},{48,64},{64,48},{80,96},{96,80},{112,128},{128,112... | collective-permute-start | bytes 589832 | tf_op jit(solution)/shard_map/ppermute | solution.py:444
  6.0 0.8 %collective-permute-start.2 = (bf16[768,128]{1,0:T(8,128)(2,1)S(1)}, bf16[768,128]{1,0:T(8,128)(2,1)S(1)}, u32[]{:S(2)}, u32[]{:S(2)}) collective-permute-start(bf16[768,128]{1,0:T(8,128)(2,1)S(1)} %get-tuple-element.21), channel_id=1, source_target_pairs={{0,16},{16,0},{32,48},{48,32},{64,80},{80,64},{96,112},{112,96},{1... | collective-permute-start | bytes 589832 | tf_op jit(solution)/shard_map/ppermute | solution.py:444
  6.8 0.0 copy-done.2
  6.8 0.1 for_prev.1
  6.9 2.8 %collective-permute-start = (bf16[2,768,128]{2,1,0:T(8,128)(2,1)S(1)}, bf16[2,768,128]{2,1,0:T(8,128)(2,1)S(1)}, u32[]{:S(2)}, u32[]{:S(2)}) collective-permute-start(bf16[2,768,128]{2,1,0:T(8,128)(2,1)S(1)} %for_prev.1), channel_id=1, source_target_pairs={{16,0},{32,16},{48,32},{64,48},{80,64},{96,80},{112,96},{128,112},... | collective-permute-start | bytes 1179656 | tf_op jit(solution)/shard_map/ppermute | solution.py:452
  9.7 0.0 copy-done
  9.7 0.0 copy-done.3
  9.7 2.5 %local_terms.1 = (bf16[4,1568,256]{2,1,0:T(8,128)(2,1)S(1)}, bf16[2,2304,128]{2,1,0:T(8,128)(2,1)S(1)}, f32[2,768,128]{2,1,0:T(8,128)S(1)}, f32[3,768,128]{2,1,0...) custom-call(bf16[32,4,48,256]{3,2,1,0:T(8,128)(2,1)S(1)} %bitcast.5, ...), custom_call_target="tpu_custom_call" | custom-call | flops 5000000000 | bytes 4036608 | tf_op jit(solution)/shard_map/local_terms/pallas_call | solution.py:345
  12.2 0.0 collective-permute-done.1.far_ref
  12.2 0.0 collective-permute-done.2.chip_ref
  12.2 3.3 %main_terms.1 = (f32[96,128]{1,0:T(8,128)S(1)}, f32[2,216,128]{2,1,0:T(8,128)S(1)}, f32[768,128]{1,0:T(8,128)S(1)}) custom-call(bf16[768,128]{1,0:T(8,128)(2,1)S(1)} %collective-permute-done.1.far_ref, bf16[768,128]{1,0:T(8,128)(2,1)S(1)} %collective-permute-done.2.chip_ref, bf16[288,256]{1,0:T(8,128)(2,1)S(1)} %get-tuple-element.19.rim_weights, ...), custom_call_target="tpu_custom_call" | custom-call | flops 5000000000 | bytes 7241728 | tf_op jit(solution)/shard_map/main_terms/pallas_call | solution.py:345
  15.5 0.0 collective-permute-done.next_ref
  15.5 1.6 %last_terms.1 = bf16[16,2,16,128]{3,2,1,0:T(8,128)(2,1)S(1)} custom-call(bf16[2,768,128]{2,1,0:T(8,128)(2,1)S(1)} %collective-permute-done.next_ref, bf16[288,256]{1,0:T(8,128)(2,1)S(1)} %get-tuple-element.19.rim_weights, f32[768,128]{1,0:T(8,128)S(1)} %get-tuple-element.28.partial_ref, bf16[128,768]{1,0:T(8,128)(2,1)S(1)} %get-tuple-element.26.spread_ref, ...), custom_call_target="tpu_custom_call" | custom-call | flops 1000000000 | bytes 4612096 | tf_op jit(solution)/shard_map/last_terms/pallas_call | solution.py:345
  17.1 15.1 %all_to_all.10.shares_ref = bf16[32,16,128]{2,1,0:T(8,128)(2,1)S(1)} all-to-all(bf16[32,16,128]{2,1,0:T(8,128)(2,1)S(1)} %bitcast.4), channel_id=1, replica_groups=mesh['space'=16,'deep'=8,'lane'=2] {'space','lane'}, dimensions={0} | all-to-all | bytes 262144 | tf_op jit(solution)/shard_map/all_to_all | solution.py:461
  32.2 17.4 %all_to_all.11.copies_ref = bf16[16,16,128]{2,1,0:T(8,128)(2,1)S(1)} all-to-all(bf16[16,16,128]{2,1,0:T(8,128)(2,1)S(1)} %share_copies.1), channel_id=1, replica_groups=mesh['space'=16,'deep'=8,'lane'=2] {'deep','lane'}, dimensions={0} | all-to-all | bytes 131072 | tf_op jit(solution)/shard_map/all_to_all | solution.py:462
  49.7 0.7 %total_rows.1 = f32[2,1728]{1,0:T(2,128)} custom-call(bf16[16,16,128]{2,1,0:T(8,128)(2,1)S(1)} %all_to_all.11.copies_ref), custom_call_target="tpu_custom_call" | custom-call | flops 1000000 | bytes 65536 | tf_op jit(solution)/shard_map/total_rows/pallas_call | solution.py:345
  (1 shorter events, 0.0 us)
Async XLA Ops:
  0.0 1.0 %copy-start.1 = (bf16[1,32,2,24,128]{4,3,2,1,0:T(8,128)(2,1)S(1)}, bf16[1,32,2,24,128]{4,3,2,1,0:T(8,128)(2,1)}, u32[]{:S(2)}) copy-start(bf16[1,32,2,24,128]{4,3,2,1,0:T(8,128)(2,1)} %param.6) | copy-start | bytes 1179652
  1.0 5.8 %copy-start.2 = (bf16[1,32,2,24,128]{4,3,2,1,0:T(8,128)(2,1)S(1)}, bf16[1,32,2,24,128]{4,3,2,1,0:T(8,128)(2,1)}, u32[]{:S(2)}) copy-start(bf16[1,32,2,24,128]{4,3,2,1,0:T(8,128)(2,1)} %param.5) | copy-start | bytes 1179652
  1.2 8.5 %copy-start = (bf16[1,32,4,48,256]{4,3,2,1,0:T(8,128)(2,1)S(1)}, bf16[1,32,4,48,256]{4,3,2,1,0:T(8,128)(2,1)}, u32[]{:S(2)}) copy-start(bf16[1,32,4,48,256]{4,3,2,1,0:T(8,128)(2,1)} %param.4) | copy-start | bytes 9437188
  1.2 8.5 %copy-start.3 = (bf16[27,32,32]{2,1,0:T(8,128)(2,1)S(1)}, bf16[27,32,32]{2,1,0:T(8,128)(2,1)}, u32[]{:S(2)}) copy-start(bf16[27,32,32]{2,1,0:T(8,128)(2,1)} %weight_ref.1) | copy-start | bytes 165892
  1.2 10.9 %collective-permute-start.1 = (bf16[768,128]{1,0:T(8,128)(2,1)S(1)}, bf16[768,128]{1,0:T(8,128)(2,1)S(1)}, u32[]{:S(2)}, u32[]{:S(2)}) collective-permute-start(bf16[768,128]{1,0:T(8,128)(2,1)S(1)} %get-tuple-element.20), channel_id=1, source_target_pairs={{16,32},{32,16},{48,64},{64,48},{80,96},{96,80},{112,128},{128,112... | collective-permute-start | bytes 589832 | tf_op jit(solution)/shard_map/ppermute | solution.py:444
  6.0 6.2 %collective-permute-start.2 = (bf16[768,128]{1,0:T(8,128)(2,1)S(1)}, bf16[768,128]{1,0:T(8,128)(2,1)S(1)}, u32[]{:S(2)}, u32[]{:S(2)}) collective-permute-start(bf16[768,128]{1,0:T(8,128)(2,1)S(1)} %get-tuple-element.21), channel_id=1, source_target_pairs={{0,16},{16,0},{32,48},{48,32},{64,80},{80,64},{96,112},{112,96},{1... | collective-permute-start | bytes 589832 | tf_op jit(solution)/shard_map/ppermute | solution.py:444
  6.9 8.6 %collective-permute-start = (bf16[2,768,128]{2,1,0:T(8,128)(2,1)S(1)}, bf16[2,768,128]{2,1,0:T(8,128)(2,1)S(1)}, u32[]{:S(2)}, u32[]{:S(2)}) collective-permute-start(bf16[2,768,128]{2,1,0:T(8,128)(2,1)S(1)} %for_prev.1), channel_id=1, source_target_pairs={{16,0},{32,16},{48,32},{64,48},{80,64},{96,80},{112,96},{128,112},... | collective-permute-start | bytes 1179656 | tf_op jit(solution)/shard_map/ppermute | solution.py:452

commit v7 on v6

--- a/solution.py
+++ b/solution.py
@@ -90,13 +90,9 @@
 
 def local_kernel(
     act_ref, pre_ref, weight_ref, planes_ref,
-    act_t, hidden_t, scale_t, partial_t, rim_weights, spread_ref, second_ref,
+    act_t, hidden_t, scale_t, partial_t, rim_weights, second_ref,
     weight_t,
 ):
-    row = lax.broadcasted_iota(jnp.int32, (QY, 3 * IY), 0)
-    col = lax.broadcasted_iota(jnp.int32, (QY, 3 * IY), 1)
-    spread_ref[...] = jnp.where(col % IY == 2 * row + col // IY - 1, 1.0, 0.0).astype(BF)
-
     for j in range(3):
         for k in range(3):
             base = (2 - j) * 9 + (2 - k) * 3
@@ -119,9 +115,14 @@
             ).astype(BF)
             scale_t[plane, z * C : (z + 1) * C, :] = gate * (1.0 + pre * (1.0 - gate))
 
+    row = lax.broadcasted_iota(jnp.int32, (IY, IY), 0)
+    col = lax.broadcasted_iota(jnp.int32, (IY, IY), 1)
+    split = jnp.where(row == 2 * (col % QY) + col // QY, 1.0, 0.0).astype(BF)
     for plane in range(IX):
         act_t[plane, 0:C, :] = jnp.zeros((C, IY), BF)
-        act_t[plane, C:, :] = by_depth(act_ref[:, plane])
+        rows = act_ref[:, plane].reshape(C * IZ, IY)
+        rows = jnp.dot(rows, split, preferred_element_type=F32).astype(BF)
+        act_t[plane, C:, :] = by_depth(rows.reshape(C, IZ, IY))
 
     for z in range(0, QZ, 2):
         slab = depth_pair([planes_ref.at[x] for x in range(QX)], z)
@@ -148,38 +149,73 @@
     second_ref[2 * T3 :, :] = total[T3:, 0:128]
 
 
-def spread_plane(grad_ref, spread_ref, wide_ref):
-    for z0 in range(0, QZ, 4):
-        wide = jnp.dot(
-            grad_ref[z0 * C : (z0 + 4) * C, :], spread_ref[...], preferred_element_type=F32
-        ).astype(BF)
-        for h in range(4):
-            for d in range(3):
-                begin = (z0 + h) * T3 + d * C
-                wide_ref[begin : begin + C, :] = wide[h * C : (h + 1) * C, d * IY : (d + 1) * IY]
-
-
-def dense_row(flips, second, ab, d):
+def put_grad(even_ref, odd_ref, z, grad):
+    here = grad.astype(BF)
+    even_ref[z * C : (z + 1) * C, :] = here
+    odd_ref[2 * z * C : (2 * z + 1) * C, :] = lane_shift(grad, -1).astype(BF)
+    odd_ref[(2 * z + 1) * C : (2 * z + 2) * C, :] = here
+
+
+def cell_sums(act_t, planes, even_refs, odd_refs):
+    totals = [0.0, 0.0]
+    for z0 in range(0, QZ, 8):
+        for side, (refs, step) in enumerate(((even_refs, C), (odd_refs, 2 * C))):
+            lanes = slice(side * QY, (side + 1) * QY)
+            acts = jnp.concatenate(
+                [
+                    jnp.concatenate(
+                        [act_t[plane, 2 * z * C : (2 * z + 3) * C, lanes] for z in range(z0, z0 + 8)],
+                        axis=1,
+                    )
+                    for plane in planes
+                ],
+                axis=0,
+            )
+            grads = jnp.concatenate(
+                [
+                    jnp.concatenate([ref[z * step : (z + 1) * step, :] for z in range(z0, z0 + 8)], axis=1)
+                    for ref in refs
+                ],
+                axis=0,
+            )
+            totals[side] = totals[side] + nt_dot(acts, grads)
+    return totals
+
+
+def dense_row(blocks):
     lane = lax.broadcasted_iota(jnp.int32, (8, 128), 1)
     row = jnp.zeros((8, 128), F32)
-    for r in range(4):
-        if second:
-            ab_rev = (2 - ab // 3) * 3 + (2 - ab % 3)
-            side, offset, begin = 0, d * C, ab_rev * C + r
-        else:
-            side, offset, begin = ab // 4, (ab % 4) * C, d * C + r
-        part = flips[side, pl.ds(begin, 8, stride=4), :]
+    for r, (source, begin, offset) in enumerate(blocks):
+        part = source[pl.ds(begin, 8, stride=4), :]
         turn = (r * C - offset) % 128
         part = pltpu.roll(part, turn, 1) if turn else part
         row = jnp.where(lane // C == r, part, row)
     return row
 
 
+def second_row(source, ab, d):
+    ab_rev = (2 - ab // 3) * 3 + (2 - ab % 3)
+    return dense_row([(source, ab_rev * C + r, d * C) for r in range(4)])
+
+
+def first_row(flips, ab, d):
+    begin = (C, 0, 2 * C)[d]
+    return dense_row([(flips.at[ab // 4], begin + r, (ab % 4) * C) for r in range(4)])
+
+
+def first_flips(flips, side, total):
+    rows = slice(0, C) if side == 0 else slice(C, T3)
+    turned = total.T
+    for begin in range(0, total.shape[0], 128):
+        width = min(128, total.shape[0] - begin)
+        flips[begin // 128, rows, 0:width] = turned[:, begin : begin + width]
+
+
 def main_kernel(
     far_ref, chip_ref, rim_weights, partial_ref, scale_ref, hidden_t, act_t,
-    spread_ref, second_in,
+    second_in,
     first_ref, dense_ref, partial_next,
-    halo_ref, grads, wide, acc, second_ref, flips,
+    halo_ref, even, odds, second_ref, flips,
 ):
     odd = on_odd()
     for x in range(QX):
@@ -200,10 +236,8 @@
                 for x in range(QX + 1)
             ]
             for x in range(QX):
-                grads[x, rows, :] = (parts[x] * scale_ref[x, rows, :]).astype(BF)
+                put_grad(even.at[x], odds.at[x], z + h, parts[x] * scale_ref[x, rows, :])
             partial_next[rows, :] = parts[QX]
-    for x in range(QX):
-        spread_plane(grads.at[x], spread_ref, wide.at[x])
 
     total = jnp.zeros((2 * T3, 256), F32)
     for z0 in range(0, QZ, 8):
@@ -215,58 +249,37 @@
             axis=0,
         )
         total = total + nt_dot(slab, hidden_rows(hidden_t, z0))
-    second_ref[0, 0:T3, :] = second_in[0:T3, :] + total[0:T3, 0:128]
-    second_ref[0, T3 : 2 * T3, :] = second_in[T3 : 2 * T3, :]
-    second_ref[0, 2 * T3 :, :] = second_in[2 * T3 :, :] + total[T3:, 128:256]
+    second_ref[0:T3, :] = second_in[0:T3, :] + total[0:T3, 0:128]
+    second_ref[T3 : 2 * T3, :] = second_in[T3 : 2 * T3, :]
+    second_ref[2 * T3 :, :] = second_in[2 * T3 :, :] + total[T3:, 128:256]
     for ab in range(9):
         for d in range(3):
             begin = (ab * 3 + d) * 8
-            dense_ref[1, begin : begin + 8, :] = dense_row(second_ref, True, ab, d)
-
-    for z0 in range(0, QZ, 4):
-        acts = jnp.concatenate(
-            [
-                jnp.concatenate(
-                    [act_t[plane, 2 * z * C : (2 * z + 3) * C, :] for z in range(z0, z0 + 4)], axis=1
-                )
-                for plane in range(IX)
-            ],
-            axis=0,
+            dense_ref[1, begin : begin + 8, :] = second_row(second_ref, ab, d)
+
+    even_sum, odd_sum = cell_sums(
+        act_t, range(IX), [even.at[x] for x in range(QX)], [odds.at[x] for x in range(QX)]
+    )
+    even_sum, odd_sum = [
+        [total[plane * T3 : (plane + 1) * T3] for plane in range(IX)] for total in (even_sum, odd_sum)
+    ]
+    first_ref[0, :, 0:C] = even_sum[1][:, C : 2 * C]
+    first_ref[1, :, 0 : 2 * C] = odd_sum[1][:, 2 * C :]
+    for side, (total, width) in enumerate(((even_sum, C), (odd_sum, 2 * C))):
+        joined = jnp.concatenate(
+            [total[p][:, 0:width] + total[p + 2][:, width : 2 * width] for p in range(2)], axis=0
         )
-        ups = jnp.concatenate(
-            [
-                jnp.concatenate(
-                    [four_blocks(wide[x, z * T3 : (z + 1) * T3, :]) for x in range(QX)], axis=0
-                )
-                for z in range(z0, z0 + 4)
-            ],
-            axis=1,
-        )
-        part = nt_dot(acts, ups)
-        if z0 == 0:
-            acc[...] = part
-        else:
-            acc[...] += part
-    first_ref[...] = acc[T3 : 2 * T3, 128:256]
-    turned = jnp.concatenate(
-        [
-            acc[0:T3, 0:128] + acc[2 * T3 : 3 * T3, 128:256],
-            acc[T3 : 2 * T3, 0:128] + acc[3 * T3 :, 128:256],
-        ],
-        axis=0,
-    ).T
-    flips[0] = turned[:, 0:128]
-    flips[1, :, 0 : 2 * T3 - 128] = turned[:, 128:]
+        first_flips(flips, side, joined)
     for ab in range(6):
         for d in range(3):
             begin = ((ab + 3) * 3 + d) * 8
-            dense_ref[0, begin : begin + 8, :] = dense_row(flips, False, ab, d)
+            dense_ref[0, begin : begin + 8, :] = first_row(flips, ab, d)
 
 
 def last_kernel(
-    next_ref, rim_weights, partial_ref, spread_ref, act_t, first_ref, dense_ref,
+    next_ref, rim_weights, partial_ref, act_t, first_ref, dense_ref,
     out_ref,
-    plane, scale, grads, wide, flips, head,
+    plane, scale, even, odds, flips, head,
 ):
     more = lax.axis_index("space") < lax.axis_size("space") - 1
     plane[0:C, :] = jnp.zeros((C, QY), BF)
@@ -282,23 +295,14 @@
         for h in range(2):
             rows = slice((z + h) * C, (z + h + 1) * C)
             grad = partial_ref[rows, :] + taps_joined(terms[:, h * QY : (h + 1) * QY])
-            grads[rows, :] = (grad * scale[rows, :]).astype(BF)
-    spread_plane(grads, spread_ref, wide)
-    total = first_ref[...]
-    for z0 in range(0, QZ, 4):
-        acts = jnp.concatenate(
-            [act_t[IX - 1, 2 * z * C : (2 * z + 3) * C, :] for z in range(z0, z0 + 4)], axis=1
-        )
-        ups = jnp.concatenate(
-            [four_blocks(wide[z * T3 : (z + 1) * T3, :]) for z in range(z0, z0 + 4)], axis=1
-        )
-        total = total + nt_dot(acts, ups)
-
-    flips[0, :, 0:T3] = total.T
+            put_grad(even, odds, z + h, grad * scale[rows, :])
+    even_sum, odd_sum = cell_sums(act_t, [IX - 1], [even], [odds])
+    first_flips(flips, 0, even_sum + first_ref[0, :, 0:C])
+    first_flips(flips, 1, odd_sum + first_ref[1, :, 0 : 2 * C])
     for ab in range(3):
         for d in range(3):
             begin = (ab * 3 + d) * 8
-            head[begin : begin + 8, :] = dense_row(flips, False, ab, d)
+            head[begin : begin + 8, :] = first_row(flips, ab, d)
 
     for s in range(16):
         begin = (27 * s) // 2
@@ -324,9 +328,9 @@
     lane = lax.broadcasted_iota(jnp.int32, (16, 128), 1)
     rows = []
     for which in range(2):
-        total = copies_ref[which].astype(F32)
+        total = copies_ref[8 * which].astype(F32)
         for deep in range(1, 8):
-            total = total + copies_ref[2 * deep + which].astype(F32)
+            total = total + copies_ref[8 * which + deep].astype(F32)
         turned = pltpu.roll(total, 64, 1)
         after = jnp.concatenate([turned[1:], turned[0:1]], axis=0)
         rows.append(jnp.where(odd, jnp.where(lane < 64, turned, after), total))
@@ -382,7 +386,6 @@
             ((QX, QZ * C, QY), F32),
             ((QX + 1, QZ * C, QY), F32),
             ((3 * T3, 256), BF),
-            ((QY, 3 * IY), BF),
             ((TAPS, 128), F32),
         ],
         [
@@ -397,14 +400,13 @@
     return call(
         main_kernel,
         "main_terms",
-        [((T3, 128), F32), ((2, 216, 128), F32), ((QZ * C, QY), F32)],
+        [((2, T3, 128), F32), ((2, 216, 128), F32), ((QZ * C, QY), F32)],
         [
             VMEM((QX, COT_ROWS, QY), BF),
             VMEM((QX, QZ * C, QY), BF),
-            VMEM((QX, QZ * T3, IY), BF),
-            VMEM((4 * T3, 256), F32),
-            VMEM((1, TAPS, 128), F32),
-            VMEM((2, 128, 128), F32),
+            VMEM((QX, QZ * 2 * C, QY), BF),
+            VMEM((TAPS, 128), F32),
+            VMEM((2, T3, 128), F32),
         ],
         5 * 10**9,
         *args,
@@ -420,8 +422,8 @@
             VMEM((COT_ROWS, QY), BF),
             VMEM((QZ * C, QY), F32),
             VMEM((QZ * C, QY), BF),
-            VMEM((QZ * T3, IY), BF),
-            VMEM((1, 128, 128), F32),
+            VMEM((QZ * 2 * C, QY), BF),
+            VMEM((1, T3, 128), F32),
             VMEM((72, 128), F32),
         ],
         10**9,
@@ -451,15 +453,15 @@
     far = swapped(to_far, 1)
     after = lax.ppermute(to_prev, "space", [(i + 1, i) for i in range(lax.axis_size("space") - 1)])
     chip = swapped(to_chip, 0)
-    act_t, hidden_t, scale, partial, rim_weights, spread, second = local_terms(
+    act_t, hidden_t, scale, partial, rim_weights, second = local_terms(
         act, pre, conv_weight, planes
     )
     first, dense, partial_next = main_terms(
-        far, chip, rim_weights, partial, scale, hidden_t, act_t, spread, second
-    )
-    terms = last_terms(after, rim_weights, partial_next, spread, act_t, first, dense)
+        far, chip, rim_weights, partial, scale, hidden_t, act_t, second
+    )
+    terms = last_terms(after, rim_weights, partial_next, act_t, first, dense)
     shares = lax.all_to_all(terms.reshape(32, 16, 128), ("space", "lane"), 0, 0, tiled=True)
-    copies = lax.all_to_all(share_copies(shares), ("deep", "lane"), 0, 0, tiled=True)
+    copies = lax.all_to_all(share_copies(shares), ("lane", "deep"), 0, 0, tiled=True)
     return total_rows(copies)
 
 

time: 51.1 us -> 50 us (0.978)
  Pallas kernels: 8.4 us -> 7.69 us
    pallas_call x7, Pallas kernels: 8.4 us -> 7.69 us  [call(): pl.pallas_call(kernel, out_shape=shapes, in_specs=[pl.BlockSpec(memory_sp...]
    all_to_all x1, blocking collectives: 17.4 us -> 16.9 us  [on_device(): lax.all_to_all(share_copies(shares), ('lane', 'deep'), 0, 0, tiled=True)]
  transfers between devices with their start and end apart: 3 -> 3, of which waited for: 0 -> 0; matrix products, arithmetic and copies ran while one was open for 0% -> 0% of each run, Pallas kernels for 12% -> 11%
where the time goes in v7:
time: 50 us; the launch traced here: 49.3 us
  blocking collectives  32.2 us (64%)
  starting transfers between devices  8.34 us (17%)
  Pallas kernels  7.69 us (15%)
  local copies, waits for them, and re-layouts  1.01 us (2%)
    all_to_all x1, blocking collectives, on_device(): lax.all_to_all(share_copies(shares), ('lane', 'deep'), 0, 0, tiled=True)  16.9 us
    all_to_all x1, blocking collectives, on_device(): lax.all_to_all(terms.reshape(32, 16, 128), ('space', 'lane'), 0, 0, tiled...  15.3 us
    pallas_call x7, Pallas kernels, call(): pl.pallas_call(kernel, out_shape=shapes, in_specs=[pl.BlockSpec(memory_sp...  7.69 us
    ppermute x2, starting transfers between devices, swapped(): return lax.ppermute(x, 'space', pairs)  5.57 us
    ppermute x1, starting transfers between devices, on_device(): lax.ppermute(to_prev, 'space', [(i + 1, i) for i in range(lax.axis_size('...  2.77 us
    unnamed x8, local copies, waits for them, and re-layouts  1.01 us
  transfers between devices with their start and end apart: 3, of which 0 were waited for; matrix products, arithmetic and copies ran while one was open for 0% of the time, Pallas kernels for 11%

profile of v7, /device:TPU:2, one launch (start us, length us, event | category | flops | bytes accessed | tf_op | source)
XLA Modules:
  0.0 49.3 jit_solution(9465919371740588552)
XLA Ops:
  0.0 0.0 copy-start.1
  0.0 1.0 %copy-done.1 = bf16[1,32,2,24,128]{4,3,2,1,0:T(8,128)(2,1)S(1)} copy-done((bf16[1,32,2,24,128]{4,3,2,1,0:T(8,128)(2,1)S(1)}, bf16[1,32,2,24,128]{4,3,2,1,0:T(8,128)(2,1)}, u32[]{:S(2)}) %copy-start.1) | copy-done | bytes 393240
  1.0 0.0 copy-start.2
  1.0 0.2 relay.1
  1.2 0.0 copy-start
  1.2 0.0 copy-start.3
  1.2 4.8 %collective-permute-start.1 = (bf16[768,128]{1,0:T(8,128)(2,1)S(1)}, bf16[768,128]{1,0:T(8,128)(2,1)S(1)}, u32[]{:S(2)}, u32[]{:S(2)}) collective-permute-start(bf16[768,128]{1,0:T(8,128)(2,1)S(1)} %get-tuple-element.19), channel_id=1, source_target_pairs={{16,32},{32,16},{48,64},{64,48},{80,96},{96,80},{112,128},{128,112... | collective-permute-start | bytes 589832 | tf_op jit(solution)/shard_map/ppermute | solution.py:446
  6.0 0.8 %collective-permute-start.2 = (bf16[768,128]{1,0:T(8,128)(2,1)S(1)}, bf16[768,128]{1,0:T(8,128)(2,1)S(1)}, u32[]{:S(2)}, u32[]{:S(2)}) collective-permute-start(bf16[768,128]{1,0:T(8,128)(2,1)S(1)} %get-tuple-element.20), channel_id=1, source_target_pairs={{0,16},{16,0},{32,48},{48,32},{64,80},{80,64},{96,112},{112,96},{1... | collective-permute-start | bytes 589832 | tf_op jit(solution)/shard_map/ppermute | solution.py:446
  6.8 0.0 copy-done.2
  6.8 0.1 for_prev.1
  6.9 2.8 %collective-permute-start = (bf16[2,768,128]{2,1,0:T(8,128)(2,1)S(1)}, bf16[2,768,128]{2,1,0:T(8,128)(2,1)S(1)}, u32[]{:S(2)}, u32[]{:S(2)}) collective-permute-start(bf16[2,768,128]{2,1,0:T(8,128)(2,1)S(1)} %for_prev.1), channel_id=1, source_target_pairs={{16,0},{32,16},{48,32},{64,48},{80,64},{96,80},{112,96},{128,112},... | collective-permute-start | bytes 1179656 | tf_op jit(solution)/shard_map/ppermute | solution.py:454
  9.7 0.0 copy-done
  9.7 0.0 copy-done.3
  9.7 2.8 %local_terms.1 = (bf16[4,1568,256]{2,1,0:T(8,128)(2,1)S(1)}, bf16[2,2304,128]{2,1,0:T(8,128)(2,1)S(1)}, f32[2,768,128]{2,1,0:T(8,128)S(1)}, f32[3,768,128]{2,1,0...) custom-call(bf16[32,4,48,256]{3,2,1,0:T(8,128)(2,1)S(1)} %bitcast.5, ...), custom_call_target="tpu_custom_call" | custom-call | flops 5000000000 | bytes 4036608 | tf_op jit(solution)/shard_map/local_terms/pallas_call | solution.py:349
  12.5 0.0 collective-permute-done.1.far_ref
  12.5 0.0 collective-permute-done.2.chip_ref
  12.5 2.8 %main_terms.1 = (f32[2,96,128]{2,1,0:T(8,128)S(1)}, f32[2,216,128]{2,1,0:T(8,128)S(1)}, f32[768,128]{1,0:T(8,128)S(1)}) custom-call(bf16[768,128]{1,0:T(8,128)(2,1)S(1)} %collective-permute-done.1.far_ref, bf16[768,128]{1,0:T(8,128)(2,1)S(1)} %collective-permute-done.2.chip_ref, bf16[288,256]{1,0:T(8,128)(2,1)S(1)} %get-tuple-element.18.rim_weights, ...), custom_call_target="tpu_custom_call" | custom-call | flops 5000000000 | bytes 7045120 | tf_op jit(solution)/shard_map/main_terms/pallas_call | solution.py:349
  15.3 0.0 collective-permute-done.next_ref
  15.3 1.1 %last_terms.1 = bf16[16,2,16,128]{3,2,1,0:T(8,128)(2,1)S(1)} custom-call(bf16[2,768,128]{2,1,0:T(8,128)(2,1)S(1)} %collective-permute-done.next_ref, bf16[288,256]{1,0:T(8,128)(2,1)S(1)} %get-tuple-element.18.rim_weights, f32[768,128]{1,0:T(8,128)S(1)} %get-tuple-element.26.partial_ref, bf16[4,1568,256]{2,1,0:T(8,128)(2,1)S(1)} %get-tuple-element.24.act_t, ...), custom_call_target="tpu_custom_call" | custom-call | flops 1000000000 | bytes 4464640 | tf_op jit(solution)/shard_map/last_terms/pallas_call | solution.py:349
  16.4 15.3 %all_to_all.10.shares_ref = bf16[32,16,128]{2,1,0:T(8,128)(2,1)S(1)} all-to-all(bf16[32,16,128]{2,1,0:T(8,128)(2,1)S(1)} %bitcast.4), channel_id=1, replica_groups=mesh['space'=16,'deep'=8,'lane'=2] {'space','lane'}, dimensions={0} | all-to-all | bytes 262144 | tf_op jit(solution)/shard_map/all_to_all | solution.py:463
  31.7 16.9 %all_to_all.11.copies_ref = bf16[16,16,128]{2,1,0:T(8,128)(2,1)S(1)} all-to-all(bf16[16,16,128]{2,1,0:T(8,128)(2,1)S(1)} %share_copies.1), channel_id=1, replica_groups=mesh['space'=16,'deep'=8,'lane'=2] {'lane','deep'}, dimensions={0} | all-to-all | bytes 131072 | tf_op jit(solution)/shard_map/all_to_all | solution.py:464
  48.6 0.7 %total_rows.1 = f32[2,1728]{1,0:T(2,128)} custom-call(bf16[16,16,128]{2,1,0:T(8,128)(2,1)S(1)} %all_to_all.11.copies_ref), custom_call_target="tpu_custom_call" | custom-call | flops 1000000 | bytes 65536 | tf_op jit(solution)/shard_map/total_rows/pallas_call | solution.py:349
  (1 shorter events, 0.0 us)
Async XLA Ops:
  0.0 1.0 %copy-start.1 = (bf16[1,32,2,24,128]{4,3,2,1,0:T(8,128)(2,1)S(1)}, bf16[1,32,2,24,128]{4,3,2,1,0:T(8,128)(2,1)}, u32[]{:S(2)}) copy-start(bf16[1,32,2,24,128]{4,3,2,1,0:T(8,128)(2,1)} %param.6) | copy-start | bytes 1179652
  1.0 5.8 %copy-start.2 = (bf16[1,32,2,24,128]{4,3,2,1,0:T(8,128)(2,1)S(1)}, bf16[1,32,2,24,128]{4,3,2,1,0:T(8,128)(2,1)}, u32[]{:S(2)}) copy-start(bf16[1,32,2,24,128]{4,3,2,1,0:T(8,128)(2,1)} %param.5) | copy-start | bytes 1179652
  1.2 8.5 %copy-start = (bf16[1,32,4,48,256]{4,3,2,1,0:T(8,128)(2,1)S(1)}, bf16[1,32,4,48,256]{4,3,2,1,0:T(8,128)(2,1)}, u32[]{:S(2)}) copy-start(bf16[1,32,4,48,256]{4,3,2,1,0:T(8,128)(2,1)} %param.4) | copy-start | bytes 9437188
  1.2 8.5 %copy-start.3 = (bf16[27,32,32]{2,1,0:T(8,128)(2,1)S(1)}, bf16[27,32,32]{2,1,0:T(8,128)(2,1)}, u32[]{:S(2)}) copy-start(bf16[27,32,32]{2,1,0:T(8,128)(2,1)} %weight_ref.1) | copy-start | bytes 165892
  1.2 11.3 %collective-permute-start.1 = (bf16[768,128]{1,0:T(8,128)(2,1)S(1)}, bf16[768,128]{1,0:T(8,128)(2,1)S(1)}, u32[]{:S(2)}, u32[]{:S(2)}) collective-permute-start(bf16[768,128]{1,0:T(8,128)(2,1)S(1)} %get-tuple-element.19), channel_id=1, source_target_pairs={{16,32},{32,16},{48,64},{64,48},{80,96},{96,80},{112,128},{128,112... | collective-permute-start | bytes 589832 | tf_op jit(solution)/shard_map/ppermute | solution.py:446
  6.0 6.5 %collective-permute-start.2 = (bf16[768,128]{1,0:T(8,128)(2,1)S(1)}, bf16[768,128]{1,0:T(8,128)(2,1)S(1)}, u32[]{:S(2)}, u32[]{:S(2)}) collective-permute-start(bf16[768,128]{1,0:T(8,128)(2,1)S(1)} %get-tuple-element.20), channel_id=1, source_target_pairs={{0,16},{16,0},{32,48},{48,32},{64,80},{80,64},{96,112},{112,96},{1... | collective-permute-start | bytes 589832 | tf_op jit(solution)/shard_map/ppermute | solution.py:446
  6.9 8.4 %collective-permute-start = (bf16[2,768,128]{2,1,0:T(8,128)(2,1)S(1)}, bf16[2,768,128]{2,1,0:T(8,128)(2,1)S(1)}, u32[]{:S(2)}, u32[]{:S(2)}) collective-permute-start(bf16[2,768,128]{2,1,0:T(8,128)(2,1)S(1)} %for_prev.1), channel_id=1, source_target_pairs={{16,0},{32,16},{48,32},{64,48},{80,64},{96,80},{112,96},{128,112},... | collective-permute-start | bytes 1179656 | tf_op jit(solution)/shard_map/ppermute | solution.py:454

commit v8 on v7

--- a/solution.py
+++ b/solution.py
@@ -17,6 +17,9 @@
 TAPS = 9 * C
 
 NT = (((1,), (1,)), ((), ()))
+
+SHARE_ORDER = [divmod((i + 22) % 32, 2) for i in range(32)]
+COPY_ORDER = [(lane, (i + 4) % 8) for lane in (1, 0) for i in range(8)]
 
 
 def nt_dot(a, b):
@@ -312,7 +315,7 @@
             if known < 14:
                 begins.append(dense_ref[which, begin + known : begin + 14, :])
             begins.append(jnp.zeros((2, 128), F32))
-            out_ref[s, which] = jnp.concatenate(begins, axis=0).astype(BF)
+            out_ref[SHARE_ORDER.index((s, which))] = jnp.concatenate(begins, axis=0).astype(BF)
 
 
 def share_kernel(shares_ref, copies_ref):
@@ -328,9 +331,10 @@
     lane = lax.broadcasted_iota(jnp.int32, (16, 128), 1)
     rows = []
     for which in range(2):
-        total = copies_ref[8 * which].astype(F32)
-        for deep in range(1, 8):
-            total = total + copies_ref[8 * which + deep].astype(F32)
+        first, *others = [i for i, (lane_at, _) in enumerate(COPY_ORDER) if lane_at == which]
+        total = copies_ref[first].astype(F32)
+        for i in others:
+            total = total + copies_ref[i].astype(F32)
         turned = pltpu.roll(total, 64, 1)
         after = jnp.concatenate([turned[1:], turned[0:1]], axis=0)
         rows.append(jnp.where(odd, jnp.where(lane < 64, turned, after), total))
@@ -417,7 +421,7 @@
     return call(
         last_kernel,
         "last_terms",
-        [((16, 2, 16, 128), BF)],
+        [((32, 16, 128), BF)],
         [
             VMEM((COT_ROWS, QY), BF),
             VMEM((QZ * C, QY), F32),
@@ -444,6 +448,13 @@
     for i in range(begin, lax.axis_size("space") - 1, 2):
         pairs += [(i, i + 1), (i + 1, i)]
     return lax.ppermute(x, "space", pairs)
+
+
+def exchanged(x, groups):
+    groups = [[(s * 8 + z) * 2 + y for s, z, y in group] for group in groups]
+    return lax.all_to_all(
+        x, ("space", "deep", "lane"), 0, 0, axis_index_groups=groups, tiled=True
+    )
 
 
 def on_device(activations, preact, cotangent, conv_weight):
@@ -460,8 +471,10 @@
         far, chip, rim_weights, partial, scale, hidden_t, act_t, second
     )
     terms = last_terms(after, rim_weights, partial_next, act_t, first, dense)
-    shares = lax.all_to_all(terms.reshape(32, 16, 128), ("space", "lane"), 0, 0, tiled=True)
-    copies = lax.all_to_all(share_copies(shares), ("lane", "deep"), 0, 0, tiled=True)
+    shares = exchanged(terms, [[(s, z, y) for s, y in SHARE_ORDER] for z in range(8)])
+    copies = exchanged(
+        share_copies(shares), [[(s, z, y) for y, z in COPY_ORDER] for s in range(16)]
+    )
     return total_rows(copies)
 
 

time: 50 us -> 44 us (0.88)
  blocking collectives: 32.2 us -> 26.6 us
    all_to_all x2, blocking collectives: 32.2 us -> 26.6 us  [exchanged(): lax.all_to_all(x, ('space', 'deep', 'lane'), 0, 0, axis_index_groups=grou...]
  transfers between devices with their start and end apart: 3 -> 3, of which waited for: 0 -> 0; matrix products, arithmetic and copies ran while one was open for 0% -> 0% of each run, Pallas kernels for 11% -> 13%
where the time goes in v8:
time: 44 us; the launch traced here: 43.8 us
  blocking collectives  26.6 us (60%)
  starting transfers between devices  8.34 us (19%)
  Pallas kernels  7.69 us (17%)
  local copies, waits for them, and re-layouts  1.01 us (2%)
    all_to_all x2, blocking collectives, exchanged(): lax.all_to_all(x, ('space', 'deep', 'lane'), 0, 0, axis_index_groups=grou...  26.6 us
    pallas_call x7, Pallas kernels, call(): pl.pallas_call(kernel, out_shape=shapes, in_specs=[pl.BlockSpec(memory_sp...  7.69 us
    ppermute x2, starting transfers between devices, swapped(): return lax.ppermute(x, 'space', pairs)  5.57 us
    ppermute x1, starting transfers between devices, on_device(): lax.ppermute(to_prev, 'space', [(i + 1, i) for i in range(lax.axis_size('...  2.77 us
    unnamed x8, local copies, waits for them, and re-layouts  1.01 us
  transfers between devices with their start and end apart: 3, of which 0 were waited for; matrix products, arithmetic and copies ran while one was open for 0% of the time, Pallas kernels for 13%

profile of v8, /device:TPU:2, one launch (start us, length us, event | category | flops | bytes accessed | tf_op | source)
XLA Modules:
  0.0 43.8 jit_solution(13781202489027179777)
XLA Ops:
  0.0 0.0 copy-start.1
  0.0 1.0 %copy-done.1 = bf16[1,32,2,24,128]{4,3,2,1,0:T(8,128)(2,1)S(1)} copy-done((bf16[1,32,2,24,128]{4,3,2,1,0:T(8,128)(2,1)S(1)}, bf16[1,32,2,24,128]{4,3,2,1,0:T(8,128)(2,1)}, u32[]{:S(2)}) %copy-start.1) | copy-done | bytes 393240
  1.0 0.0 copy-start.2
  1.0 0.2 relay.1
  1.2 0.0 copy-start
  1.2 0.0 copy-start.3
  1.2 4.8 %collective-permute-start.1 = (bf16[768,128]{1,0:T(8,128)(2,1)S(1)}, bf16[768,128]{1,0:T(8,128)(2,1)S(1)}, u32[]{:S(2)}, u32[]{:S(2)}) collective-permute-start(bf16[768,128]{1,0:T(8,128)(2,1)S(1)} %get-tuple-element.19), channel_id=1, source_target_pairs={{16,32},{32,16},{48,64},{64,48},{80,96},{96,80},{112,128},{128,112... | collective-permute-start | bytes 589832 | tf_op jit(solution)/shard_map/ppermute | solution.py:450
  6.0 0.8 %collective-permute-start.2 = (bf16[768,128]{1,0:T(8,128)(2,1)S(1)}, bf16[768,128]{1,0:T(8,128)(2,1)S(1)}, u32[]{:S(2)}, u32[]{:S(2)}) collective-permute-start(bf16[768,128]{1,0:T(8,128)(2,1)S(1)} %get-tuple-element.20), channel_id=1, source_target_pairs={{0,16},{16,0},{32,48},{48,32},{64,80},{80,64},{96,112},{112,96},{1... | collective-permute-start | bytes 589832 | tf_op jit(solution)/shard_map/ppermute | solution.py:450
  6.8 0.0 copy-done.2
  6.8 0.1 for_prev.1
  6.9 2.8 %collective-permute-start = (bf16[2,768,128]{2,1,0:T(8,128)(2,1)S(1)}, bf16[2,768,128]{2,1,0:T(8,128)(2,1)S(1)}, u32[]{:S(2)}, u32[]{:S(2)}) collective-permute-start(bf16[2,768,128]{2,1,0:T(8,128)(2,1)S(1)} %for_prev.1), channel_id=1, source_target_pairs={{16,0},{32,16},{48,32},{64,48},{80,64},{96,80},{112,96},{128,112},... | collective-permute-start | bytes 1179656 | tf_op jit(solution)/shard_map/ppermute | solution.py:465
  9.7 0.0 copy-done
  9.7 0.0 copy-done.3
  9.7 2.8 %local_terms.1 = (bf16[4,1568,256]{2,1,0:T(8,128)(2,1)S(1)}, bf16[2,2304,128]{2,1,0:T(8,128)(2,1)S(1)}, f32[2,768,128]{2,1,0:T(8,128)S(1)}, f32[3,768,128]{2,1,0...) custom-call(bf16[32,4,48,256]{3,2,1,0:T(8,128)(2,1)S(1)} %bitcast.3, ...), custom_call_target="tpu_custom_call" | custom-call | flops 5000000000 | bytes 4036608 | tf_op jit(solution)/shard_map/local_terms/pallas_call | solution.py:353
  12.5 0.0 collective-permute-done.1.far_ref
  12.5 0.0 collective-permute-done.2.chip_ref
  12.5 2.8 %main_terms.1 = (f32[2,96,128]{2,1,0:T(8,128)S(1)}, f32[2,216,128]{2,1,0:T(8,128)S(1)}, f32[768,128]{1,0:T(8,128)S(1)}) custom-call(bf16[768,128]{1,0:T(8,128)(2,1)S(1)} %collective-permute-done.1.far_ref, bf16[768,128]{1,0:T(8,128)(2,1)S(1)} %collective-permute-done.2.chip_ref, bf16[288,256]{1,0:T(8,128)(2,1)S(1)} %get-tuple-element.18.rim_weights, ...), custom_call_target="tpu_custom_call" | custom-call | flops 5000000000 | bytes 7045120 | tf_op jit(solution)/shard_map/main_terms/pallas_call | solution.py:353
  15.3 0.0 collective-permute-done.next_ref
  15.3 1.1 %last_terms.1 = bf16[32,16,128]{2,1,0:T(8,128)(2,1)S(1)} custom-call(bf16[2,768,128]{2,1,0:T(8,128)(2,1)S(1)} %collective-permute-done.next_ref, bf16[288,256]{1,0:T(8,128)(2,1)S(1)} %get-tuple-element.18.rim_weights, f32[768,128]{1,0:T(8,128)S(1)} %get-tuple-element.26.partial_ref, bf16[4,1568,256]{2,1,0:T(8,128)(2,1)S(1)} %get-tuple-element.24.act_t, ...), custom_call_target="tpu_custom_call" | custom-call | flops 1000000000 | bytes 4464640 | tf_op jit(solution)/shard_map/last_terms/pallas_call | solution.py:353
  16.4 12.5 %all_to_all.10.shares_ref = bf16[32,16,128]{2,1,0:T(8,128)(2,1)S(1)} all-to-all(bf16[32,16,128]{2,1,0:T(8,128)(2,1)S(1)} %last_terms.1), channel_id=1, replica_groups={{176,177,192,193,208,209,224,225,240,241,0,1,16,17,32,33,48,49,64,65,80..., dimensions={0} | all-to-all | bytes 262144 | tf_op jit(solution)/shard_map/all_to_all | solution.py:455
  29.0 14.1 %all_to_all.11.copies_ref = bf16[16,16,128]{2,1,0:T(8,128)(2,1)S(1)} all-to-all(bf16[16,16,128]{2,1,0:T(8,128)(2,1)S(1)} %share_copies.1), channel_id=1, replica_groups={{9,11,13,15,1,3,5,7,8,10,12,14,0,2,4,6},{25,27,29,31,17,19,21,23,24,26,..., dimensions={0} | all-to-all | bytes 131072 | tf_op jit(solution)/shard_map/all_to_all | solution.py:455
  43.1 0.7 %total_rows.1 = f32[2,1728]{1,0:T(2,128)} custom-call(bf16[16,16,128]{2,1,0:T(8,128)(2,1)S(1)} %all_to_all.11.copies_ref), custom_call_target="tpu_custom_call" | custom-call | flops 1000000 | bytes 65536 | tf_op jit(solution)/shard_map/total_rows/pallas_call | solution.py:353
  (1 shorter events, 0.0 us)
Async XLA Ops:
  0.0 1.0 %copy-start.1 = (bf16[1,32,2,24,128]{4,3,2,1,0:T(8,128)(2,1)S(1)}, bf16[1,32,2,24,128]{4,3,2,1,0:T(8,128)(2,1)}, u32[]{:S(2)}) copy-start(bf16[1,32,2,24,128]{4,3,2,1,0:T(8,128)(2,1)} %param.6) | copy-start | bytes 1179652
  1.0 5.8 %copy-start.2 = (bf16[1,32,2,24,128]{4,3,2,1,0:T(8,128)(2,1)S(1)}, bf16[1,32,2,24,128]{4,3,2,1,0:T(8,128)(2,1)}, u32[]{:S(2)}) copy-start(bf16[1,32,2,24,128]{4,3,2,1,0:T(8,128)(2,1)} %param.5) | copy-start | bytes 1179652
  1.2 8.5 %copy-start = (bf16[1,32,4,48,256]{4,3,2,1,0:T(8,128)(2,1)S(1)}, bf16[1,32,4,48,256]{4,3,2,1,0:T(8,128)(2,1)}, u32[]{:S(2)}) copy-start(bf16[1,32,4,48,256]{4,3,2,1,0:T(8,128)(2,1)} %param.4) | copy-start | bytes 9437188
  1.2 8.5 %copy-start.3 = (bf16[27,32,32]{2,1,0:T(8,128)(2,1)S(1)}, bf16[27,32,32]{2,1,0:T(8,128)(2,1)}, u32[]{:S(2)}) copy-start(bf16[27,32,32]{2,1,0:T(8,128)(2,1)} %weight_ref.1) | copy-start | bytes 165892
  1.2 11.3 %collective-permute-start.1 = (bf16[768,128]{1,0:T(8,128)(2,1)S(1)}, bf16[768,128]{1,0:T(8,128)(2,1)S(1)}, u32[]{:S(2)}, u32[]{:S(2)}) collective-permute-start(bf16[768,128]{1,0:T(8,128)(2,1)S(1)} %get-tuple-element.19), channel_id=1, source_target_pairs={{16,32},{32,16},{48,64},{64,48},{80,96},{96,80},{112,128},{128,112... | collective-permute-start | bytes 589832 | tf_op jit(solution)/shard_map/ppermute | solution.py:450
  6.0 6.5 %collective-permute-start.2 = (bf16[768,128]{1,0:T(8,128)(2,1)S(1)}, bf16[768,128]{1,0:T(8,128)(2,1)S(1)}, u32[]{:S(2)}, u32[]{:S(2)}) collective-permute-start(bf16[768,128]{1,0:T(8,128)(2,1)S(1)} %get-tuple-element.20), channel_id=1, source_target_pairs={{0,16},{16,0},{32,48},{48,32},{64,80},{80,64},{96,112},{112,96},{1... | collective-permute-start | bytes 589832 | tf_op jit(solution)/shard_map/ppermute | solution.py:450
  6.9 8.4 %collective-permute-start = (bf16[2,768,128]{2,1,0:T(8,128)(2,1)S(1)}, bf16[2,768,128]{2,1,0:T(8,128)(2,1)S(1)}, u32[]{:S(2)}, u32[]{:S(2)}) collective-permute-start(bf16[2,768,128]{2,1,0:T(8,128)(2,1)S(1)} %for_prev.1), channel_id=1, source_target_pairs={{16,0},{32,16},{48,32},{64,48},{80,64},{96,80},{112,96},{128,112},... | collective-permute-start | bytes 1179656 | tf_op jit(solution)/shard_map/ppermute | solution.py:465

commit v9 on v8

--- a/solution.py
+++ b/solution.py
@@ -70,9 +70,33 @@
     far_ref[...] = jnp.where(odd, last, first)
 
 
-def prev_kernel(pre_ref, planes_ref, prev_ref):
+def flipped_weights(weight_ref, weight_t, j):
+    for k in range(3):
+        base = (2 - j) * 9 + (2 - k) * 3
+        wide = jnp.concatenate([weight_ref[base + d].astype(F32) for d in range(3)], axis=1)
+        weight_t[k * C : (k + 1) * C, 0:T3] = wide
+    weight_t[3 * C :, :] = jnp.zeros((C, 128), F32)
+    return weight_t[:, 0:T3].T.astype(BF)
+
+
+def prev_kernel(pre_ref, planes_ref, weight_ref, prev_ref, weight_t):
     prev_ref[0] = by_depth(pre_ref[:, 0])
-    prev_ref[1] = planes_ref[1, C : (QZ + 1) * C, :]
+    odd = on_odd()
+
+    @pl.when(odd)
+    def _():
+        prev_ref[1] = planes_ref[1, C : (QZ + 1) * C, :]
+
+    @pl.when(jnp.logical_not(odd))
+    def _():
+        weights = flipped_weights(weight_ref, weight_t, 2)
+        for z in range(0, QZ, 2):
+            terms = jnp.dot(
+                weights, depth_pair([planes_ref.at[1]], z), preferred_element_type=F32
+            )
+            for h in range(2):
+                rows = slice((z + h) * C, (z + h + 1) * C)
+                prev_ref[1, rows, :] = taps_joined(terms[:, h * QY : (h + 1) * QY]).astype(BF)
 
 
 def hidden_rows(hidden_t, z0):
@@ -285,20 +309,32 @@
     plane, scale, even, odds, flips, head,
 ):
     more = lax.axis_index("space") < lax.axis_size("space") - 1
-    plane[0:C, :] = jnp.zeros((C, QY), BF)
-    plane[(QZ + 1) * C :, :] = jnp.zeros((2 * C, QY), BF)
-    plane[C : (QZ + 1) * C, :] = next_ref[1]
     pre = next_ref[0].astype(F32)
     gate = jax.nn.sigmoid(pre)
     scale[...] = jnp.where(more, gate * (1.0 + pre * (1.0 - gate)), 0.0)
 
-    weights = rim_weights[T3 : 2 * T3, 128:256]
-    for z in range(0, QZ, 2):
-        terms = jnp.dot(weights, depth_pair([plane], z), preferred_element_type=F32)
-        for h in range(2):
-            rows = slice((z + h) * C, (z + h + 1) * C)
-            grad = partial_ref[rows, :] + taps_joined(terms[:, h * QY : (h + 1) * QY])
-            put_grad(even, odds, z + h, grad * scale[rows, :])
+    odd = on_odd()
+
+    @pl.when(odd)
+    def _():
+        for z in range(QZ):
+            rows = slice(z * C, (z + 1) * C)
+            grad = partial_ref[rows, :] + next_ref[1, rows, :].astype(F32)
+            put_grad(even, odds, z, grad * scale[rows, :])
+
+    @pl.when(jnp.logical_not(odd))
+    def _():
+        plane[0:C, :] = jnp.zeros((C, QY), BF)
+        plane[(QZ + 1) * C :, :] = jnp.zeros((2 * C, QY), BF)
+        plane[C : (QZ + 1) * C, :] = next_ref[1]
+        weights = rim_weights[T3 : 2 * T3, 128:256]
+        for z in range(0, QZ, 2):
+            terms = jnp.dot(weights, depth_pair([plane], z), preferred_element_type=F32)
+            for h in range(2):
+                rows = slice((z + h) * C, (z + h + 1) * C)
+                grad = partial_ref[rows, :] + taps_joined(terms[:, h * QY : (h + 1) * QY])
+                put_grad(even, odds, z + h, grad * scale[rows, :])
+
     even_sum, odd_sum = cell_sums(act_t, [IX - 1], [even], [odds])
     first_flips(flips, 0, even_sum + first_ref[0, :, 0:C])
     first_flips(flips, 1, odd_sum + first_ref[1, :, 0 : 2 * C])
@@ -374,9 +410,14 @@
     )
 
 
-def for_prev(pre, planes):
+def for_prev(pre, planes, weight):
     return call(
-        prev_kernel, "for_prev", [((2, QZ * C, QY), BF)], [], 10**9, pre, planes
+        prev_kernel,
+        "for_prev",
+        [((2, QZ * C, QY), BF)],
+        [VMEM((128, 128), F32)],
+        10**9,
+        pre, planes, weight,
     )[0]
 
 
@@ -460,7 +501,7 @@
 def on_device(activations, preact, cotangent, conv_weight):
     act, pre, cot = activations[0], preact[0], cotangent[0]
     planes, to_chip, to_far = relay(cot)
-    to_prev = for_prev(pre, planes)
+    to_prev = for_prev(pre, planes, conv_weight)
     far = swapped(to_far, 1)
     after = lax.ppermute(to_prev, "space", [(i + 1, i) for i in range(lax.axis_size("space") - 1)])
     chip = swapped(to_chip, 0)

time: 44 us -> 43.8 us (level)
  Pallas kernels: 7.69 us -> 8.52 us
  starting transfers between devices: 8.34 us -> 7.77 us
    pallas_call x7, Pallas kernels: 7.69 us -> 8.52 us  [call(): pl.pallas_call(kernel, out_shape=shapes, in_specs=[pl.BlockSpec(memory_sp...]
    ppermute x1, starting transfers between devices: 2.77 us -> 2.2 us  [on_device(): lax.ppermute(to_prev, 'space', [(i + 1, i) for i in range(lax.axis_size('...]
  transfers between devices with their start and end apart: 3 -> 3, of which waited for: 0 -> 0; matrix products, arithmetic and copies ran while one was open for 0% -> 0% of each run, Pallas kernels for 13% -> 14%
where the time goes in v9:
time: 43.8 us; the launch traced here: 43.6 us
  blocking collectives  26.2 us (60%)
  Pallas kernels  8.52 us (19%)
  starting transfers between devices  7.77 us (18%)
  local copies, waits for them, and re-layouts  1.01 us (2%)
    all_to_all x2, blocking collectives, exchanged(): lax.all_to_all(x, ('space', 'deep', 'lane'), 0, 0, axis_index_groups=grou...  26.2 us
    pallas_call x7, Pallas kernels, call(): pl.pallas_call(kernel, out_shape=shapes, in_specs=[pl.BlockSpec(memory_sp...  8.52 us
    ppermute x2, starting transfers between devices, swapped(): return lax.ppermute(x, 'space', pairs)  5.57 us
    ppermute x1, starting transfers between devices, on_device(): lax.ppermute(to_prev, 'space', [(i + 1, i) for i in range(lax.axis_size('...  2.2 us
    unnamed x8, local copies, waits for them, and re-layouts  1.01 us
  transfers between devices with their start and end apart: 3, of which 0 were waited for; matrix products, arithmetic and copies ran while one was open for 0% of the time, Pallas kernels for 14%

profile of v9, /device:TPU:2, one launch (start us, length us, event | category | flops | bytes accessed | tf_op | source)
XLA Modules:
  0.0 43.6 jit_solution(14971724559892747386)
XLA Ops:
  0.0 0.0 copy-start.1
  0.0 1.0 %copy-done.1 = bf16[1,32,2,24,128]{4,3,2,1,0:T(8,128)(2,1)S(1)} copy-done((bf16[1,32,2,24,128]{4,3,2,1,0:T(8,128)(2,1)S(1)}, bf16[1,32,2,24,128]{4,3,2,1,0:T(8,128)(2,1)}, u32[]{:S(2)}) %copy-start.1) | copy-done | bytes 393240
  1.0 0.0 copy-start.2
  1.0 0.0 copy-start.3
  1.0 0.2 relay.1
  1.2 0.0 copy-start
  1.2 4.8 %collective-permute-start.1 = (bf16[768,128]{1,0:T(8,128)(2,1)S(1)}, bf16[768,128]{1,0:T(8,128)(2,1)S(1)}, u32[]{:S(2)}, u32[]{:S(2)}) collective-permute-start(bf16[768,128]{1,0:T(8,128)(2,1)S(1)} %get-tuple-element.19), channel_id=1, source_target_pairs={{16,32},{32,16},{48,64},{64,48},{80,96},{96,80},{112,128},{128,112... | collective-permute-start | bytes 589832 | tf_op jit(solution)/shard_map/ppermute | solution.py:491
  6.0 0.8 %collective-permute-start.2 = (bf16[768,128]{1,0:T(8,128)(2,1)S(1)}, bf16[768,128]{1,0:T(8,128)(2,1)S(1)}, u32[]{:S(2)}, u32[]{:S(2)}) collective-permute-start(bf16[768,128]{1,0:T(8,128)(2,1)S(1)} %get-tuple-element.20), channel_id=1, source_target_pairs={{0,16},{16,0},{32,48},{48,32},{64,80},{80,64},{96,112},{112,96},{1... | collective-permute-start | bytes 589832 | tf_op jit(solution)/shard_map/ppermute | solution.py:491
  6.8 0.0 copy-done.2
  6.8 0.0 copy-done.3
  6.8 0.7 %for_prev.1 = bf16[2,768,128]{2,1,0:T(8,128)(2,1)S(1)} custom-call(bf16[32,2,24,128]{3,2,1,0:T(8,128)(2,1)S(1)} %bitcast.5, bf16[2,864,128]{2,1,0:T(8,128)(2,1)S(1)} %get-tuple-element.17.planes_ref, bf16[27,32,32]{2,1,0:T(8,128)(2,1)S(1)} %copy-done.3), custom_call_target="tpu_custom_call" | custom-call | flops 1000000000 | bytes 890880 | tf_op jit(solution)/shard_map/for_prev/pallas_call | solution.py:389
  7.5 2.2 %collective-permute-start = (bf16[2,768,128]{2,1,0:T(8,128)(2,1)S(1)}, bf16[2,768,128]{2,1,0:T(8,128)(2,1)S(1)}, u32[]{:S(2)}, u32[]{:S(2)}) collective-permute-start(bf16[2,768,128]{2,1,0:T(8,128)(2,1)S(1)} %for_prev.1), channel_id=1, source_target_pairs={{16,0},{32,16},{48,32},{64,48},{80,64},{96,80},{112,96},{128,112},... | collective-permute-start | bytes 1179656 | tf_op jit(solution)/shard_map/ppermute | solution.py:506
  9.7 0.0 copy-done
  9.7 2.8 %local_terms.1 = (bf16[4,1568,256]{2,1,0:T(8,128)(2,1)S(1)}, bf16[2,2304,128]{2,1,0:T(8,128)(2,1)S(1)}, f32[2,768,128]{2,1,0:T(8,128)S(1)}, f32[3,768,128]{2,1,0...) custom-call(bf16[32,4,48,256]{3,2,1,0:T(8,128)(2,1)S(1)} %bitcast.3, ...), custom_call_target="tpu_custom_call" | custom-call | flops 5000000000 | bytes 4036608 | tf_op jit(solution)/shard_map/local_terms/pallas_call | solution.py:389
  12.5 0.0 collective-permute-done.1.far_ref
  12.5 0.0 collective-permute-done.2.chip_ref
  12.5 2.8 %main_terms.1 = (f32[2,96,128]{2,1,0:T(8,128)S(1)}, f32[2,216,128]{2,1,0:T(8,128)S(1)}, f32[768,128]{1,0:T(8,128)S(1)}) custom-call(bf16[768,128]{1,0:T(8,128)(2,1)S(1)} %collective-permute-done.1.far_ref, bf16[768,128]{1,0:T(8,128)(2,1)S(1)} %collective-permute-done.2.chip_ref, bf16[288,256]{1,0:T(8,128)(2,1)S(1)} %get-tuple-element.18.rim_weights, ...), custom_call_target="tpu_custom_call" | custom-call | flops 5000000000 | bytes 7045120 | tf_op jit(solution)/shard_map/main_terms/pallas_call | solution.py:389
  15.3 0.0 collective-permute-done.next_ref
  15.3 1.3 %last_terms.1 = bf16[32,16,128]{2,1,0:T(8,128)(2,1)S(1)} custom-call(bf16[2,768,128]{2,1,0:T(8,128)(2,1)S(1)} %collective-permute-done.next_ref, bf16[288,256]{1,0:T(8,128)(2,1)S(1)} %get-tuple-element.18.rim_weights, f32[768,128]{1,0:T(8,128)S(1)} %get-tuple-element.26.partial_ref, bf16[4,1568,256]{2,1,0:T(8,128)(2,1)S(1)} %get-tuple-element.24.act_t, ...), custom_call_target="tpu_custom_call" | custom-call | flops 1000000000 | bytes 4464640 | tf_op jit(solution)/shard_map/last_terms/pallas_call | solution.py:389
  16.7 12.1 %all_to_all.10.shares_ref = bf16[32,16,128]{2,1,0:T(8,128)(2,1)S(1)} all-to-all(bf16[32,16,128]{2,1,0:T(8,128)(2,1)S(1)} %last_terms.1), channel_id=1, replica_groups={{176,177,192,193,208,209,224,225,240,241,0,1,16,17,32,33,48,49,64,65,80..., dimensions={0} | all-to-all | bytes 262144 | tf_op jit(solution)/shard_map/all_to_all | solution.py:496
  28.8 14.1 %all_to_all.11.copies_ref = bf16[16,16,128]{2,1,0:T(8,128)(2,1)S(1)} all-to-all(bf16[16,16,128]{2,1,0:T(8,128)(2,1)S(1)} %share_copies.1), channel_id=1, replica_groups={{9,11,13,15,1,3,5,7,8,10,12,14,0,2,4,6},{25,27,29,31,17,19,21,23,24,26,..., dimensions={0} | all-to-all | bytes 131072 | tf_op jit(solution)/shard_map/all_to_all | solution.py:496
  42.9 0.7 %total_rows.1 = f32[2,1728]{1,0:T(2,128)} custom-call(bf16[16,16,128]{2,1,0:T(8,128)(2,1)S(1)} %all_to_all.11.copies_ref), custom_call_target="tpu_custom_call" | custom-call | flops 1000000 | bytes 65536 | tf_op jit(solution)/shard_map/total_rows/pallas_call | solution.py:389
  (1 shorter events, 0.0 us)
Async XLA Ops:
  0.0 1.0 %copy-start.1 = (bf16[1,32,2,24,128]{4,3,2,1,0:T(8,128)(2,1)S(1)}, bf16[1,32,2,24,128]{4,3,2,1,0:T(8,128)(2,1)}, u32[]{:S(2)}) copy-start(bf16[1,32,2,24,128]{4,3,2,1,0:T(8,128)(2,1)} %param.6) | copy-start | bytes 1179652
  1.0 5.8 %copy-start.2 = (bf16[1,32,2,24,128]{4,3,2,1,0:T(8,128)(2,1)S(1)}, bf16[1,32,2,24,128]{4,3,2,1,0:T(8,128)(2,1)}, u32[]{:S(2)}) copy-start(bf16[1,32,2,24,128]{4,3,2,1,0:T(8,128)(2,1)} %param.5) | copy-start | bytes 1179652
  1.0 5.8 %copy-start.3 = (bf16[27,32,32]{2,1,0:T(8,128)(2,1)S(1)}, bf16[27,32,32]{2,1,0:T(8,128)(2,1)}, u32[]{:S(2)}) copy-start(bf16[27,32,32]{2,1,0:T(8,128)(2,1)} %weight_ref.3) | copy-start | bytes 165892
  1.2 8.5 %copy-start = (bf16[1,32,4,48,256]{4,3,2,1,0:T(8,128)(2,1)S(1)}, bf16[1,32,4,48,256]{4,3,2,1,0:T(8,128)(2,1)}, u32[]{:S(2)}) copy-start(bf16[1,32,4,48,256]{4,3,2,1,0:T(8,128)(2,1)} %param.4) | copy-start | bytes 9437188
  1.2 11.3 %collective-permute-start.1 = (bf16[768,128]{1,0:T(8,128)(2,1)S(1)}, bf16[768,128]{1,0:T(8,128)(2,1)S(1)}, u32[]{:S(2)}, u32[]{:S(2)}) collective-permute-start(bf16[768,128]{1,0:T(8,128)(2,1)S(1)} %get-tuple-element.19), channel_id=1, source_target_pairs={{16,32},{32,16},{48,64},{64,48},{80,96},{96,80},{112,128},{128,112... | collective-permute-start | bytes 589832 | tf_op jit(solution)/shard_map/ppermute | solution.py:491
  6.0 6.5 %collective-permute-start.2 = (bf16[768,128]{1,0:T(8,128)(2,1)S(1)}, bf16[768,128]{1,0:T(8,128)(2,1)S(1)}, u32[]{:S(2)}, u32[]{:S(2)}) collective-permute-start(bf16[768,128]{1,0:T(8,128)(2,1)S(1)} %get-tuple-element.20), channel_id=1, source_target_pairs={{0,16},{16,0},{32,48},{48,32},{64,80},{80,64},{96,112},{112,96},{1... | collective-permute-start | bytes 589832 | tf_op jit(solution)/shard_map/ppermute | solution.py:491
  7.5 7.9 %collective-permute-start = (bf16[2,768,128]{2,1,0:T(8,128)(2,1)S(1)}, bf16[2,768,128]{2,1,0:T(8,128)(2,1)S(1)}, u32[]{:S(2)}, u32[]{:S(2)}) collective-permute-start(bf16[2,768,128]{2,1,0:T(8,128)(2,1)S(1)} %for_prev.1), channel_id=1, source_target_pairs={{16,0},{32,16},{48,32},{64,48},{80,64},{96,80},{112,96},{128,112},... | collective-permute-start | bytes 1179656 | tf_op jit(solution)/shard_map/ppermute | solution.py:506

commit v10 on v9

--- a/solution.py
+++ b/solution.py
@@ -135,7 +135,7 @@
         rows = by_depth(pre_ref[:, plane]).astype(F32)
         for z in range(QZ):
             pre = rows[z * C : (z + 1) * C]
-            gate = jax.nn.sigmoid(pre)
+            gate = 0.5 + 0.5 * jnp.tanh(0.5 * pre)
             hidden = (pre * gate).astype(BF).astype(F32)
             hidden_t[plane, z * T3 : (z + 1) * T3, :] = jnp.concatenate(
                 [lane_shift(hidden, 1), hidden, lane_shift(hidden, -1)], axis=0
@@ -310,7 +310,7 @@
 ):
     more = lax.axis_index("space") < lax.axis_size("space") - 1
     pre = next_ref[0].astype(F32)
-    gate = jax.nn.sigmoid(pre)
+    gate = 0.5 + 0.5 * jnp.tanh(0.5 * pre)
     scale[...] = jnp.where(more, gate * (1.0 + pre * (1.0 - gate)), 0.0)
 
     odd = on_odd()

time: 43.8 us -> 43.8 us (level)
  no operation moved by 1% of the time
where the time goes in v10:
time: 43.8 us; the launch traced here: 43.6 us
  blocking collectives  26.2 us (60%)
  Pallas kernels  8.59 us (20%)
  starting transfers between devices  7.77 us (18%)
  local copies, waits for them, and re-layouts  1.01 us (2%)
    all_to_all x2, blocking collectives, exchanged(): lax.all_to_all(x, ('space', 'deep', 'lane'), 0, 0, axis_index_groups=grou...  26.2 us
    pallas_call x7, Pallas kernels, call(): pl.pallas_call(kernel, out_shape=shapes, in_specs=[pl.BlockSpec(memory_sp...  8.59 us
    ppermute x2, starting transfers between devices, swapped(): return lax.ppermute(x, 'space', pairs)  5.57 us
    ppermute x1, starting transfers between devices, on_device(): lax.ppermute(to_prev, 'space', [(i + 1, i) for i in range(lax.axis_size('...  2.2 us
    unnamed x8, local copies, waits for them, and re-layouts  1.01 us
  transfers between devices with their start and end apart: 3, of which 0 were waited for; matrix products, arithmetic and copies ran while one was open for 0% of the time, Pallas kernels for 14%

profile of v10, /device:TPU:2, one launch (start us, length us, event | category | flops | bytes accessed | tf_op | source)
XLA Modules:
  0.0 43.6 jit_solution(14710458915061920283)
XLA Ops:
  0.0 0.0 copy-start.1
  0.0 1.0 %copy-done.1 = bf16[1,32,2,24,128]{4,3,2,1,0:T(8,128)(2,1)S(1)} copy-done((bf16[1,32,2,24,128]{4,3,2,1,0:T(8,128)(2,1)S(1)}, bf16[1,32,2,24,128]{4,3,2,1,0:T(8,128)(2,1)}, u32[]{:S(2)}) %copy-start.1) | copy-done | bytes 393240
  1.0 0.0 copy-start.2
  1.0 0.0 copy-start.3
  1.0 0.2 relay.1
  1.2 0.0 copy-start
  1.2 4.8 %collective-permute-start.1 = (bf16[768,128]{1,0:T(8,128)(2,1)S(1)}, bf16[768,128]{1,0:T(8,128)(2,1)S(1)}, u32[]{:S(2)}, u32[]{:S(2)}) collective-permute-start(bf16[768,128]{1,0:T(8,128)(2,1)S(1)} %get-tuple-element.19), channel_id=1, source_target_pairs={{16,32},{32,16},{48,64},{64,48},{80,96},{96,80},{112,128},{128,112... | collective-permute-start | bytes 589832 | tf_op jit(solution)/shard_map/ppermute | solution.py:491
  6.0 0.8 %collective-permute-start.2 = (bf16[768,128]{1,0:T(8,128)(2,1)S(1)}, bf16[768,128]{1,0:T(8,128)(2,1)S(1)}, u32[]{:S(2)}, u32[]{:S(2)}) collective-permute-start(bf16[768,128]{1,0:T(8,128)(2,1)S(1)} %get-tuple-element.20), channel_id=1, source_target_pairs={{0,16},{16,0},{32,48},{48,32},{64,80},{80,64},{96,112},{112,96},{1... | collective-permute-start | bytes 589832 | tf_op jit(solution)/shard_map/ppermute | solution.py:491
  6.8 0.0 copy-done.2
  6.8 0.0 copy-done.3
  6.8 0.7 %for_prev.1 = bf16[2,768,128]{2,1,0:T(8,128)(2,1)S(1)} custom-call(bf16[32,2,24,128]{3,2,1,0:T(8,128)(2,1)S(1)} %bitcast.5, bf16[2,864,128]{2,1,0:T(8,128)(2,1)S(1)} %get-tuple-element.17.planes_ref, bf16[27,32,32]{2,1,0:T(8,128)(2,1)S(1)} %copy-done.3), custom_call_target="tpu_custom_call" | custom-call | flops 1000000000 | bytes 890880 | tf_op jit(solution)/shard_map/for_prev/pallas_call | solution.py:389
  7.5 2.2 %collective-permute-start = (bf16[2,768,128]{2,1,0:T(8,128)(2,1)S(1)}, bf16[2,768,128]{2,1,0:T(8,128)(2,1)S(1)}, u32[]{:S(2)}, u32[]{:S(2)}) collective-permute-start(bf16[2,768,128]{2,1,0:T(8,128)(2,1)S(1)} %for_prev.1), channel_id=1, source_target_pairs={{16,0},{32,16},{48,32},{64,48},{80,64},{96,80},{112,96},{128,112},... | collective-permute-start | bytes 1179656 | tf_op jit(solution)/shard_map/ppermute | solution.py:506
  9.7 0.0 copy-done
  9.7 2.9 %local_terms.1 = (bf16[4,1568,256]{2,1,0:T(8,128)(2,1)S(1)}, bf16[2,2304,128]{2,1,0:T(8,128)(2,1)S(1)}, f32[2,768,128]{2,1,0:T(8,128)S(1)}, f32[3,768,128]{2,1,0...) custom-call(bf16[32,4,48,256]{3,2,1,0:T(8,128)(2,1)S(1)} %bitcast.3, ...), custom_call_target="tpu_custom_call" | custom-call | flops 5000000000 | bytes 4036608 | tf_op jit(solution)/shard_map/local_terms/pallas_call | solution.py:389
  12.6 0.0 collective-permute-done.1.far_ref
  12.6 0.0 collective-permute-done.2.chip_ref
  12.6 2.8 %main_terms.1 = (f32[2,96,128]{2,1,0:T(8,128)S(1)}, f32[2,216,128]{2,1,0:T(8,128)S(1)}, f32[768,128]{1,0:T(8,128)S(1)}) custom-call(bf16[768,128]{1,0:T(8,128)(2,1)S(1)} %collective-permute-done.1.far_ref, bf16[768,128]{1,0:T(8,128)(2,1)S(1)} %collective-permute-done.2.chip_ref, bf16[288,256]{1,0:T(8,128)(2,1)S(1)} %get-tuple-element.18.rim_weights, ...), custom_call_target="tpu_custom_call" | custom-call | flops 5000000000 | bytes 7045120 | tf_op jit(solution)/shard_map/main_terms/pallas_call | solution.py:389
  15.4 0.0 collective-permute-done.next_ref
  15.4 1.3 %last_terms.1 = bf16[32,16,128]{2,1,0:T(8,128)(2,1)S(1)} custom-call(bf16[2,768,128]{2,1,0:T(8,128)(2,1)S(1)} %collective-permute-done.next_ref, bf16[288,256]{1,0:T(8,128)(2,1)S(1)} %get-tuple-element.18.rim_weights, f32[768,128]{1,0:T(8,128)S(1)} %get-tuple-element.26.partial_ref, bf16[4,1568,256]{2,1,0:T(8,128)(2,1)S(1)} %get-tuple-element.24.act_t, ...), custom_call_target="tpu_custom_call" | custom-call | flops 1000000000 | bytes 4464640 | tf_op jit(solution)/shard_map/last_terms/pallas_call | solution.py:389
  16.7 12.0 %all_to_all.10.shares_ref = bf16[32,16,128]{2,1,0:T(8,128)(2,1)S(1)} all-to-all(bf16[32,16,128]{2,1,0:T(8,128)(2,1)S(1)} %last_terms.1), channel_id=1, replica_groups={{176,177,192,193,208,209,224,225,240,241,0,1,16,17,32,33,48,49,64,65,80..., dimensions={0} | all-to-all | bytes 262144 | tf_op jit(solution)/shard_map/all_to_all | solution.py:496
  28.8 14.1 %all_to_all.11.copies_ref = bf16[16,16,128]{2,1,0:T(8,128)(2,1)S(1)} all-to-all(bf16[16,16,128]{2,1,0:T(8,128)(2,1)S(1)} %share_copies.1), channel_id=1, replica_groups={{9,11,13,15,1,3,5,7,8,10,12,14,0,2,4,6},{25,27,29,31,17,19,21,23,24,26,..., dimensions={0} | all-to-all | bytes 131072 | tf_op jit(solution)/shard_map/all_to_all | solution.py:496
  42.9 0.7 %total_rows.1 = f32[2,1728]{1,0:T(2,128)} custom-call(bf16[16,16,128]{2,1,0:T(8,128)(2,1)S(1)} %all_to_all.11.copies_ref), custom_call_target="tpu_custom_call" | custom-call | flops 1000000 | bytes 65536 | tf_op jit(solution)/shard_map/total_rows/pallas_call | solution.py:389
  (1 shorter events, 0.0 us)
Async XLA Ops:
  0.0 1.0 %copy-start.1 = (bf16[1,32,2,24,128]{4,3,2,1,0:T(8,128)(2,1)S(1)}, bf16[1,32,2,24,128]{4,3,2,1,0:T(8,128)(2,1)}, u32[]{:S(2)}) copy-start(bf16[1,32,2,24,128]{4,3,2,1,0:T(8,128)(2,1)} %param.6) | copy-start | bytes 1179652
  1.0 5.8 %copy-start.2 = (bf16[1,32,2,24,128]{4,3,2,1,0:T(8,128)(2,1)S(1)}, bf16[1,32,2,24,128]{4,3,2,1,0:T(8,128)(2,1)}, u32[]{:S(2)}) copy-start(bf16[1,32,2,24,128]{4,3,2,1,0:T(8,128)(2,1)} %param.5) | copy-start | bytes 1179652
  1.0 5.8 %copy-start.3 = (bf16[27,32,32]{2,1,0:T(8,128)(2,1)S(1)}, bf16[27,32,32]{2,1,0:T(8,128)(2,1)}, u32[]{:S(2)}) copy-start(bf16[27,32,32]{2,1,0:T(8,128)(2,1)} %weight_ref.3) | copy-start | bytes 165892
  1.2 8.5 %copy-start = (bf16[1,32,4,48,256]{4,3,2,1,0:T(8,128)(2,1)S(1)}, bf16[1,32,4,48,256]{4,3,2,1,0:T(8,128)(2,1)}, u32[]{:S(2)}) copy-start(bf16[1,32,4,48,256]{4,3,2,1,0:T(8,128)(2,1)} %param.4) | copy-start | bytes 9437188
  1.2 11.4 %collective-permute-start.1 = (bf16[768,128]{1,0:T(8,128)(2,1)S(1)}, bf16[768,128]{1,0:T(8,128)(2,1)S(1)}, u32[]{:S(2)}, u32[]{:S(2)}) collective-permute-start(bf16[768,128]{1,0:T(8,128)(2,1)S(1)} %get-tuple-element.19), channel_id=1, source_target_pairs={{16,32},{32,16},{48,64},{64,48},{80,96},{96,80},{112,128},{128,112... | collective-permute-start | bytes 589832 | tf_op jit(solution)/shard_map/ppermute | solution.py:491
  6.0 6.6 %collective-permute-start.2 = (bf16[768,128]{1,0:T(8,128)(2,1)S(1)}, bf16[768,128]{1,0:T(8,128)(2,1)S(1)}, u32[]{:S(2)}, u32[]{:S(2)}) collective-permute-start(bf16[768,128]{1,0:T(8,128)(2,1)S(1)} %get-tuple-element.20), channel_id=1, source_target_pairs={{0,16},{16,0},{32,48},{48,32},{64,80},{80,64},{96,112},{112,96},{1... | collective-permute-start | bytes 589832 | tf_op jit(solution)/shard_map/ppermute | solution.py:491
  7.5 7.9 %collective-permute-start = (bf16[2,768,128]{2,1,0:T(8,128)(2,1)S(1)}, bf16[2,768,128]{2,1,0:T(8,128)(2,1)S(1)}, u32[]{:S(2)}, u32[]{:S(2)}) collective-permute-start(bf16[2,768,128]{2,1,0:T(8,128)(2,1)S(1)} %for_prev.1), channel_id=1, source_target_pairs={{16,0},{32,16},{48,32},{64,48},{80,64},{96,80},{112,96},{128,112},... | collective-permute-start | bytes 1179656 | tf_op jit(solution)/shard_map/ppermute | solution.py:506
